TPU v7x, 32 devices: a whole 2x2x4 slice. The times are simulated.
32 devices in a mesh: section: 2 (over x), dp: 8 (over z, y), tensor: 2 (over core).
Axes of the slice: x: 2, y: 2, z: 4, core: 2. Of those that a mesh axis runs over, the one named last changes fastest.
Arguments:
- text_stream: bfloat16 [2, 32, 92, 768], P('section', 'dp'), may hold values from -6 to 6
- image_stream: bfloat16 [2, 32, 100, 1024], P('section', 'dp'), may hold values from -6 to 6
- region_mask: int32 [32, 100], P('dp'), may hold values from 0 to 1, as said below
- co_text_in: bfloat16 [768, 3, 1024], P(None, None, 'tensor'), may hold values from -0.21875 to 0.21875
- co_text_out: bfloat16 [1024, 768], P('tensor'), may hold values from -0.75 to 0.75
- self_text_in: bfloat16 [768, 3, 768], P(None, None, 'tensor'), may hold values from -0.21875 to 0.21875
- self_text_out: bfloat16 [768, 768], P('tensor'), may hold values from -0.875 to 0.875
- image_attn_in: bfloat16 [2, 1024, 3, 1024], P('section', None, None, 'tensor'), may hold values from -0.1875 to 0.1875
- image_attn_out: bfloat16 [2, 1024, 1024], P('section', 'tensor'), may hold values from -0.75 to 0.75
- text_up: bfloat16 [2, 768, 3072], P('section', None, 'tensor'), may hold values from -0.21875 to 0.21875
- text_down: bfloat16 [2, 3072, 768], P('section', 'tensor'), may hold values from -0.15625 to 0.15625
- image_up: bfloat16 [2, 1024, 1024], P('section', None, 'tensor'), may hold values from -0.1875 to 0.1875
- image_down: bfloat16 [2, 1024, 1024], P('section', 'tensor'), may hold values from -0.25 to 0.25
- text_gain: float32 [2, 2, 768], P('section'), may hold values from 0.1 to 1.9
- text_shift: float32 [2, 2, 768], P('section'), may hold values from -1.5 to 1.5
- image_gain: float32 [2, 2, 1024], P('section'), may hold values from 0.1 to 1.9
- image_shift: float32 [2, 2, 1024], P('section'), may hold values from -1.5 to 1.5
Outputs:
- text_result: bfloat16 [2, 32, 92, 768], P('section', 'dp')
- image_result: bfloat16 [2, 32, 100, 1024], P('section', 'dp')
- co_text_in_grad: float32 [768, 3, 1024], P(None, None, 'tensor')
- co_text_out_grad: float32 [1024, 768], P('tensor')
- self_text_in_grad: float32 [768, 3, 768], P(None, None, 'tensor')
- self_text_out_grad: float32 [768, 768], P('tensor')
- image_attn_in_grad: float32 [2, 1024, 3, 1024], P('section', None, None, 'tensor')
- image_attn_out_grad: float32 [2, 1024, 1024], P('section', 'tensor')
- text_up_grad: float32 [2, 768, 3072], P('section', None, 'tensor')
- text_down_grad: float32 [2, 3072, 768], P('section', 'tensor')
- image_up_grad: float32 [2, 1024, 1024], P('section', None, 'tensor')
- image_down_grad: float32 [2, 1024, 1024], P('section', 'tensor')
- text_gain_grad: float32 [2, 2, 768], P('section')
- text_shift_grad: float32 [2, 2, 768], P('section')
- image_gain_grad: float32 [2, 2, 1024], P('section')
- image_shift_grad: float32 [2, 2, 1024], P('section')
Inputs may be any that keep to these rules, and one draw needn't show every extreme that they name: `region_mask`: each row is 1 on a leading run of 10 to 100 region slots and 0 after it.
All inputs are finite; a program needn't handle non-finite values.
Results may differ from a plain program's by a relative error of at most 0.03.
Values may be sent and summed in bfloat16 or wider, within the bound.
No kernel may reach another device: no remote copies, remote signals or barrier semaphores. Data moves between devices by JAX's collectives and lax.ppermute only.
A program may use at most 192 MiB of HBM per device.

v0:
```python
import math

import jax
import jax.numpy as jnp
from jax import lax
from jax.sharding import PartitionSpec as P

D_TEXT = 768
HEADS_TEXT = 12
D_IMAGE = 1024
HEADS_IMAGE = 8
D_CO = 1024
HEADS_CO = 8

LOW = jnp.bfloat16
FULL = jnp.float32


def dot(spec, left, right):
    return jnp.einsum(spec, left, right, preferred_element_type=FULL)


def norm_parts(rows):
    centre = rows - jnp.mean(rows, axis=-1, keepdims=True)
    spread = jnp.mean(centre * centre, axis=-1, keepdims=True)
    inverse = lax.rsqrt(spread + 1e-05)
    return centre * inverse, inverse


def norm_back(unit, inverse, gain, grad):
    scaled = grad * gain
    first = jnp.mean(scaled, axis=-1, keepdims=True)
    second = jnp.mean(scaled * unit, axis=-1, keepdims=True)
    dgain = jnp.sum(grad * unit, axis=(0, 1))
    dshift = jnp.sum(grad, axis=(0, 1))
    return inverse * (scaled - first - unit * second), dgain, dshift


def gelu_both(inputs):
    rate = 0.7978845608028654
    bent = jnp.tanh(rate * (inputs + 0.044715 * inputs * inputs * inputs))
    value = 0.5 * inputs * (1.0 + bent)
    slope = 0.5 * (1.0 + bent) + 0.5 * inputs * (1.0 - bent * bent) * rate * (
        1.0 + 0.134145 * inputs * inputs
    )
    return value, slope


def heads_of(values, size):
    return values.reshape(values.shape[0], values.shape[1], values.shape[2] // size, size)


def attend(query, keys, values, keeping, size):
    scaling = 1.0 / math.sqrt(size)
    scores = dot("pqhd,pkhd->phqk", heads_of(query, size), heads_of(keys, size)) * scaling
    if keeping is not None:
        scores = jnp.where(keeping[:, None, None, :], scores, -1000000000.0)
    highest = jnp.max(scores, axis=-1, keepdims=True)
    raised = jnp.exp(scores - highest)
    weight = raised / jnp.sum(raised, axis=-1, keepdims=True)
    context = dot("phqk,pkhd->pqhd", weight.astype(LOW), heads_of(values, size))
    return context.reshape(query.shape).astype(LOW), weight


def attend_back(query, keys, values, weight, size, dcontext):
    scaling = 1.0 / math.sqrt(size)
    queries, keyed = heads_of(query, size), heads_of(keys, size)
    valued, dheads = heads_of(values, size), heads_of(dcontext, size)
    dvalues = dot("phqk,pqhd->pkhd", weight.astype(LOW), dheads)
    dweight = dot("pqhd,pkhd->phqk", dheads, valued)
    dscores = weight * (dweight - jnp.sum(dweight * weight, axis=-1, keepdims=True))
    dscores = dscores.astype(LOW)
    dquery = dot("phqk,pkhd->pqhd", dscores, keyed) * scaling
    dkeys = dot("phqk,pqhd->pkhd", dscores, queries) * scaling
    return (
        dquery.reshape(query.shape).astype(LOW),
        dkeys.reshape(keys.shape).astype(LOW),
        dvalues.reshape(values.shape).astype(LOW),
    )


def project(values, weights):
    return [dot("pld,dce->cple", values, half).astype(LOW) for half in weights]


def project_back(grads, weights):
    return sum(dot("cple,dce->pld", grad, half) for grad, half in zip(grads, weights))


def tail(residual, contexts, out_w, gain, shift, up_w, down_w):
    branch = sum(dot("ple,ed->pld", c, w) for c, w in zip(contexts, out_w))
    unit1, inv1 = norm_parts(residual.astype(FULL) + branch)
    normed = unit1 * gain[0] + shift[0]
    low_normed = normed.astype(LOW)
    uppers = [dot("pld,df->plf", low_normed, w) for w in up_w]
    both = [gelu_both(u) for u in uppers]
    hidden = [value.astype(LOW) for value, unused in both]
    mixed = sum(dot("plf,fd->pld", h, w) for h, w in zip(hidden, down_w))
    unit2, inv2 = norm_parts(normed + mixed)
    out = unit2 * gain[1] + shift[1]
    kept = (unit1, inv1, low_normed, [slope for unused, slope in both], hidden, unit2, inv2)
    return out, kept


def tail_back(kept, seed, out_w, gain, up_w, down_w):
    unit1, inv1, low_normed, slopes, hidden, unit2, inv2 = kept
    dsecond, dgain1, dshift1 = norm_back(unit2, inv2, gain[1], seed)
    dmixed = dsecond.astype(LOW)
    duppers = [
        (dot("pld,fd->plf", dmixed, w) * slope).astype(LOW) for w, slope in zip(down_w, slopes)
    ]
    dnormed = dsecond + sum(dot("plf,df->pld", du, w) for du, w in zip(duppers, up_w))
    dfirst, dgain0, dshift0 = norm_back(unit1, inv1, gain[0], dnormed)
    dbranch = dfirst.astype(LOW)
    dcontexts = [dot("pld,ed->ple", dbranch, w).astype(LOW) for w in out_w]
    gains = (jnp.stack([dgain0, dgain1]), jnp.stack([dshift0, dshift1]))
    return dfirst, dcontexts, (dmixed, duppers, dbranch), gains


def pair_up(weight, core_route):
    return [weight, lax.ppermute(weight, "tensor", core_route)]


def bit_route(axis, bit):
    return [(i, i ^ (1 << bit)) for i in range(lax.axis_size(axis))]


def scatter_sum(block, order):
    place = lax.axis_index("dp")
    for bit in order:
        high = (place >> bit) & 1
        halves = block.reshape((2, block.shape[0] // 2) + block.shape[1:])
        keep = lax.dynamic_index_in_dim(halves, high, 0, keepdims=False)
        give = lax.dynamic_index_in_dim(halves, 1 - high, 0, keepdims=False)
        got = lax.ppermute(give, "dp", bit_route("dp", bit))
        block = (keep.astype(FULL) + got.astype(FULL)).astype(LOW)
    return block


def gather_back(block, order):
    place = lax.axis_index("dp")
    for bit in reversed(order):
        high = ((place >> bit) & 1) == 1
        got = lax.ppermute(block, "dp", bit_route("dp", bit))
        block = jnp.concatenate([jnp.where(high, got, block), jnp.where(high, block, got)], axis=0)
    return block


def shards(
    text_stream,
    image_stream,
    region_mask,
    co_text_in,
    co_text_out,
    self_text_in,
    self_text_out,
    image_attn_in,
    image_attn_out,
    text_up,
    text_down,
    image_up,
    image_down,
    text_gain,
    text_shift,
    image_gain,
    image_shift,
):
    front = lax.axis_index("section") == 0
    core = lax.axis_index("tensor")
    core_route = [(0, 1), (1, 0)]
    pairs = text_stream.shape[1] // 2
    own = lambda values: lax.dynamic_slice_in_dim(values, core * pairs, pairs, 0)
    co_size = D_CO // HEADS_CO
    text_size = D_TEXT // HEADS_TEXT
    image_size = D_IMAGE // HEADS_IMAGE
    text_own = own(text_stream[0])
    image_own = own(image_stream[0])
    keeping = own(region_mask) > 0
    gain_t, shift_t, gain_i, shift_i = text_gain[0], text_shift[0], image_gain[0], image_shift[0]
    image_in = pair_up(image_attn_in[0], core_route)
    cross_in = pair_up(co_text_in, core_route)
    image_out = pair_up(image_attn_out[0], core_route)
    cross_out = pair_up(co_text_out, core_route)
    up_t = pair_up(text_up[0], core_route)
    down_t = pair_up(text_down[0], core_route)
    up_i = pair_up(image_up[0], core_route)
    down_i = pair_up(image_down[0], core_route)
    single_in = pair_up(self_text_in, core_route)
    single_out = pair_up(self_text_out, core_route)

    tp1 = project(text_own, cross_in)
    ip1 = project(image_own, image_in)
    ct1, wt1 = zip(*[attend(t[0], i[1], i[2], keeping, co_size) for t, i in zip(tp1, ip1)])
    ci1, wi1 = zip(*[attend(i[0], t[1], t[2], None, co_size) for t, i in zip(tp1, ip1)])
    out_t1, kept_t1 = tail(text_own, ct1, cross_out, gain_t, shift_t, up_t, down_t)
    out_i1, kept_i1 = tail(image_own, ci1, image_out, gain_i, shift_i, up_i, down_i)
    bt = lax.ppermute(out_t1.astype(LOW), "section", core_route)
    bi = lax.ppermute(out_i1.astype(LOW), "section", core_route)

    tp2 = project(bt, single_in)
    ip2 = project(bi, image_in)
    ct2, wt2 = zip(*[attend(t[0], t[1], t[2], None, text_size) for t in tp2])
    ci2, wi2 = zip(*[attend(i[0], i[1], i[2], keeping, image_size) for i in ip2])
    out_t2, kept_t2 = tail(bt, ct2, single_out, gain_t, shift_t, up_t, down_t)
    out_i2, kept_i2 = tail(bi, ci2, image_out, gain_i, shift_i, up_i, down_i)
    dres_t2, dct2, grads_t2, gains_t2 = tail_back(
        kept_t2, text_own.astype(FULL), single_out, gain_t, up_t, down_t
    )
    dres_i2, dci2, grads_i2, gains_i2 = tail_back(
        kept_i2, image_own.astype(FULL), image_out, gain_i, up_i, down_i
    )
    dtp2 = [
        jnp.stack(attend_back(t[0], t[1], t[2], w, text_size, dc))
        for t, w, dc in zip(tp2, wt2, dct2)
    ]
    dip2 = [
        jnp.stack(attend_back(i[0], i[1], i[2], w, image_size, dc))
        for i, w, dc in zip(ip2, wi2, dci2)
    ]
    dbt = (dres_t2 + project_back(dtp2, single_in)).astype(LOW)
    dbi = (dres_i2 + project_back(dip2, image_in)).astype(LOW)
    seed_t = lax.ppermute(dbt, "section", core_route).astype(FULL)
    seed_i = lax.ppermute(dbi, "section", core_route).astype(FULL)

    dres_t1, dct1, grads_t1, gains_t1 = tail_back(kept_t1, seed_t, cross_out, gain_t, up_t, down_t)
    dres_i1, dci1, grads_i1, gains_i1 = tail_back(kept_i1, seed_i, image_out, gain_i, up_i, down_i)
    dtp1, dip1 = [], []
    for half in range(2):
        t, i = tp1[half], ip1[half]
        tq, ik, iv = attend_back(t[0], i[1], i[2], wt1[half], co_size, dct1[half])
        iq, tk, tv = attend_back(i[0], t[1], t[2], wi1[half], co_size, dci1[half])
        dtp1.append(jnp.stack([tq, tk, tv]))
        dip1.append(jnp.stack([iq, ik, iv]))
    dxt = dres_t1 + project_back(dtp1, cross_in)
    dxi = dres_i1 + project_back(dip1, image_in)

    def choose(first, second):
        return jnp.where(front, first, second)

    def padded(values, like):
        grow = [(0, 0)] * (values.ndim - 1) + [(0, like.shape[-1] - values.shape[-1])]
        return jnp.pad(values, grow)

    def crossed(mine, given):
        return jnp.concatenate([mine, lax.ppermute(given, "tensor", core_route)], axis=-3)

    def split_factor(halves):
        return crossed(halves[0], halves[1])

    def whole_factor(values):
        return crossed(values, values)

    def select_halves(first, second):
        return [choose(a, padded(b, a)) for a, b in zip(first, second)]

    df_t, du_t, da_t = [
        select_halves(a, b) if isinstance(a, list) else choose(a, b)
        for a, b in zip(grads_t1, grads_t2)
    ]
    df_i, du_i, da_i = [
        select_halves(a, b) if isinstance(a, list) else choose(a, b)
        for a, b in zip(grads_i1, grads_i2)
    ]
    y_t, y_i = choose(kept_t1[2], kept_t2[2]), choose(kept_i1[2], kept_i2[2])
    hid_t = select_halves(kept_t1[4], kept_t2[4])
    hid_i = select_halves(kept_i1[4], kept_i2[4])
    c_t = select_halves(ct1, ct2)
    c_i = select_halves(ci1, ci2)
    dtp = select_halves(dtp1, dtp2)
    dip = select_halves(dip1, dip2)
    x_t, x_i = choose(text_own, bt), choose(image_own, bi)

    plain = "pla,plb->ab"
    y_order = tuple(range(lax.axis_size("dp").bit_length() - 1))
    z_order = y_order[1:] + y_order[:1]
    pieces = {}
    pieces["down_t"] = (dot(plain, split_factor(hid_t), whole_factor(df_t)), y_order)
    pieces["up_t"] = (dot(plain, whole_factor(y_t), split_factor(du_t)), y_order)
    pieces["down_i"] = (dot(plain, split_factor(hid_i), whole_factor(df_i)), y_order)
    pieces["up_i"] = (dot(plain, whole_factor(y_i), split_factor(du_i)), z_order)
    pieces["out_t"] = (dot(plain, split_factor(c_t), whole_factor(da_t)), y_order)
    pieces["out_i"] = (dot(plain, split_factor(c_i), whole_factor(da_i)), z_order)
    pieces["in_t"] = (dot("pla,cplb->acb", whole_factor(x_t), split_factor(dtp)), y_order)
    pieces["in_i"] = (dot("pla,cplb->acb", whole_factor(x_i), split_factor(dip)), y_order)
    sums = {
        name: scatter_sum(value.astype(LOW), order) for name, (value, order) in pieces.items()
    }
    wholes = {}
    for name in ("in_t", "out_t", "in_i", "out_i", "down_t", "up_t", "down_i", "up_i"):
        wholes[name] = gather_back(sums[name], pieces[name][1])
    in_t, out_t = wholes["in_t"], wholes["out_t"]
    other_in = lax.ppermute(in_t, "section", core_route)
    other_out = lax.ppermute(out_t, "section", core_route)
    single_width = self_text_in.shape[2]
    co_in_grad = choose(in_t, other_in).astype(FULL)
    co_out_grad = choose(out_t, other_out).astype(FULL)
    self_in_grad = choose(other_in, in_t)[:, :, :single_width].astype(FULL)
    self_out_grad = choose(other_out, out_t)[:single_width].astype(FULL)

    small = [choose(a, b) for a, b in zip(gains_t1 + gains_i1, gains_t2 + gains_i2)]
    widths = [value.shape[1] for value in small]
    flat = jnp.concatenate(small, axis=1)
    flat = flat + lax.ppermute(flat, "tensor", core_route)
    for bit in y_order:
        flat = flat + lax.ppermute(flat, "dp", bit_route("dp", bit))
    starts = [sum(widths[:n]) for n in range(4)]
    small = [flat[:, s : s + w] for s, w in zip(starts, widths)]

    def joined(values):
        values = values.astype(LOW)
        got = lax.ppermute(values, "tensor", core_route)
        low = core == 0
        return jnp.concatenate([jnp.where(low, values, got), jnp.where(low, got, values)], axis=0)

    text_result = joined(choose(dxt, out_t2))
    image_result = joined(choose(dxi, out_i2))
    return (
        text_result[None],
        image_result[None],
        co_in_grad,
        co_out_grad,
        self_in_grad,
        self_out_grad,
        wholes["in_i"].astype(FULL)[None],
        wholes["out_i"].astype(FULL)[None],
        wholes["up_t"].astype(FULL)[None],
        wholes["down_t"].astype(FULL)[None],
        wholes["up_i"].astype(FULL)[None],
        wholes["down_i"].astype(FULL)[None],
        small[0][None],
        small[1][None],
        small[2][None],
        small[3][None],
    )


def solution(mesh):
    in_specs = (
        P("section", "dp", None, None),
        P("section", "dp", None, None),
        P("dp", None),
        P(None, None, "tensor"),
        P("tensor", None),
        P(None, None, "tensor"),
        P("tensor", None),
        P("section", None, None, "tensor"),
        P("section", "tensor", None),
        P("section", None, "tensor"),
        P("section", "tensor", None),
        P("section", None, "tensor"),
        P("section", "tensor", None),
        P("section", None, None),
        P("section", None, None),
        P("section", None, None),
        P("section", None, None),
    )
    out_specs = (
        P("section", "dp", None, None),
        P("section", "dp", None, None),
        P(None, None, "tensor"),
        P("tensor", None),
        P(None, None, "tensor"),
        P("tensor", None),
        P("section", None, None, "tensor"),
        P("section", "tensor", None),
        P("section", None, "tensor"),
        P("section", "tensor", None),
        P("section", None, "tensor"),
        P("section", "tensor", None),
        P("section", None, None),
        P("section", None, None),
        P("section", None, None),
        P("section", None, None),
    )
    return jax.shard_map(shards, mesh=mesh, in_specs=in_specs, out_specs=out_specs, check_vma=False)
```

profile of v0, /device:TPU:0, one launch (start us, length us, event | category | flops | bytes accessed | tf_op | source)
XLA Modules:
  0.0 831.1 jit_solution(13698401357073835747)
XLA Ops:
  97.3 3.6 broadcast_select_fusion.8
  239.1 3.8 fusion.100
  243.1 3.9 fusion.152
  253.9 4.0 broadcast_select_fusion.11
  259.3 3.8 broadcast_select_fusion.10
  269.2 3.6 fusion.308
  280.0 3.6 fusion.309
  317.6 4.2 fusion.103
  370.8 5.9 collective-permute-done.27
  387.8 18.8 %collective-permute-done.28 = bf16[128,768]{1,0:T(8,128)(2,1)S(1)} collective-permute-done((bf16[128,768]{1,0:T(8,128)(2,1)S(1)}, bf16[128,768]{1,0:T(8,128)(2,1)S(1)}, u32[]{:S(2)}, u32[]{:S(2)}) %collective-permute-start.28) | collective-permute-done | bytes 196640 | tf_op jit(solution)/shard_map/ppermute | solution.py:135
  423.5 18.6 %collective-permute-done.76 = bf16[256,1024]{1,0:T(8,128)(2,1)S(1)} collective-permute-done((bf16[256,1024]{1,0:T(8,128)(2,1)S(1)}, bf16[256,1024]{1,0:T(8,128)(2,1)S(1)}, u32[]{:S(2)}, u32[]{:S(2)}) %collective-permute-start.76) | collective-permute-done | bytes 524320 | tf_op jit(solution)/shard_map/ppermute | solution.py:135
  449.7 18.7 %collective-permute-done.70 = bf16[128,512]{1,0:T(8,128)(2,1)S(1)} collective-permute-done((bf16[128,512]{1,0:T(8,128)(2,1)S(1)}, bf16[128,512]{1,0:T(8,128)(2,1)S(1)}, u32[]{:S(2)}, u32[]{:S(2)}) %collective-permute-start.70) | collective-permute-done | bytes 131104 | tf_op jit(solution)/shard_map/ppermute | solution.py:135
  471.6 4.7 collective-permute-done.77
  478.9 35.4 %collective-permute-done.71 = bf16[128,512]{1,0:T(8,128)(2,1)S(1)} collective-permute-done((bf16[128,512]{1,0:T(8,128)(2,1)S(1)}, bf16[128,512]{1,0:T(8,128)(2,1)S(1)}, u32[]{:S(2)}, u32[]{:S(2)}) %collective-permute-start.71) | collective-permute-done | bytes 131104 | tf_op jit(solution)/shard_map/ppermute | solution.py:144
  521.9 4.7 collective-permute-done.78
  536.0 4.6 collective-permute-done.79
  544.6 8.4 %collective-permute-done.72 = bf16[256,512]{1,0:T(8,128)(2,1)S(1)} collective-permute-done((bf16[256,512]{1,0:T(8,128)(2,1)S(1)}, bf16[256,512]{1,0:T(8,128)(2,1)S(1)}, u32[]{:S(2)}, u32[]{:S(2)}) %collective-permute-start.72) | collective-permute-done | bytes 262176 | tf_op jit(solution)/shard_map/ppermute | solution.py:144
  553.0 10.1 %collective-permute-start.80 = (bf16[128,1024]{1,0:T(8,128)(2,1)S(1)}, bf16[128,1024]{1,0:T(8,128)(2,1)S(1)}, u32[]{:S(2)}, u32[]{:S(2)}) collective-permute-start(bf16[128,1024]{1,0:T(8,128)(2,1)S(1)} %pad_maximum_fusion.24), channel_id=1, source_target_pairs={{0,4},{2,6},{4,0},{6,2},{8,12},{10,14},{12,8},{14,10},{1,5},{3,7},... | collective-permute-start | bytes 786440 | tf_op jit(solution)/shard_map/ppermute | solution.py:144
  563.9 6.4 collective-permute-done.80
  575.4 19.5 %collective-permute-done.73 = bf16[512,512]{1,0:T(8,128)(2,1)S(1)} collective-permute-done((bf16[512,512]{1,0:T(8,128)(2,1)S(1)}, bf16[512,512]{1,0:T(8,128)(2,1)S(1)}, u32[]{:S(2)}, u32[]{:S(2)}) %collective-permute-start.73) | collective-permute-done | bytes 524320 | tf_op jit(solution)/shard_map/ppermute | solution.py:144
  594.9 4.6 collective-permute-start.81
  601.5 12.5 %collective-permute-done.62 = bf16[192,768]{1,0:T(8,128)(2,1)S(1)} collective-permute-done((bf16[192,768]{1,0:T(8,128)(2,1)S(1)}, bf16[192,768]{1,0:T(8,128)(2,1)S(1)}, u32[]{:S(2)}, u32[]{:S(2)}) %collective-permute-start.62) | collective-permute-done | bytes 294944 | tf_op jit(solution)/shard_map/ppermute | solution.py:135
  625.9 12.8 %collective-permute-done.19 = bf16[192,3,512]{2,0,1:T(8,128)(2,1)S(1)} collective-permute-done((bf16[192,3,512]{2,0,1:T(8,128)(2,1)S(1)}, bf16[192,3,512]{2,0,1:T(8,128)(2,1)S(1)}, u32[]{:S(2)}, u32[]{:S(2)}) %collective-permute-start.19) | collective-permute-done | bytes 589856 | tf_op jit(solution)/shard_map/ppermute | solution.py:135
  642.6 21.0 %collective-permute-done.20 = bf16[96,3,512]{2,0,1:T(8,128)(2,1)S(1)} collective-permute-done((bf16[96,3,512]{2,0,1:T(8,128)(2,1)S(1)}, bf16[96,3,512]{2,0,1:T(8,128)(2,1)S(1)}, u32[]{:S(2)}, u32[]{:S(2)}) %collective-permute-start.20) | collective-permute-done | bytes 294944 | tf_op jit(solution)/shard_map/ppermute | solution.py:135
  670.0 16.0 %collective-permute-done.21 = bf16[96,3,512]{2,0,1:T(8,128)(2,1)S(1)} collective-permute-done((bf16[96,3,512]{2,0,1:T(8,128)(2,1)S(1)}, bf16[96,3,512]{2,0,1:T(8,128)(2,1)S(1)}, u32[]{:S(2)}, u32[]{:S(2)}) %collective-permute-start.21) | collective-permute-done | bytes 294944 | tf_op jit(solution)/shard_map/ppermute | solution.py:144
  692.2 17.8 %collective-permute-done.38 = bf16[128,3,512]{2,0,1:T(8,128)(2,1)S(1)} collective-permute-done((bf16[128,3,512]{2,0,1:T(8,128)(2,1)S(1)}, bf16[128,3,512]{2,0,1:T(8,128)(2,1)S(1)}, u32[]{:S(2)}, u32[]{:S(2)}) %collective-permute-start.38) | collective-permute-done | bytes 393248 | tf_op jit(solution)/shard_map/ppermute | solution.py:135
  714.9 15.4 %collective-permute-done.39 = bf16[128,3,512]{2,0,1:T(8,128)(2,1)S(1)} collective-permute-done((bf16[128,3,512]{2,0,1:T(8,128)(2,1)S(1)}, bf16[128,3,512]{2,0,1:T(8,128)(2,1)S(1)}, u32[]{:S(2)}, u32[]{:S(2)}) %collective-permute-start.39) | collective-permute-done | bytes 393248 | tf_op jit(solution)/shard_map/ppermute | solution.py:144
  733.1 11.3 %collective-permute-done.40 = bf16[256,3,512]{2,0,1:T(8,128)(2,1)S(1)} collective-permute-done((bf16[256,3,512]{2,0,1:T(8,128)(2,1)S(1)}, bf16[256,3,512]{2,0,1:T(8,128)(2,1)S(1)}, u32[]{:S(2)}, u32[]{:S(2)}) %collective-permute-start.40) | collective-permute-done | bytes 786464 | tf_op jit(solution)/shard_map/ppermute | solution.py:144
  747.2 21.0 %collective-permute-done.65 = bf16[768,768]{1,0:T(8,128)(2,1)S(1)} collective-permute-done((bf16[768,768]{1,0:T(8,128)(2,1)S(1)}, bf16[768,768]{1,0:T(8,128)(2,1)S(1)}, u32[]{:S(2)}, u32[]{:S(2)}) %collective-permute-start.65) | collective-permute-done | bytes 1179680 | tf_op jit(solution)/shard_map/ppermute | solution.py:144
  771.2 22.3 %collective-permute-done.57 = bf16[384,1536]{1,0:T(8,128)(2,1)S(1)} collective-permute-done((bf16[384,1536]{1,0:T(8,128)(2,1)S(1)}, bf16[384,1536]{1,0:T(8,128)(2,1)S(1)}, u32[]{:S(2)}, u32[]{:S(2)}) %collective-permute-start.57) | collective-permute-done | bytes 1179680 | tf_op jit(solution)/shard_map/ppermute | solution.py:144
  796.7 24.8 %collective-permute-done.41 = bf16[512,3,512]{2,0,1:T(8,128)(2,1)S(1)} collective-permute-done((bf16[512,3,512]{2,0,1:T(8,128)(2,1)S(1)}, bf16[512,3,512]{2,0,1:T(8,128)(2,1)S(1)}, u32[]{:S(2)}, u32[]{:S(2)}) %collective-permute-start.41) | collective-permute-done | bytes 1572896 | tf_op jit(solution)/shard_map/ppermute | solution.py:144
  822.2 3.6 maximum_convert_fusion
  (1088 shorter events, 456.3 us)
Async XLA Ops:
  1.3 53.2 %collective-permute-start.9 = (bf16[512,1024]{1,0:T(8,128)(2,1)}, bf16[512,1024]{1,0:T(8,128)(2,1)}, u32[]{:S(2)}, u32[]{:S(2)}) collective-permute-start(bf16[512,1024]{1,0:T(8,128)(2,1)} %bitcast.861), channel_id=1, source_target_pairs={{0,1},{1,0},{2,3},{3,2},{4,5},{5,4},{6,7},{7,6},{8,9},{9,8},{10,11... | collective-permute-start | bytes 3145736 | tf_op jit(solution)/shard_map/ppermute | solution.py:121
  1.7 60.7 %collective-permute-start.11 = (bf16[512,1024]{1,0:T(8,128)(2,1)}, bf16[512,1024]{1,0:T(8,128)(2,1)}, u32[]{:S(2)}, u32[]{:S(2)}) collective-permute-start(bf16[512,1024]{1,0:T(8,128)(2,1)} %bitcast.871), channel_id=1, source_target_pairs={{0,1},{1,0},{2,3},{3,2},{4,5},{5,4},{6,7},{7,6},{8,9},{9,8},{10,11... | collective-permute-start | bytes 3145736 | tf_op jit(solution)/shard_map/ppermute | solution.py:121
  1.8 40.0 %collective-permute-start.2 = (bf16[512,768]{1,0:T(8,128)(2,1)}, bf16[512,768]{1,0:T(8,128)(2,1)}, u32[]{:S(2)}, u32[]{:S(2)}) collective-permute-start(bf16[512,768]{1,0:T(8,128)(2,1)} %param.21), channel_id=1, source_target_pairs={{0,1},{1,0},{2,3},{3,2},{4,5},{5,4},{6,7},{7,6},{8,9},{9,8},{10,11... | collective-permute-start | bytes 2359304 | tf_op jit(solution)/shard_map/ppermute | solution.py:121
  16.8 33.6 %collective-permute-start.4 = (bf16[1536,768]{1,0:T(8,128)(2,1)}, bf16[1536,768]{1,0:T(8,128)(2,1)}, u32[]{:S(2)}, u32[]{:S(2)}) collective-permute-start(bf16[1536,768]{1,0:T(8,128)(2,1)} %bitcast.23), channel_id=1, source_target_pairs={{0,1},{1,0},{2,3},{3,2},{4,5},{5,4},{6,7},{7,6},{8,9},{9,8},{10,11... | collective-permute-start | bytes 7077896 | tf_op jit(solution)/shard_map/ppermute | solution.py:121
  50.4 38.9 %collective-permute-start.7 = (bf16[384,768]{1,0:T(8,128)(2,1)}, bf16[384,768]{1,0:T(8,128)(2,1)}, u32[]{:S(2)}, u32[]{:S(2)}) collective-permute-start(bf16[384,768]{1,0:T(8,128)(2,1)} %param.23), channel_id=1, source_target_pairs={{0,1},{1,0},{2,3},{3,2},{4,5},{5,4},{6,7},{7,6},{8,9},{9,8},{10,11... | collective-permute-start | bytes 1769480 | tf_op jit(solution)/shard_map/ppermute | solution.py:121
  65.6 101.6 %collective-permute-start.12 = (bf16[2,100,1024]{2,1,0:T(8,128)(2,1)}, bf16[2,100,1024]{2,1,0:T(8,128)(2,1)}, u32[]{:S(2)}, u32[]{:S(2)}) collective-permute-start(bf16[2,100,1024]{2,1,0:T(8,128)(2,1)} %add_convert_fusion), channel_id=1, source_target_pairs={{0,16},{16,0},{1,17},{17,1},{2,18},{18,2},{3,19},{19,3},{4,20},{20... | collective-permute-start | bytes 1228808 | tf_op jit(solution)/shard_map/ppermute | solution.py:198
  157.8 91.1 %collective-permute-start.8 = (bf16[2,92,768]{2,1,0:T(8,128)(2,1)}, bf16[2,92,768]{2,1,0:T(8,128)(2,1)}, u32[]{:S(2)}, u32[]{:S(2)}) collective-permute-start(bf16[2,92,768]{2,1,0:T(8,128)(2,1)} %fusion.230), channel_id=1, source_target_pairs={{0,16},{16,0},{1,17},{17,1},{2,18},{18,2},{3,19},{19,3},{4,20},{20... | collective-permute-start | bytes 847880 | tf_op jit(solution)/shard_map/ppermute | solution.py:222
  160.7 219.3 %collective-permute-start.16 = (bf16[2,92,768]{2,1,0:T(8,128)(2,1)}, bf16[2,92,768]{2,1,0:T(8,128)(2,1)}, u32[]{:S(2)}, u32[]{:S(2)}) collective-permute-start(bf16[2,92,768]{2,1,0:T(8,128)(2,1)} %bitcast_select_fusion.1), channel_id=1, source_target_pairs={{0,1},{1,0},{2,3},{3,2},{4,5},{5,4},{6,7},{7,6},{8,9},{9,8},{10,11... | collective-permute-start | bytes 847880 | tf_op jit(solution)/shard_map/ppermute | solution.py:245
  161.4 185.6 %collective-permute-start.25 = (bf16[2,92,512]{2,1,0:T(8,128)(2,1)}, bf16[2,92,512]{2,1,0:T(8,128)(2,1)}, u32[]{:S(2)}, u32[]{:S(2)}) collective-permute-start(bf16[2,92,512]{2,1,0:T(8,128)(2,1)} %pad_select_fusion.2), channel_id=1, source_target_pairs={{0,1},{1,0},{2,3},{3,2},{4,5},{5,4},{6,7},{7,6},{8,9},{9,8},{10,11... | collective-permute-start | bytes 565256 | tf_op jit(solution)/shard_map/ppermute | solution.py:245
  161.9 199.0 %collective-permute-start.50 = (bf16[2,92,768]{2,1,0:T(8,128)(2,1)}, bf16[2,92,768]{2,1,0:T(8,128)(2,1)}, u32[]{:S(2)}, u32[]{:S(2)}) collective-permute-start(bf16[2,92,768]{2,1,0:T(8,128)(2,1)} %get-tuple-element.122), channel_id=1, source_target_pairs={{0,1},{1,0},{2,3},{3,2},{4,5},{5,4},{6,7},{7,6},{8,9},{9,8},{10,11... | collective-permute-start | bytes 847880 | tf_op jit(solution)/shard_map/ppermute | solution.py:245
  167.2 174.0 %collective-permute-start.58 = (bf16[2,92,1536]{2,0,1:T(2,128)(2,1)}, bf16[2,92,1536]{2,0,1:T(2,128)(2,1)}, u32[]{:S(2)}, u32[]{:S(2)}) collective-permute-start(bf16[2,92,1536]{2,0,1:T(2,128)(2,1)} %copy.524), channel_id=1, source_target_pairs={{0,1},{1,0},{2,3},{3,2},{4,5},{5,4},{6,7},{7,6},{8,9},{9,8},{10,11... | collective-permute-start | bytes 1695752 | tf_op jit(solution)/shard_map/ppermute | solution.py:245
  248.9 42.8 %collective-permute-start.13 = (bf16[2,100,1024]{2,1,0:T(8,128)(2,1)}, bf16[2,100,1024]{2,1,0:T(8,128)(2,1)}, u32[]{:S(2)}, u32[]{:S(2)}) collective-permute-start(bf16[2,100,1024]{2,1,0:T(8,128)(2,1)} %fusion.152), channel_id=1, source_target_pairs={{0,16},{16,0},{1,17},{17,1},{2,18},{18,2},{3,19},{19,3},{4,20},{20... | collective-permute-start | bytes 1228808 | tf_op jit(solution)/shard_map/ppermute | solution.py:223
  376.7 100.3 %collective-permute-start.60 = (bf16[768,768]{1,0:T(8,128)(2,1)S(1)}, bf16[768,768]{1,0:T(8,128)(2,1)S(1)}, u32[]{:S(2)}, u32[]{:S(2)}) collective-permute-start(bf16[768,768]{1,0:T(8,128)(2,1)S(1)} %dynamic-slice_bitcast_fusion.1), channel_id=1, source_target_pairs={{0,2},{2,0},{4,6},{6,4},{8,10},{10,8},{12,14},{14,12},{1,3},{3,1},... | collective-permute-start | bytes 3538952 | tf_op jit(solution)/shard_map/ppermute | solution.py:135
  378.3 34.6 %collective-permute-start.68 = (bf16[512,512]{1,0:T(8,128)(2,1)S(1)}, bf16[512,512]{1,0:T(8,128)(2,1)S(1)}, u32[]{:S(2)}, u32[]{:S(2)}) collective-permute-start(bf16[512,512]{1,0:T(8,128)(2,1)S(1)} %dynamic-slice_bitcast_fusion.9), channel_id=1, source_target_pairs={{0,4},{2,6},{4,0},{6,2},{8,12},{10,14},{12,8},{14,10},{1,5},{3,7},... | collective-permute-start | bytes 1572872 | tf_op jit(solution)/shard_map/ppermute | solution.py:135
  380.0 164.1 %collective-permute-start.52 = (bf16[384,1536]{1,0:T(8,128)(2,1)S(1)}, bf16[384,1536]{1,0:T(8,128)(2,1)S(1)}, u32[]{:S(2)}, u32[]{:S(2)}) collective-permute-start(bf16[384,1536]{1,0:T(8,128)(2,1)S(1)} %dynamic-slice_bitcast_fusion.2), channel_id=1, source_target_pairs={{0,2},{2,0},{4,6},{6,4},{8,10},{10,8},{12,14},{14,12},{1,3},{3,1},... | collective-permute-start | bytes 3538952 | tf_op jit(solution)/shard_map/ppermute | solution.py:135
  383.2 37.1 %collective-permute-start.44 = (bf16[256,1024]{1,0:T(8,128)(2,1)S(1)}, bf16[256,1024]{1,0:T(8,128)(2,1)S(1)}, u32[]{:S(2)}, u32[]{:S(2)}) collective-permute-start(bf16[256,1024]{1,0:T(8,128)(2,1)S(1)} %dynamic-slice_bitcast_fusion.10), channel_id=1, source_target_pairs={{0,4},{2,6},{4,0},{6,2},{8,12},{10,14},{12,8},{14,10},{1,5},{3,7},... | collective-permute-start | bytes 1572872 | tf_op jit(solution)/shard_map/ppermute | solution.py:135
  418.5 154.1 %collective-permute-start.18 = (bf16[384,3,512]{2,0,1:T(8,128)(2,1)S(1)}, bf16[384,3,512]{2,0,1:T(8,128)(2,1)S(1)}, u32[]{:S(2)}, u32[]{:S(2)}) collective-permute-start(bf16[384,3,512]{2,0,1:T(8,128)(2,1)S(1)} %dynamic-slice_bitcast_fusion.3), channel_id=1, source_target_pairs={{0,2},{2,0},{4,6},{6,4},{8,10},{10,8},{12,14},{14,12},{1,3},{3,1},... | collective-permute-start | bytes 3538952 | tf_op jit(solution)/shard_map/ppermute | solution.py:135
  468.4 145.7 %collective-permute-start.36 = (bf16[512,3,512]{2,0,1:T(8,128)(2,1)S(1)}, bf16[512,3,512]{2,0,1:T(8,128)(2,1)S(1)}, u32[]{:S(2)}, u32[]{:S(2)}) collective-permute-start(bf16[512,3,512]{2,0,1:T(8,128)(2,1)S(1)} %dynamic-slice_bitcast_fusion), channel_id=1, source_target_pairs={{0,2},{2,0},{4,6},{6,4},{8,10},{10,8},{12,14},{14,12},{1,3},{3,1},... | collective-permute-start | bytes 4718600 | tf_op jit(solution)/shard_map/ppermute | solution.py:135
  476.3 51.1 %collective-permute-start.32 = (bf16[256,768]{1,0:T(8,128)(2,1)S(1)}, bf16[256,768]{1,0:T(8,128)(2,1)S(1)}, u32[]{:S(2)}, u32[]{:S(2)}) collective-permute-start(bf16[256,768]{1,0:T(8,128)(2,1)S(1)} %pad_maximum_fusion.21), channel_id=1, source_target_pairs={{0,2},{2,0},{4,6},{6,4},{8,10},{10,8},{12,14},{14,12},{1,3},{3,1},... | collective-permute-start | bytes 1179656 | tf_op jit(solution)/shard_map/ppermute | solution.py:144
  477.0 37.2 %collective-permute-start.71 = (bf16[128,512]{1,0:T(8,128)(2,1)S(1)}, bf16[128,512]{1,0:T(8,128)(2,1)S(1)}, u32[]{:S(2)}, u32[]{:S(2)}) collective-permute-start(bf16[128,512]{1,0:T(8,128)(2,1)S(1)} %fusion.480), channel_id=1, source_target_pairs={{0,2},{2,0},{4,6},{6,4},{8,10},{10,8},{12,14},{14,12},{1,3},{3,1},... | collective-permute-start | bytes 393224 | tf_op jit(solution)/shard_map/ppermute | solution.py:144
  526.6 46.5 %collective-permute-start.61 = (bf16[384,768]{1,0:T(8,128)(2,1)S(1)}, bf16[384,768]{1,0:T(8,128)(2,1)S(1)}, u32[]{:S(2)}, u32[]{:S(2)}) collective-permute-start(bf16[384,768]{1,0:T(8,128)(2,1)S(1)} %dynamic-slice_bitcast_fusion.5), channel_id=1, source_target_pairs={{0,4},{2,6},{4,0},{6,2},{8,12},{10,14},{12,8},{14,10},{1,5},{3,7},... | collective-permute-start | bytes 1769480 | tf_op jit(solution)/shard_map/ppermute | solution.py:135
  563.2 51.6 %collective-permute-start.33 = (bf16[512,768]{1,0:T(8,128)(2,1)S(1)}, bf16[512,768]{1,0:T(8,128)(2,1)S(1)}, u32[]{:S(2)}, u32[]{:S(2)}) collective-permute-start(bf16[512,768]{1,0:T(8,128)(2,1)S(1)} %pad_maximum_fusion.5), channel_id=1, source_target_pairs={{0,16},{16,0},{1,17},{17,1},{2,18},{18,2},{3,19},{19,3},{4,20},{20... | collective-permute-start | bytes 2359304 | tf_op jit(solution)/shard_map/ppermute | solution.py:293
  570.3 31.0 %collective-permute-start.53 = (bf16[192,1536]{1,0:T(8,128)(2,1)S(1)}, bf16[192,1536]{1,0:T(8,128)(2,1)S(1)}, u32[]{:S(2)}, u32[]{:S(2)}) collective-permute-start(bf16[192,1536]{1,0:T(8,128)(2,1)S(1)} %dynamic-slice_bitcast_fusion.6), channel_id=1, source_target_pairs={{0,4},{2,6},{4,0},{6,2},{8,12},{10,14},{12,8},{14,10},{1,5},{3,7},... | collective-permute-start | bytes 1769480 | tf_op jit(solution)/shard_map/ppermute | solution.py:135
  573.1 47.2 %collective-permute-start.49 = (bf16[256,1024]{1,0:T(8,128)(2,1)S(1)}, bf16[256,1024]{1,0:T(8,128)(2,1)S(1)}, u32[]{:S(2)}, u32[]{:S(2)}) collective-permute-start(bf16[256,1024]{1,0:T(8,128)(2,1)S(1)} %pad_maximum_fusion.16), channel_id=1, source_target_pairs={{0,4},{2,6},{4,0},{6,2},{8,12},{10,14},{12,8},{14,10},{1,5},{3,7},... | collective-permute-start | bytes 1572872 | tf_op jit(solution)/shard_map/ppermute | solution.py:144
  620.3 67.5 %collective-permute-start.37 = (bf16[256,3,512]{2,0,1:T(8,128)(2,1)S(1)}, bf16[256,3,512]{2,0,1:T(8,128)(2,1)S(1)}, u32[]{:S(2)}, u32[]{:S(2)}) collective-permute-start(bf16[256,3,512]{2,0,1:T(8,128)(2,1)S(1)} %dynamic-slice_bitcast_fusion.4), channel_id=1, source_target_pairs={{0,4},{2,6},{4,0},{6,2},{8,12},{10,14},{12,8},{14,10},{1,5},{3,7},... | collective-permute-start | bytes 2359304 | tf_op jit(solution)/shard_map/ppermute | solution.py:135
  639.1 30.9 %collective-permute-start.55 = (bf16[96,1536]{1,0:T(8,128)(2,1)S(1)}, bf16[96,1536]{1,0:T(8,128)(2,1)S(1)}, u32[]{:S(2)}, u32[]{:S(2)}) collective-permute-start(bf16[96,1536]{1,0:T(8,128)(2,1)S(1)} %fusion.424), channel_id=1, source_target_pairs={{0,8},{2,10},{4,12},{6,14},{8,0},{10,2},{12,4},{14,6},{1,9},{3,11}... | collective-permute-start | bytes 884744 | tf_op jit(solution)/shard_map/ppermute | solution.py:144
  642.1 49.8 %collective-permute-start.64 = (bf16[384,768]{1,0:T(8,128)(2,1)S(1)}, bf16[384,768]{1,0:T(8,128)(2,1)S(1)}, u32[]{:S(2)}, u32[]{:S(2)}) collective-permute-start(bf16[384,768]{1,0:T(8,128)(2,1)S(1)} %pad_maximum_fusion.15), channel_id=1, source_target_pairs={{0,4},{2,6},{4,0},{6,2},{8,12},{10,14},{12,8},{14,10},{1,5},{3,7},... | collective-permute-start | bytes 1769480 | tf_op jit(solution)/shard_map/ppermute | solution.py:144
  689.9 41.2 %collective-permute-start.56 = (bf16[192,1536]{1,0:T(8,128)(2,1)S(1)}, bf16[192,1536]{1,0:T(8,128)(2,1)S(1)}, u32[]{:S(2)}, u32[]{:S(2)}) collective-permute-start(bf16[192,1536]{1,0:T(8,128)(2,1)S(1)} %pad_maximum_fusion.14), channel_id=1, source_target_pairs={{0,4},{2,6},{4,0},{6,2},{8,12},{10,14},{12,8},{14,10},{1,5},{3,7},... | collective-permute-start | bytes 1769480 | tf_op jit(solution)/shard_map/ppermute | solution.py:144
  730.6 37.6 %collective-permute-start.65 = (bf16[768,768]{1,0:T(8,128)(2,1)S(1)}, bf16[768,768]{1,0:T(8,128)(2,1)S(1)}, u32[]{:S(2)}, u32[]{:S(2)}) collective-permute-start(bf16[768,768]{1,0:T(8,128)(2,1)S(1)} %pad_maximum_fusion.4), channel_id=1, source_target_pairs={{0,2},{2,0},{4,6},{6,4},{8,10},{10,8},{12,14},{14,12},{1,3},{3,1},... | collective-permute-start | bytes 3538952 | tf_op jit(solution)/shard_map/ppermute | solution.py:144
  731.5 62.0 %collective-permute-start.57 = (bf16[384,1536]{1,0:T(8,128)(2,1)S(1)}, bf16[384,1536]{1,0:T(8,128)(2,1)S(1)}, u32[]{:S(2)}, u32[]{:S(2)}) collective-permute-start(bf16[384,1536]{1,0:T(8,128)(2,1)S(1)} %pad_maximum_fusion.3), channel_id=1, source_target_pairs={{0,2},{2,0},{4,6},{6,4},{8,10},{10,8},{12,14},{14,12},{1,3},{3,1},... | collective-permute-start | bytes 3538952 | tf_op jit(solution)/shard_map/ppermute | solution.py:144
  745.5 80.3 %collective-permute-start.24 = (bf16[768,3,512]{2,0,1:T(8,128)(2,1)S(1)}, bf16[768,3,512]{2,0,1:T(8,128)(2,1)S(1)}, u32[]{:S(2)}, u32[]{:S(2)}) collective-permute-start(bf16[768,3,512]{2,0,1:T(8,128)(2,1)S(1)} %pad_maximum_fusion), channel_id=1, source_target_pairs={{0,16},{16,0},{1,17},{17,1},{2,18},{18,2},{3,19},{19,3},{4,20},{20... | collective-permute-start | bytes 7077896 | tf_op jit(solution)/shard_map/ppermute | solution.py:292
  746.4 75.2 %collective-permute-start.41 = (bf16[512,3,512]{2,0,1:T(8,128)(2,1)S(1)}, bf16[512,3,512]{2,0,1:T(8,128)(2,1)S(1)}, u32[]{:S(2)}, u32[]{:S(2)}) collective-permute-start(bf16[512,3,512]{2,0,1:T(8,128)(2,1)S(1)} %pad_maximum_fusion.1), channel_id=1, source_target_pairs={{0,2},{2,0},{4,6},{6,4},{8,10},{10,8},{12,14},{14,12},{1,3},{3,1},... | collective-permute-start | bytes 4718600 | tf_op jit(solution)/shard_map/ppermute | solution.py:144
  (311 other events, 1808.2 us)
where the time goes:
time: 843 us; the launch traced here: 831 us
  waiting for transfers between devices  342 us (41%)
  matrix products  211 us (25%)
  starting transfers between devices  108 us (13%)
  local copies, waits for them, and re-layouts  104 us (12%)
  other arithmetic  60.6 us (7%)
    dot_general x116, matrix products, dot(): return jnp.einsum(spec, left, right, preferred_element_type=FULL)  204 us
    ppermute x24, waiting for transfers between devices, gather_back(): got = lax.ppermute(block, 'dp', bit_route('dp', bit))  195 us
    ppermute x24, waiting for transfers between devices, scatter_sum(): got = lax.ppermute(give, 'dp', bit_route('dp', bit))  142 us
    ppermute x24, starting transfers between devices, gather_back(): got = lax.ppermute(block, 'dp', bit_route('dp', bit))  52.9 us
    ppermute x24, starting transfers between devices, scatter_sum(): got = lax.ppermute(give, 'dp', bit_route('dp', bit))  33.5 us
    unnamed x516, local copies, waits for them, and re-layouts  17.5 us
  transfers between devices with their start and end apart: 86, of which 31 were waited for; matrix products, arithmetic and copies ran while one was open for 43% of the time, Pallas kernels for 0%

commit v1 on v0

v1 whole, which is shorter than its diff:
```python
import functools
import math

import jax
import jax.numpy as jnp
from jax import lax
from jax.experimental import pallas as pl
from jax.experimental.pallas import tpu as pltpu
from jax.sharding import PartitionSpec as P

D_TEXT = 768
HEADS_TEXT = 12
D_IMAGE = 1024
HEADS_IMAGE = 8
D_CO = 1024
HEADS_CO = 8

LOW = jnp.bfloat16
FULL = jnp.float32
TILE = 512
UNIT = 256
ROOM = 56 * 1024 * 1024


def times(left, right):
    return jnp.dot(left, right, preferred_element_type=FULL)


def times_back(left, right):
    return lax.dot_general(left, right, (((1,), (1,)), ((), ())), preferred_element_type=FULL)


def back_times(left, right):
    return lax.dot_general(left, right, (((0,), (0,)), ((), ())), preferred_element_type=FULL)


def norm_rows(rows):
    centre = rows - jnp.mean(rows, axis=-1, keepdims=True)
    spread = jnp.mean(centre * centre, axis=-1, keepdims=True)
    inverse = lax.rsqrt(spread + 1e-05)
    return centre * inverse, inverse


def norm_back(unit, inverse, gain, grad):
    scaled = grad * gain
    first = jnp.mean(scaled, axis=-1, keepdims=True)
    second = jnp.mean(scaled * unit, axis=-1, keepdims=True)
    dgain = jnp.sum(grad * unit, axis=0, keepdims=True)
    dshift = jnp.sum(grad, axis=0, keepdims=True)
    return inverse * (scaled - first - unit * second), dgain, dshift


def gelu_both(inputs):
    rate = 0.7978845608028654
    square = inputs * inputs
    bent = jnp.tanh(rate * inputs * (1.0 + 0.044715 * square))
    half = 0.5 * (1.0 + bent)
    slope = half + 0.5 * inputs * (1.0 - bent * bent) * rate * (1.0 + 0.134145 * square)
    return inputs * half, slope


def softmax_of(query, keys, allowed, size):
    scores = times_back(query, keys) * (1.0 / math.sqrt(size))
    scores = jnp.where(allowed, scores, -1000000000.0)
    raised = jnp.exp(scores - jnp.max(scores, axis=-1, keepdims=True))
    return raised / jnp.sum(raised, axis=-1, keepdims=True)


def attend(query, keys, values, allowed, size):
    if size == query.shape[1]:
        weight = softmax_of(query, keys, allowed, size)
        return times(weight.astype(LOW), values).astype(LOW)
    lower = lax.broadcasted_iota(jnp.int32, query.shape, 1) < size
    nothing = jnp.zeros_like(query)
    parts = []
    for mine in (jnp.where(lower, query, nothing), jnp.where(lower, nothing, query)):
        weight = softmax_of(mine, keys, allowed, size)
        parts.append(times(weight.astype(LOW), values))
    return jnp.where(lower, parts[0], parts[1]).astype(LOW)


def attend_back(query, keys, values, allowed, size, dcontext):
    scaling = 1.0 / math.sqrt(size)

    def one(masked_query, masked_dcontext):
        weight = softmax_of(masked_query, keys, allowed, size)
        dvalues = back_times(weight.astype(LOW), dcontext)
        dweight = times_back(masked_dcontext, values)
        dscores = weight * (dweight - jnp.sum(dweight * weight, axis=-1, keepdims=True))
        dscores = dscores.astype(LOW)
        return times(dscores, keys) * scaling, back_times(dscores, query) * scaling, dvalues

    if size == query.shape[1]:
        results = one(query, dcontext)
    else:
        results = []
        low_q = lax.broadcasted_iota(jnp.int32, query.shape, 1) < size
        low_k = lax.broadcasted_iota(jnp.int32, keys.shape, 1) < size
        zero_q = jnp.zeros_like(query)
        first = one(jnp.where(low_q, query, zero_q), jnp.where(low_q, dcontext, zero_q))
        second = one(jnp.where(low_q, zero_q, query), jnp.where(low_q, zero_q, dcontext))
        for lower, a, b in zip((low_q, low_k, low_k), first, second):
            results.append(jnp.where(lower, a, b))
    return [value.astype(LOW) for value in results]


def wide(column):
    return jnp.broadcast_to(column, (column.shape[0], 128))


def tail_forward(residual, contexts, out_w, gain, shift, up_w, down_w, kept, mixed):
    normed_ref, hidden, slopes, unit1, inv1, unit2, inv2 = kept
    branch = times(contexts[0], out_w[0][...]) + times(contexts[1], out_w[1][...])
    unit, inverse = norm_rows(residual.astype(FULL) + branch)
    unit1[...] = unit
    inv1[...] = wide(inverse)
    normed = unit * gain[0:1, :] + shift[0:1, :]
    normed_ref[...] = normed.astype(LOW)
    mixed[...] = normed
    for half in range(2):
        width = up_w[half].shape[1]
        for start in range(0, width, TILE):
            span = pl.ds(start, TILE)
            value, slope = gelu_both(times(normed_ref[...], up_w[half][:, span]))
            hidden[half][:, span] = value.astype(LOW)
            slopes[half][:, span] = slope
            mixed[...] += times(hidden[half][:, span], down_w[half][span, :])
    unit, inverse = norm_rows(mixed[...])
    unit2[...] = unit
    inv2[...] = wide(inverse)
    return unit * gain[1:2, :] + shift[1:2, :]


def tail_backward(seed, kept, out_w, gain, up_w, down_w, grads, total):
    slopes, unit1, inv1, unit2, inv2 = kept
    df, du, da, dgain, dshift = grads
    dsecond, dgain1, dshift1 = norm_back(unit2[...], inv2[:, 0:1], gain[1:2, :], seed)
    total[...] = dsecond
    df[...] = dsecond.astype(LOW)
    for half in range(2):
        width = up_w[half].shape[1]
        for start in range(0, width, TILE):
            span = pl.ds(start, TILE)
            dhidden = times_back(df[...], down_w[half][span, :])
            du[half][:, span] = (dhidden * slopes[half][:, span]).astype(LOW)
            total[...] += times_back(du[half][:, span], up_w[half][:, span])
    dfirst, dgain0, dshift0 = norm_back(unit1[...], inv1[:, 0:1], gain[0:1, :], total[...])
    dgain[...] = jnp.concatenate([dgain0, dgain1], axis=0)
    dshift[...] = jnp.concatenate([dshift0, dshift1], axis=0)
    total[...] = dfirst
    da[...] = dfirst.astype(LOW)
    return [times_back(da[...], w[...]).astype(LOW) for w in out_w]


def shape_of(rows, columns, kind=LOW):
    return jax.ShapeDtypeStruct((rows, columns), kind)


def launch(body, outputs, args, scratch=(), flag=None, work=0, name=None):
    whole = pl.BlockSpec(memory_space=pltpu.VMEM)
    moved = sum(math.prod(v.shape) * v.dtype.itemsize for v in tuple(args) + tuple(outputs))
    specs = [whole] * len(args)
    if flag is not None:
        specs = [pl.BlockSpec(memory_space=pltpu.SMEM)] + specs
        args = (flag,) + tuple(args)
    return pl.pallas_call(
        body,
        out_shape=tuple(outputs),
        in_specs=specs,
        out_specs=tuple([whole] * len(outputs)),
        scratch_shapes=list(scratch),
        compiler_params=pltpu.CompilerParams(vmem_limit_bytes=ROOM),
        cost_estimate=pl.CostEstimate(flops=work, bytes_accessed=moved, transcendentals=0),
        name=name,
    )(*args)


def rows_at(pair, rows):
    return pl.ds(pl.multiple_of(pair * rows, 16), rows)


def slab(index):
    return pl.ds(index * 128, 128)


def cross_forward(pairs, rows_t, rows_i, real_t, xt, xi, wt, wi, keep, tp, ip, ct, ci):
    width = ct.shape[1]
    for slot in range(3):
        span = pl.ds(slot * width, width)
        tp[:, span] = times(xt[...], wt[:, span]).astype(LOW)
        ip[:, span] = times(xi[...], wi[:, span]).astype(LOW)
    text_keys = lax.broadcasted_iota(jnp.int32, (1, rows_t), 1) < real_t
    slabs = width // 128

    def each(pair, carry):
        at_t, at_i = rows_at(pair, rows_t), rows_at(pair, rows_i)
        kept = keep[pair] > 0
        for n in range(slabs):
            ct[at_t, slab(n)] = attend(
                tp[at_t, slab(n)], ip[at_i, slab(slabs + n)], ip[at_i, slab(2 * slabs + n)], kept, 128
            )
            ci[at_i, slab(n)] = attend(
                ip[at_i, slab(n)],
                tp[at_t, slab(slabs + n)],
                tp[at_t, slab(2 * slabs + n)],
                text_keys,
                128,
            )
        return carry

    lax.fori_loop(0, pairs, each, 0)


def first_tail(x, c0, c1, o0, o1, gain, shift, u0, u1, d0, d1, out, y, h0, h1, s0, s1, n1, i1, n2, i2, mixed):
    kept = (y, (h0, h1), (s0, s1), n1, i1, n2, i2)
    out[...] = tail_forward(
        x[...], (c0[...], c1[...]), (o0, o1), gain, shift, (u0, u1), (d0, d1), kept, mixed
    ).astype(LOW)


def self_layer(
    pairs, rows, real, size, stride, front,
    x, w0, w1, keep, o0, o1, gain, shift, u0, u1, d0, d1, seed, y_in, h0_in, h1_in, c_in,
    out, dx, c0, c1, p0, p1, da, df, du0, du1, y, h0, h1, dgain, dshift,
    q0, q1, s0, s1, n1, i1, n2, i2, mixed, dc0, dc1,
):
    width = w0.shape[1] // 3

    @pl.when(front[0] == 1)
    def pass_on():
        y[...] = y_in[...]
        h0[...] = h0_in[...]
        h1[...] = h1_in[...]
        c0[...] = c_in[...]

    @pl.when(front[0] == 0)
    def work():
        slabs = width // 128
        if c0.shape[1] != width:
            rest = pl.ds(width, c0.shape[1] - width)
            c0[:, rest] = jnp.zeros((c0.shape[0], c0.shape[1] - width), LOW)
            c1[:, rest] = jnp.zeros((c0.shape[0], c0.shape[1] - width), LOW)
            for slot in range(3):
                rest = pl.ds(slot * stride + width, stride - width)
                p0[:, rest] = jnp.zeros((p0.shape[0], stride - width), LOW)
                p1[:, rest] = jnp.zeros((p0.shape[0], stride - width), LOW)
        for w, q in ((w0, q0), (w1, q1)):
            for slot in range(3):
                span = pl.ds(slot * width, width)
                q[:, span] = times(x[...], w[:, span]).astype(LOW)

        def allowed(pair):
            if keep is None:
                return lax.broadcasted_iota(jnp.int32, (1, rows), 1) < real
            return keep[pair] > 0

        def forward(pair, carry):
            at = rows_at(pair, rows)
            for q, c in ((q0, c0), (q1, c1)):
                for n in range(slabs):
                    c[at, slab(n)] = attend(
                        q[at, slab(n)],
                        q[at, slab(slabs + n)],
                        q[at, slab(2 * slabs + n)],
                        allowed(pair),
                        size,
                    )
            return carry

        lax.fori_loop(0, pairs, forward, 0)
        used = pl.ds(0, width)
        kept = (y, (h0, h1), (s0, s1), n1, i1, n2, i2)
        out[...] = tail_forward(
            x[...], (c0[:, used], c1[:, used]), (o0, o1), gain, shift, (u0, u1), (d0, d1), kept, mixed
        ).astype(LOW)
        dcs = tail_backward(
            seed[...].astype(FULL),
            ((s0, s1), n1, i1, n2, i2),
            (o0, o1),
            gain,
            (u0, u1),
            (d0, d1),
            (df, (du0, du1), da, dgain, dshift),
            mixed,
        )
        dc0[...] = dcs[0]
        dc1[...] = dcs[1]

        def backward(pair, carry):
            at = rows_at(pair, rows)
            for q, dc, p in ((q0, dc0, p0), (q1, dc1, p1)):
                for n in range(slabs):
                    grads = attend_back(
                        q[at, slab(n)],
                        q[at, slab(slabs + n)],
                        q[at, slab(2 * slabs + n)],
                        allowed(pair),
                        size,
                        dc[at, slab(n)],
                    )
                    for slot in range(3):
                        p[at, pl.ds(slot * stride + n * 128, 128)] = grads[slot]
            return carry

        lax.fori_loop(0, pairs, backward, 0)
        for w, p in ((w0, p0), (w1, p1)):
            for slot in range(3):
                mixed[...] += times_back(
                    p[:, pl.ds(slot * stride, width)], w[:, pl.ds(slot * width, width)]
                )
        dx[...] = mixed[...].astype(LOW)


def self_layer_open(pairs, rows, real, size, stride, front, x, w0, w1, *rest):
    self_layer(pairs, rows, real, size, stride, front, x, w0, w1, None, *rest)


def first_tail_back(
    front, seed, s0, s1, n1, i1, n2, i2, o0, o1, gain, u0, u1, d0, d1,
    df_in, du0_in, du1_in, da_in, dgain_in, dshift_in,
    df, du0, du1, da, dgain, dshift, dres, dc0, dc1,
):
    @pl.when(front[0] == 0)
    def pass_on():
        df[...] = df_in[...]
        du0[...] = du0_in[...]
        du1[...] = du1_in[...]
        da[...] = da_in[...]
        dgain[...] = dgain_in[...]
        dshift[...] = dshift_in[...]

    @pl.when(front[0] == 1)
    def work():
        dcs = tail_backward(
            seed[...].astype(FULL),
            ((s0, s1), n1, i1, n2, i2),
            (o0, o1),
            gain,
            (u0, u1),
            (d0, d1),
            (df, (du0, du1), da, dgain, dshift),
            dres,
        )
        dc0[...] = dcs[0]
        dc1[...] = dcs[1]


def cross_backward(
    pairs, rows_t, rows_i, real_t, front,
    tp, ip, dct, dci, keep, wt, wi, dtp0_in, dtp1_in, dip0_in, dip1_in,
    dtp, dip, dxt, dxi,
):
    width = dct.shape[1]
    slabs = width // 128
    half_t, half_i = dtp0_in.shape[0], dip0_in.shape[0]

    @pl.when(front[0] == 0)
    def pass_on():
        dtp[0:half_t, :] = dtp0_in[...]
        dtp[half_t:, :] = dtp1_in[...]
        dip[0:half_i, :] = dip0_in[...]
        dip[half_i:, :] = dip1_in[...]

    @pl.when(front[0] == 1)
    def work():
        text_keys = lax.broadcasted_iota(jnp.int32, (1, rows_t), 1) < real_t

        def each(pair, carry):
            at_t, at_i = rows_at(pair, rows_t), rows_at(pair, rows_i)
            kept = keep[pair] > 0
            for n in range(slabs):
                first, second, third = slab(n), slab(slabs + n), slab(2 * slabs + n)
                dq, dk, dv = attend_back(
                    tp[at_t, first], ip[at_i, second], ip[at_i, third], kept, 128, dct[at_t, first]
                )
                dtp[at_t, first] = dq
                dip[at_i, second] = dk
                dip[at_i, third] = dv
                dq, dk, dv = attend_back(
                    ip[at_i, first], tp[at_t, second], tp[at_t, third], text_keys, 128, dci[at_i, first]
                )
                dip[at_i, first] = dq
                dtp[at_t, second] = dk
                dtp[at_t, third] = dv
            return carry

        lax.fori_loop(0, pairs, each, 0)
        for dp, w, dx in ((dtp, wt, dxt), (dip, wi, dxi)):
            dx[...] = times_back(dp[:, pl.ds(0, width)], w[:, pl.ds(0, width)])
            for slot in range(1, 3):
                span = pl.ds(slot * width, width)
                dx[...] += times_back(dp[:, span], w[:, span])


def round_up(value, step):
    return -(-value // step) * step


def masks_of(order):
    count = len(order)
    return [
        sum(((place >> (count - 1 - n)) & 1) << bit for n, bit in enumerate(order))
        for place in range(1 << count)
    ]


def block_rows(weights, blocks):
    layout, start = [], 0
    for depth, width in weights:
        rows = round_up(depth // blocks, 16)
        layout.append((depth // blocks, rows, start))
        start += rows * (width // UNIT)
    return layout, start


def pack_body(shapes, order, me, *refs):
    count = len(order)
    blocks = 1 << count
    masks = masks_of(order)
    layout, size = block_rows(shapes, blocks)
    factors, rest = refs[: 4 * len(shapes)], refs[4 * len(shapes) :]
    outs, total = rest[: count + 1], rest[count + 1]
    for index, (depth, width) in enumerate(shapes):
        x0, x1, y0, y1 = factors[4 * index : 4 * index + 4]
        real, rows, start = layout[index]
        for column in range(0, width, TILE if width % TILE == 0 else UNIT):
            span = TILE if width % TILE == 0 else UNIT
            area = pl.ds(column, span)
            total[0:depth, 0:span] = back_times(x0[...], y0[:, area]) + back_times(
                x1[...], y1[:, area]
            )
            for place in range(blocks):
                level = place.bit_length()
                target = outs[count - level]
                inside = place - (1 << (level - 1)) if level else 0
                block = me[0] ^ masks[place]
                source = pl.ds(pl.multiple_of(block * real, 8), rows)
                for piece in range(0, span, UNIT):
                    row = inside * size + start + ((column + piece) // UNIT) * rows
                    target[row : row + rows, :] = total[source, piece : piece + UNIT].astype(LOW)


def pack(weights, order, me):
    shapes = [(w[0].shape[1], w[2].shape[1]) for w in weights]
    blocks = 1 << len(order)
    layout, size = block_rows(shapes, blocks)
    sizes = [size << (len(order) - 1 - n) for n in range(len(order))] + [size]
    deepest = max(depth for depth, unused in shapes) + 32
    work = sum(2 * (w[0].shape[0] + w[1].shape[0]) * s[0] * s[1] for w, s in zip(weights, shapes))
    return launch(
        functools.partial(pack_body, shapes, order),
        [shape_of(rows, UNIT) for rows in sizes],
        tuple(v for w in weights for v in w),
        scratch=[pltpu.VMEM((deepest, TILE), FULL)],
        flag=me,
        work=work,
        name="pack",
    )


def unpack_body(shapes, order, me, near, far, *outs):
    place = pl.program_id(0)
    blocks = 1 << len(order)
    layout, size = block_rows(shapes, blocks)

    def write(source):
        for (depth, width), (real, rows, start), out in zip(shapes, layout, outs):
            for column in range(0, width, UNIT):
                row = start + (column // UNIT) * rows
                values = source[row : row + rows, :].astype(FULL)
                out[:, column : column + UNIT] = values[0:real]

    @pl.when(place < blocks // 2)
    def first():
        write(near)

    @pl.when(place >= blocks // 2)
    def second():
        write(far)


def unpack(near, far, shapes, order, me):
    count = len(order)
    blocks = 1 << count
    layout, size = block_rows(shapes, blocks)

    def block_of(place, me):
        mask = 0
        for n, bit in enumerate(order):
            mask = mask | (((place >> (count - 1 - n)) & 1) << bit)
        return me[0] ^ mask

    grid_spec = pltpu.PrefetchScalarGridSpec(
        num_scalar_prefetch=1,
        grid=(blocks,),
        in_specs=[
            pl.BlockSpec((size, UNIT), lambda p, me: (jnp.minimum(p, blocks // 2 - 1), 0)),
            pl.BlockSpec((size, UNIT), lambda p, me: (jnp.maximum(p - blocks // 2, 0), 0)),
        ],
        out_specs=[
            pl.BlockSpec((real, width), lambda p, me: (block_of(p, me), 0))
            for (depth, width), (real, rows, start) in zip(shapes, layout)
        ],
    )
    return pl.pallas_call(
        functools.partial(unpack_body, shapes, order),
        out_shape=tuple(jax.ShapeDtypeStruct(shape, FULL) for shape in shapes),
        grid_spec=grid_spec,
        compiler_params=pltpu.CompilerParams(vmem_limit_bytes=ROOM),
        cost_estimate=pl.CostEstimate(
            flops=0, bytes_accessed=6 * sum(a * b for a, b in shapes), transcendentals=0
        ),
        name="unpack",
    )(me, near, far)


CORES = [(0, 1), (1, 0)]


def to_other_core(values):
    return lax.ppermute(values, "tensor", CORES)


def to_other_section(values):
    return lax.ppermute(values, "section", CORES)


def over_data(values, bit):
    route = [(place, place ^ (1 << bit)) for place in range(lax.axis_size("dp"))]
    return lax.ppermute(values, "dp", route)


def after(values, token):
    if token is None:
        return values
    return lax.optimization_barrier((values, token))[0]


def planned(chunks):
    free = {"low": 0.0, "near": 0.0, "far": 0.0}
    state = {name: [0, ready] for name, order, rows, ready, rank in chunks}
    events = []
    while True:
        best = None
        for name, order, rows, ready, rank in chunks:
            step, moment = state[name]
            count = len(order)
            if step == 2 * count:
                continue
            turn = step if step < count else 2 * count - 1 - step
            bit = order[turn]
            amount = rows << (count - 1 - turn)
            uses = {"low": amount}
            if bit == 1:
                uses = {"near": amount}
            elif bit > 1:
                uses = {"far": amount * bit, "near": amount * 0.5 * bit}
            begin = max([moment] + [free[link] for link in uses])
            key = (begin, rank)
            if best is None or key < best[0]:
                best = (key, name, step, uses, begin)
        if best is None:
            break
        unused, name, step, uses, begin = best
        end = begin + max(uses.values())
        for link, amount in uses.items():
            free[link] = max(free[link], begin + amount)
        state[name] = [step + 1, end + 50]
        events.append((begin, 1, name, step))
        events.append((end, 0, name, step))
    return sorted(events)


def summed(chunks, parts):
    sizes = {chunk[0]: chunk[2] for chunk in chunks}
    orders = {chunk[0]: chunk[1] for chunk in chunks}
    held = {name: list(values) for name, values in parts.items()}
    flying, pieces, token = {}, {name: [] for name in held}, None
    for unused, starting, name, step in planned(chunks):
        order, rows = orders[name], sizes[name]
        count = len(order)
        if starting:
            if step < count:
                given, bit = held[name][step], order[step]
            else:
                given, bit = held[name], order[2 * count - 1 - step]
            if step > 0:
                given = after(given, token)
            flying[name] = over_data(given, bit)
            continue
        got = after(flying.pop(name), token)
        token = got
        if step < count:
            mine = held[name]
            for later in range(step + 1, count):
                first = rows << (count - 1 - later)
                mine[later] = mine[later] + got[first : 2 * first]
            mine[count] = mine[count] + got[:rows]
            if step == count - 1:
                held[name] = mine[count]
                pieces[name].append(mine[count])
        else:
            pieces[name].append(got)
            if step < 2 * count - 1:
                held[name] = jnp.concatenate([held[name], got], axis=0)
    return {name: (held[name], pieces[name][-1]) for name in held}, pieces


def shards(
    text_stream,
    image_stream,
    region_mask,
    co_text_in,
    co_text_out,
    self_text_in,
    self_text_out,
    image_attn_in,
    image_attn_out,
    text_up,
    text_down,
    image_up,
    image_down,
    text_gain,
    text_shift,
    image_gain,
    image_shift,
):
    front = lax.axis_index("section") == 0
    core = lax.axis_index("tensor")
    flag = front.astype(jnp.int32).reshape(1)
    me = lax.axis_index("dp").astype(jnp.int32).reshape(1)
    pairs = text_stream.shape[1]
    half = pairs // 2
    real_t, real_i = text_stream.shape[2], image_stream.shape[2]
    rows_t, rows_i = round_up(real_t, 16), round_up(real_i, 16)
    wide_t, wide_i = text_stream.shape[3], image_stream.shape[3]
    text_size = D_TEXT // HEADS_TEXT
    image_size = D_IMAGE // HEADS_IMAGE

    def own_first(values):
        return jnp.where(core == 0, values, jnp.roll(values, half, axis=0))

    def flat_rows(values, rows):
        grown = jnp.pad(values, ((0, 0), (0, rows - values.shape[1]), (0, 0)))
        return grown.reshape(values.shape[0] * rows, values.shape[2])

    def fold(weight):
        return weight.reshape(weight.shape[0], -1)

    own_t, own_i = half * rows_t, half * rows_i
    all_t, all_i = pairs * rows_t, pairs * rows_i
    xt = flat_rows(own_first(text_stream[0]), rows_t)
    xi = flat_rows(own_first(image_stream[0]), rows_i)
    keep = own_first(jnp.pad(region_mask, ((0, 0), (0, rows_i - real_i)))).reshape(pairs, 1, rows_i)
    gain_t, shift_t, gain_i, shift_i = text_gain[0], text_shift[0], image_gain[0], image_shift[0]
    cross_in, image_in, single_in = fold(co_text_in), fold(image_attn_in[0]), fold(self_text_in)
    image_out, up_i, down_i = image_attn_out[0], image_up[0], image_down[0]
    up_t, down_t = text_up[0], text_down[0]
    image_out_2, cross_out_2 = to_other_core(image_out), to_other_core(co_text_out)
    up_i_2, down_i_2 = to_other_core(up_i), to_other_core(down_i)
    up_t_2, down_t_2 = to_other_core(up_t), to_other_core(down_t)
    image_in_2, single_in_2 = to_other_core(image_in), to_other_core(single_in)
    single_out_2 = to_other_core(self_text_out)
    cross = cross_in.shape[1] // 3
    single = single_in.shape[1] // 3
    ff_t, ff_i = up_t.shape[1], up_i.shape[1]
    tail_t = (up_t, up_t_2, down_t, down_t_2)
    tail_i = (up_i, up_i_2, down_i, down_i_2)

    tp, ip, ct, ci = launch(
        functools.partial(cross_forward, pairs, rows_t, rows_i, real_t),
        [shape_of(all_t, 3 * cross), shape_of(all_i, 3 * cross), shape_of(all_t, cross), shape_of(all_i, cross)],
        (xt, xi, cross_in, image_in, keep),
        work=6 * cross * (all_t * wide_t + all_i * wide_i),
        name="cross_forward",
    )
    ci_2 = to_other_core(ci[own_i:])
    ct_2 = to_other_core(ct[own_t:])

    def tail_shapes(rows, width, hidden):
        return [
            shape_of(rows, width),
            shape_of(rows, width),
            shape_of(rows, hidden),
            shape_of(rows, hidden),
            shape_of(rows, hidden, FULL),
            shape_of(rows, hidden, FULL),
            shape_of(rows, width, FULL),
            shape_of(rows, 128, FULL),
            shape_of(rows, width, FULL),
            shape_of(rows, 128, FULL),
        ]

    def run_first_tail(x, c0, c1, o0, o1, gain, shift, ff, rows, width, hidden, name):
        return launch(
            first_tail,
            tail_shapes(rows, width, hidden),
            (x, c0, c1, o0, o1, gain, shift) + ff,
            scratch=[pltpu.VMEM((rows, width), FULL)],
            work=4 * rows * width * (o0.shape[0] + 2 * hidden),
            name=name,
        )

    bi, yi, hi0, hi1, si0, si1, ni1, ii1, ni2, ii2 = run_first_tail(
        xi[:own_i], ci[:own_i], ci_2, image_out, image_out_2, gain_i, shift_i, tail_i, own_i, wide_i, ff_i, "tail_i"
    )
    bi = to_other_section(bi)
    bt, yt, ht0, ht1, st0, st1, nt1, it1, nt2, it2 = run_first_tail(
        xt[:own_t], ct[:own_t], ct_2, co_text_out, cross_out_2, gain_t, shift_t, tail_t, own_t, wide_t, ff_t, "tail_t"
    )
    bt = to_other_section(bt)

    def run_self(rows, real, size, width, hidden, x, w0, w1, masked, o0, o1, gain, shift, ff, seed, y, h0, h1, c, name):
        count = half * rows
        inner = w0.shape[1] // 3
        body = functools.partial(self_layer if masked else self_layer_open, half, rows, real, size, cross)
        low_w, low_h = shape_of(count, width), shape_of(count, hidden)
        grads = [shape_of(2, width, FULL)] * 2
        outputs = [low_w, low_w] + [shape_of(count, cross)] * 2 + [shape_of(count, 3 * cross)] * 2
        outputs += [low_w, low_w, low_h, low_h, low_w, low_h, low_h] + grads
        scratch = [pltpu.VMEM((count, 3 * inner), LOW)] * 2
        scratch += [pltpu.VMEM((count, hidden), FULL)] * 2
        scratch += [pltpu.VMEM((count, width), FULL), pltpu.VMEM((count, 128), FULL)] * 2
        scratch += [pltpu.VMEM((count, width), FULL)] + [pltpu.VMEM((count, inner), LOW)] * 2
        return launch(
            body,
            outputs,
            (x, w0, w1) + ((keep,) if masked else ()) + (o0, o1, gain, shift) + ff + (seed, y, h0, h1, c),
            scratch=scratch,
            flag=flag,
            work=8 * count * width * (4 * inner + 2 * hidden),
            name=name,
        )

    i2 = run_self(
        rows_i, real_i, image_size, wide_i, ff_i, bi, image_in, image_in_2, True, image_out, image_out_2,
        gain_i, shift_i, tail_i, xi[:own_i], yi, hi0, hi1, ci[:own_i], "self_i",
    )
    seed_i = to_other_section(i2[1])
    t2 = run_self(
        rows_t, real_t, text_size, wide_t, ff_t, bt, single_in, single_in_2, False, self_text_out, single_out_2,
        gain_t, shift_t, tail_t, xt[:own_t], yt, ht0, ht1, ct[:own_t], "self_t",
    )
    seed_t = to_other_section(t2[1])
    (oi, unused, ci_own, ci_give, pi0, pi1, dai, dfi, dui0, dui1, yi, hi0, hi1, dgi, dsi) = i2
    (ot, unused, ct_own, ct_give, pt0, pt1, dat, dft, dut0, dut1, yt, ht0, ht1, dgt, dst) = t2

    def run_tail_back(seed, kept, o0, o1, gain, ff, given, rows, width, hidden, name):
        low_w, low_h = shape_of(rows, width), shape_of(rows, hidden)
        grads = [shape_of(2, width, FULL)] * 2
        outputs = [low_w, low_h, low_h, low_w] + grads + [shape_of(rows, width, FULL)]
        return launch(
            first_tail_back,
            outputs + [shape_of(rows, cross)] * 2,
            (seed,) + kept + (o0, o1, gain) + ff + given,
            flag=flag,
            work=4 * rows * width * (cross + 2 * hidden),
            name=name,
        )

    dfi, dui0, dui1, dai, dgi, dsi, dri, dci_own, dci_give = run_tail_back(
        seed_i, (si0, si1, ni1, ii1, ni2, ii2), image_out, image_out_2, gain_i, tail_i,
        (dfi, dui0, dui1, dai, dgi, dsi), own_i, wide_i, ff_i, "tail_back_i",
    )
    dft, dut0, dut1, dat, dgt, dst, drt, dct_own, dct_give = run_tail_back(
        seed_t, (st0, st1, nt1, it1, nt2, it2), co_text_out, cross_out_2, gain_t, tail_t,
        (dft, dut0, dut1, dat, dgt, dst), own_t, wide_t, ff_t, "tail_back_t",
    )
    dci_2, dct_2 = to_other_core(dci_give), to_other_core(dct_give)
    dtp, dip, dxt, dxi = launch(
        functools.partial(cross_backward, pairs, rows_t, rows_i, real_t),
        [
            shape_of(all_t, 3 * cross),
            shape_of(all_i, 3 * cross),
            shape_of(all_t, wide_t, FULL),
            shape_of(all_i, wide_i, FULL),
        ],
        (
            tp,
            ip,
            jnp.concatenate([dct_own, dct_2], axis=0),
            jnp.concatenate([dci_own, dci_2], axis=0),
            keep,
            cross_in,
            image_in,
            pt0,
            to_other_core(pt1),
            pi0,
            to_other_core(pi1),
        ),
        flag=flag,
        work=6 * cross * (all_t * wide_t + all_i * wide_i),
        name="cross_backward",
    )

    low_bits = tuple(range(lax.axis_size("dp").bit_length() - 1))
    turned = low_bits[1:] + low_bits[:1]

    def choose(first, second):
        return jnp.where(front, first, second)

    ct_other = choose(ct[own_t:], to_other_core(ct_give))
    ci_other = choose(ci[own_i:], to_other_core(ci_give))
    xt_own, xt_other = choose(xt[:own_t], bt), choose(xt[own_t:], to_other_core(bt))
    xi_own, xi_other = choose(xi[:own_i], bi), choose(xi[own_i:], to_other_core(bi))
    up_i_factors = (yi, to_other_core(yi), dui0, to_other_core(dui1))
    down_i_factors = (hi0, to_other_core(hi1), dfi, to_other_core(dfi))
    up_t_factors = (yt, to_other_core(yt), dut0, to_other_core(dut1))
    down_t_factors = (ht0, to_other_core(ht1), dft, to_other_core(dft))
    out_i_factors = (ci_own, ci_other, dai, to_other_core(dai))
    out_t_factors = (ct_own, ct_other, dat, to_other_core(dat))
    in_t_factors = (xt_own, xt_other, dtp[:own_t], dtp[own_t:])
    in_i_factors = (xi_own, xi_other, dip[:own_i], dip[own_i:])
    groups = {
        "ff_i": ((up_i_factors, down_i_factors), turned, 0, 2),
        "up_t": ((up_t_factors,), low_bits, 0, 3),
        "down_t": ((down_t_factors,), low_bits, 0, 4),
        "outs": ((out_i_factors, out_t_factors), low_bits, 150, 0),
        "in_t": ((in_t_factors,), low_bits, 500, 1),
        "in_i": ((in_i_factors,), low_bits, 500, 5),
    }
    parts = {name: pack(group[0], group[1], me) for name, group in groups.items()}
    chunks = [
        (name, group[1], parts[name][-1].shape[0], group[2], group[3]) for name, group in groups.items()
    ]
    sums, pieces = summed(chunks, parts)
    wholes = {}
    for name, (weights, order, unused, unused) in groups.items():
        shapes = [(w[0].shape[1], w[2].shape[1]) for w in weights]
        wholes[name] = unpack(sums[name][0], sums[name][1], shapes, order, me)

    def from_other_section(name):
        got = [to_other_section(piece) for piece in pieces[name]]
        weights, order = groups[name][0], groups[name][1]
        shapes = [(w[0].shape[1], w[2].shape[1]) for w in weights]
        return unpack(jnp.concatenate(got[:-1], axis=0), got[-1], shapes, order, me)

    out_t, in_t = wholes["outs"][1], wholes["in_t"][0]
    other_out, other_in = from_other_section("outs")[1], from_other_section("in_t")[0]

    def slots(values):
        return values.reshape(values.shape[0], 3, cross)

    co_in_grad = slots(choose(in_t, other_in))
    co_out_grad = choose(out_t, other_out)
    self_in_grad = slots(choose(other_in, in_t))[:, :, :single]
    self_out_grad = choose(other_out, out_t)[:single]

    flat = jnp.concatenate([dgt, dst, dgi, dsi], axis=1)
    flat = flat + to_other_core(flat)
    for bit in low_bits:
        flat = flat + over_data(flat, bit)
    ends = [wide_t, 2 * wide_t, 2 * wide_t + wide_i]
    small = jnp.split(flat, ends, axis=1)

    def result(rest, partial, output, count, rows, real):
        mine = choose(rest + partial[:count] + to_other_core(partial[count:]), output.astype(FULL))
        mine = mine.astype(LOW).reshape(half, rows, -1)[:, :real]
        got = to_other_core(mine)
        return jnp.concatenate(
            [jnp.where(core == 0, mine, got), jnp.where(core == 0, got, mine)], axis=0
        )[None]

    return (
        result(drt, dxt, ot, own_t, rows_t, real_t),
        result(dri, dxi, oi, own_i, rows_i, real_i),
        co_in_grad,
        co_out_grad,
        self_in_grad,
        self_out_grad,
        slots(wholes["in_i"][0])[None],
        wholes["outs"][0][None],
        wholes["up_t"][0][None],
        wholes["down_t"][0][None],
        wholes["ff_i"][0][None],
        wholes["ff_i"][1][None],
        small[0][None],
        small[1][None],
        small[2][None],
        small[3][None],
    )


def solution(mesh):
    in_specs = (
        P("section", "dp", None, None),
        P("section", "dp", None, None),
        P("dp", None),
        P(None, None, "tensor"),
        P("tensor", None),
        P(None, None, "tensor"),
        P("tensor", None),
        P("section", None, None, "tensor"),
        P("section", "tensor", None),
        P("section", None, "tensor"),
        P("section", "tensor", None),
        P("section", None, "tensor"),
        P("section", "tensor", None),
        P("section", None, None),
        P("section", None, None),
        P("section", None, None),
        P("section", None, None),
    )
    out_specs = (
        P("section", "dp", None, None),
        P("section", "dp", None, None),
        P(None, None, "tensor"),
        P("tensor", None),
        P(None, None, "tensor"),
        P("tensor", None),
        P("section", None, None, "tensor"),
        P("section", "tensor", None),
        P("section", None, "tensor"),
        P("section", "tensor", None),
        P("section", None, "tensor"),
        P("section", "tensor", None),
        P("section", None, None),
        P("section", None, None),
        P("section", None, None),
        P("section", None, None),
    )
    return jax.shard_map(shards, mesh=mesh, in_specs=in_specs, out_specs=out_specs, check_vma=False)
```

time: 843 us -> 688 us (0.82)
  matrix products: 211 us -> 0 us
  Pallas kernels: 0 us -> 174 us
  waiting for transfers between devices: 342 us -> 261 us
  local copies, waits for them, and re-layouts: 104 us -> 78.3 us
  other arithmetic: 60.6 us -> 40.9 us
  starting transfers between devices: 108 us -> 127 us
    dot_general x116 -> x0, matrix products: 204 us -> none  [dot(): return jnp.einsum(spec, left, right, preferred_element_type=FULL)]
    pallas_call x0 -> x22, Pallas kernels: none -> 174 us  [the longest x14 123 us: launch(): pl.pallas_call(body, out_shape=tuple(outputs), in_specs=specs, out_specs=...]
    ppermute x86 -> x85, waiting for transfers between devices: 342 us -> 261 us  [the longest x39 205 us: over_data(): return lax.ppermute(values, 'dp', route)]
    convert_element_type x58 -> x0, local copies, waits for them, and re-layouts: 51 us -> none  [the longest x14 14.6 us: attend_back(): dkeys.reshape(keys.shape).astype(LOW)]
    convert_element_type x48 -> x2, other arithmetic: 28.2 us -> 0.48 us  [result(): mine = mine.astype(LOW).reshape(half, rows, -1)[:, :real]]
    ppermute x86 -> x85, starting transfers between devices: 108 us -> 127 us  [the longest x39 63.3 us: over_data(): return lax.ppermute(values, 'dp', route)]
    unnamed x516 -> x183, local copies, waits for them, and re-layouts: 17.5 us -> 31.6 us
  transfers between devices with their start and end apart: 86 -> 85, of which waited for: 31 -> 35; matrix products, arithmetic and copies ran while one was open for 43% -> 15% of each run, Pallas kernels for 0% -> 25%
where the time goes in v1:
time: 688 us; the launch traced here: 683 us
  waiting for transfers between devices  261 us (38%)
  Pallas kernels  174 us (25%)
  starting transfers between devices  127 us (18%)
  local copies, waits for them, and re-layouts  78.3 us (11%)
  other arithmetic  40.9 us (6%)
    ppermute x39, waiting for transfers between devices, over_data(): return lax.ppermute(values, 'dp', route)  205 us
    pallas_call x14, Pallas kernels, launch(): pl.pallas_call(body, out_shape=tuple(outputs), in_specs=specs, out_specs=...  123 us
    ppermute x39, starting transfers between devices, over_data(): return lax.ppermute(values, 'dp', route)  63.3 us
    ppermute x12, starting transfers between devices, to_other_section(): return lax.ppermute(values, 'section', CORES)  55 us
    pallas_call x8, Pallas kernels, unpack(): pl.pallas_call(functools.partial(unpack_body, shapes, order), out_shape=t...  51.4 us
    ppermute x12, waiting for transfers between devices, to_other_section(): return lax.ppermute(values, 'section', CORES)  46.5 us
    unnamed x183, local copies, waits for them, and re-layouts  31.6 us
    select_n x9, other arithmetic, choose(): return jnp.where(front, first, second)  14.6 us
  transfers between devices with their start and end apart: 85, of which 35 were waited for; matrix products, arithmetic and copies ran while one was open for 15% of the time, Pallas kernels for 25%

profile of v1, /device:TPU:0, one launch (start us, length us, event | category | flops | bytes accessed | tf_op | source)
XLA Modules:
  0.0 683.3 jit_solution(8236919058894883814)
XLA Ops:
  21.5 12.7 %cross_forward.1 = (bf16[384,1536]{1,0:T(8,128)(2,1)}, bf16[448,1536]{1,0:T(8,128)(2,1)}, bf16[384,512]{1,0:T(8,128)(2,1)}, bf16[448,512]{1,0:T(8,128)(2,1)}) custom-call(bf16[384,768]{1,0:T(8,128)(2,1)} %bitcast.80, bf16[448,1024]{1,0:T(8,128)(2,1)} %bitcast.79, bf16[768,1536]{1,0:T(8,128)(2,1)} %copy.52.wt, bf16[1024,1536]{1,0:T(8,128)(2,1)} %copy.53.wi.w0, ...), custom_call_target="tpu_custom_call" | custom-call | flops 2315255808 | bytes 10422016 | tf_op jit(solution)/shard_map/cross_forward/pallas_call | solution.py:166
  60.2 7.4 %tail_i.1 = (bf16[224,1024]{1,0:T(8,128)(2,1)}, bf16[224,1024]{1,0:T(8,128)(2,1)}, bf16[224,512]{1,0:T(8,128)(2,1)}, bf16[224,512]{1,0:T(8,128)(2,1)}, f32[224,5...) custom-call(bf16[224,1024]{1,0:T(8,128)(2,1)} %bitcast.72, ...), custom_call_target="tpu_custom_call" | custom-call | flops 1409286144 | bytes 11583488 | tf_op jit(solution)/shard_map/tail_i/pallas_call | solution.py:166
  70.3 10.5 %tail_t.1 = (bf16[192,768]{1,0:T(8,128)(2,1)}, bf16[192,768]{1,0:T(8,128)(2,1)}, bf16[192,1536]{1,0:T(8,128)(2,1)}, bf16[192,1536]{1,0:T(8,128)(2,1)}, f32[192,1...) custom-call(bf16[192,768]{1,0:T(8,128)(2,1)} %bitcast.74, ...), custom_call_target="tpu_custom_call" | custom-call | flops 2113929216 | bytes 17215488 | tf_op jit(solution)/shard_map/tail_t/pallas_call | solution.py:166
  81.7 8.5 %collective-permute-done.4.x = bf16[192,768]{1,0:T(8,128)(2,1)} collective-permute-done((bf16[192,768]{1,0:T(8,128)(2,1)}, bf16[192,768]{1,0:T(8,128)(2,1)}, u32[]{:S(2)}, u32[]{:S(2)}) %collective-permute-start.4) | collective-permute-done | bytes 294944 | tf_op jit(solution)/shard_map/ppermute | solution.py:525
  90.2 15.7 %self_t.1 = (bf16[192,768]{1,0:T(8,128)(2,1)}, bf16[192,768]{1,0:T(8,128)(2,1)}, bf16[192,512]{1,0:T(8,128)(2,1)}, bf16[192,512]{1,0:T(8,128)(2,1)}, bf16[192,15...) custom-call(s32[1]{0:T(128)} %bitcast.front, ...), custom_call_target="tpu_custom_call" | custom-call | flops 5435817984 | bytes 21848064 | tf_op jit(solution)/shard_map/self_t/pallas_call | solution.py:166
  105.9 28.9 %collective-permute-start.7 = (bf16[192,768]{1,0:T(8,128)(2,1)}, bf16[192,768]{1,0:T(8,128)(2,1)}, u32[]{:S(2)}, u32[]{:S(2)}) collective-permute-start(bf16[192,768]{1,0:T(8,128)(2,1)} %get-tuple-element.191), channel_id=1, source_target_pairs={{0,16},{16,0},{1,17},{17,1},{2,18},{18,2},{3,19},{19,3},{4,20},{20... | collective-permute-start | bytes 884744 | tf_op jit(solution)/shard_map/ppermute | solution.py:525
  134.8 7.6 %self_i.1 = (bf16[224,1024]{1,0:T(8,128)(2,1)}, bf16[224,1024]{1,0:T(8,128)(2,1)}, bf16[224,512]{1,0:T(8,128)(2,1)}, bf16[224,512]{1,0:T(8,128)(2,1)}, bf16[224,...) custom-call(s32[1]{0:T(128)} %bitcast.front, ...), custom_call_target="tpu_custom_call" | custom-call | flops 5637144576 | bytes 19728128 | tf_op jit(solution)/shard_map/self_i/pallas_call | solution.py:166
  142.5 18.7 %collective-permute-start.15 = (bf16[224,1024]{1,0:T(8,128)(2,1)}, bf16[224,1024]{1,0:T(8,128)(2,1)S(1)}, u32[]{:S(2)}, u32[]{:S(2)}) collective-permute-start(bf16[224,1024]{1,0:T(8,128)(2,1)} %get-tuple-element.214), channel_id=1, source_target_pairs={{0,16},{16,0},{1,17},{17,1},{2,18},{18,2},{3,19},{19,3},{4,20},{20... | collective-permute-start | bytes 1376264 | tf_op jit(solution)/shard_map/ppermute | solution.py:525
  162.8 12.1 %tail_back_t.1 = (bf16[192,768]{1,0:T(8,128)(2,1)}, bf16[192,1536]{1,0:T(8,128)(2,1)}, bf16[192,1536]{1,0:T(8,128)(2,1)}, bf16[192,768]{1,0:T(8,128)(2,1)}, f32[...) custom-call(s32[1]{0:T(128)} %bitcast.front, ...), custom_call_target="tpu_custom_call" | custom-call | flops 2113929216 | bytes 19593216 | tf_op jit(solution)/shard_map/tail_back_t/pallas_call | solution.py:166
  176.5 8.8 %tail_back_i.1 = (bf16[224,1024]{1,0:T(8,128)(2,1)}, bf16[224,512]{1,0:T(8,128)(2,1)}, bf16[224,512]{1,0:T(8,128)(2,1)}, bf16[224,1024]{1,0:T(8,128)(2,1)}, f32[...) custom-call(s32[1]{0:T(128)} %bitcast.front, ...), custom_call_target="tpu_custom_call" | custom-call | flops 1409286144 | bytes 13901824 | tf_op jit(solution)/shard_map/tail_back_i/pallas_call | solution.py:166
  213.3 20.9 %cross_backward.1 = (bf16[384,1536]{1,0:T(8,128)(2,1)}, bf16[448,1536]{1,0:T(8,128)(2,1)}, f32[384,768]{1,0:T(8,128)}, f32[448,1024]{1,0:T(8,128)}) custom-call(s32[1]{0:T(128)} %bitcast.front, bf16[384,1536]{1,0:T(8,128)(2,1)} %get-tuple-element.205.tp, bf16[448,1536]{1,0:T(8,128)(2,1)} %get-tuple-element.206.ip, bf16[384,512]{1,0:T(8,128)(2,1)} %pad_maximum_fusion.15.dct, ...), custom_call_target="tpu_custom_call" | custom-call | flops 2315255808 | bytes 17041152 | tf_op jit(solution)/shard_map/cross_backward/pallas_call | solution.py:166
  250.9 18.3 %collective-permute-done.39 = bf16[1792,256]{1,0:T(8,128)(2,1)S(1)} collective-permute-done((bf16[1792,256]{1,0:T(8,128)(2,1)}, bf16[1792,256]{1,0:T(8,128)(2,1)S(1)}, u32[]{:S(2)}, u32[]{:S(2)}) %collective-permute-start.39) | collective-permute-done | bytes 917536 | tf_op jit(solution)/shard_map/ppermute | solution.py:530
  273.4 7.3 %collective-permute-done.40 = bf16[896,256]{1,0:T(8,128)(2,1)S(1)} collective-permute-done((bf16[896,256]{1,0:T(8,128)(2,1)S(1)}, bf16[896,256]{1,0:T(8,128)(2,1)S(1)}, u32[]{:S(2)}, u32[]{:S(2)}) %collective-permute-start.40) | collective-permute-done | bytes 458784 | tf_op jit(solution)/shard_map/ppermute | solution.py:530
  285.9 9.0 %collective-permute-done.41 = bf16[576,256]{1,0:T(8,128)(2,1)S(1)} collective-permute-done((bf16[576,256]{1,0:T(8,128)(2,1)S(1)}, bf16[576,256]{1,0:T(8,128)(2,1)S(1)}, u32[]{:S(2)}, u32[]{:S(2)}) %collective-permute-start.41) | collective-permute-done | bytes 294944 | tf_op jit(solution)/shard_map/ppermute | solution.py:530
  309.7 6.7 collective-permute-done.42
  318.2 10.4 %collective-permute-done.45 = bf16[448,256]{1,0:T(8,128)(2,1)S(1)} collective-permute-done((bf16[448,256]{1,0:T(8,128)(2,1)S(1)}, bf16[448,256]{1,0:T(8,128)(2,1)S(1)}, u32[]{:S(2)}, u32[]{:S(2)}) %collective-permute-start.45) | collective-permute-done | bytes 229408 | tf_op jit(solution)/shard_map/ppermute | solution.py:530
  333.5 13.7 %collective-permute-done.50 = bf16[512,256]{1,0:T(8,128)(2,1)S(1)} collective-permute-done((bf16[512,256]{1,0:T(8,128)(2,1)S(1)}, bf16[512,256]{1,0:T(8,128)(2,1)S(1)}, u32[]{:S(2)}, u32[]{:S(2)}) %collective-permute-start.50) | collective-permute-done | bytes 262176 | tf_op jit(solution)/shard_map/ppermute | solution.py:530
  352.0 14.5 %collective-permute-done.52 = bf16[576,256]{1,0:T(8,128)(2,1)S(1)} collective-permute-done((bf16[576,256]{1,0:T(8,128)(2,1)S(1)}, bf16[576,256]{1,0:T(8,128)(2,1)S(1)}, u32[]{:S(2)}, u32[]{:S(2)}) %collective-permute-start.52) | collective-permute-done | bytes 294944 | tf_op jit(solution)/shard_map/ppermute | solution.py:530
  371.7 10.6 %collective-permute-done.54 = bf16[1152,256]{1,0:T(8,128)(2,1)} collective-permute-done((bf16[1152,256]{1,0:T(8,128)(2,1)S(1)}, bf16[1152,256]{1,0:T(8,128)(2,1)}, u32[]{:S(2)}, u32[]{:S(2)}) %collective-permute-start.54) | collective-permute-done | bytes 589856 | tf_op jit(solution)/shard_map/ppermute | solution.py:530
  392.1 17.3 %collective-permute-done.60 = bf16[1024,256]{1,0:T(8,128)(2,1)S(1)} collective-permute-done((bf16[1024,256]{1,0:T(8,128)(2,1)S(1)}, bf16[1024,256]{1,0:T(8,128)(2,1)S(1)}, u32[]{:S(2)}, u32[]{:S(2)}) %collective-permute-start.60) | collective-permute-done | bytes 524320 | tf_op jit(solution)/shard_map/ppermute | solution.py:530
  417.2 17.2 %collective-permute-done.69.far = bf16[2048,256]{1,0:T(8,128)(2,1)S(1)} collective-permute-done((bf16[2048,256]{1,0:T(8,128)(2,1)S(1)}, bf16[2048,256]{1,0:T(8,128)(2,1)S(1)}, u32[]{:S(2)}, u32[]{:S(2)}) %collective-permute-start.69) | collective-permute-done | bytes 1048608 | tf_op jit(solution)/shard_map/ppermute | solution.py:530
  456.7 14.3 %collective-permute-done.71 = bf16[576,256]{1,0:T(8,128)(2,1)S(1)} collective-permute-done((bf16[576,256]{1,0:T(8,128)(2,1)S(1)}, bf16[576,256]{1,0:T(8,128)(2,1)S(1)}, u32[]{:S(2)}, u32[]{:S(2)}) %collective-permute-start.71) | collective-permute-done | bytes 294944 | tf_op jit(solution)/shard_map/ppermute | solution.py:530
  476.0 13.2 %collective-permute-done.73 = bf16[576,256]{1,0:T(8,128)(2,1)S(1)} collective-permute-done((bf16[576,256]{1,0:T(8,128)(2,1)S(1)}, bf16[576,256]{1,0:T(8,128)(2,1)S(1)}, u32[]{:S(2)}, u32[]{:S(2)}) %collective-permute-start.73) | collective-permute-done | bytes 294944 | tf_op jit(solution)/shard_map/ppermute | solution.py:530
  493.4 7.0 %collective-permute-done.75.far = bf16[2304,256]{1,0:T(8,128)(2,1)S(1)} collective-permute-done((bf16[2304,256]{1,0:T(8,128)(2,1)S(1)}, bf16[2304,256]{1,0:T(8,128)(2,1)S(1)}, u32[]{:S(2)}, u32[]{:S(2)}) %collective-permute-start.75) | collective-permute-done | bytes 1179680 | tf_op jit(solution)/shard_map/ppermute | solution.py:530
  500.4 7.8 %collective-permute-done.74 = bf16[768,256]{1,0:T(8,128)(2,1)S(1)} collective-permute-done((bf16[768,256]{1,0:T(8,128)(2,1)S(1)}, bf16[768,256]{1,0:T(8,128)(2,1)S(1)}, u32[]{:S(2)}, u32[]{:S(2)}) %collective-permute-start.74) | collective-permute-done | bytes 393248 | tf_op jit(solution)/shard_map/ppermute | solution.py:530
  518.1 14.0 %collective-permute-done.77 = bf16[768,256]{1,0:T(8,128)(2,1)S(1)} collective-permute-done((bf16[768,256]{1,0:T(8,128)(2,1)S(1)}, bf16[768,256]{1,0:T(8,128)(2,1)S(1)}, u32[]{:S(2)}, u32[]{:S(2)}) %collective-permute-start.77) | collective-permute-done | bytes 393248 | tf_op jit(solution)/shard_map/ppermute | solution.py:530
  536.6 8.9 %collective-permute-done.67 = bf16[896,256]{1,0:T(8,128)(2,1)S(1)} collective-permute-done((bf16[896,256]{1,0:T(8,128)(2,1)S(1)}, bf16[896,256]{1,0:T(8,128)(2,1)S(1)}, u32[]{:S(2)}, u32[]{:S(2)}) %collective-permute-start.67) | collective-permute-done | bytes 458784 | tf_op jit(solution)/shard_map/ppermute | solution.py:525
  554.5 28.4 %collective-permute-done.62 = bf16[576,256]{1,0:T(8,128)(2,1)} collective-permute-done((bf16[576,256]{1,0:T(8,128)(2,1)S(1)}, bf16[576,256]{1,0:T(8,128)(2,1)}, u32[]{:S(2)}, u32[]{:S(2)}) %collective-permute-start.62) | collective-permute-done | bytes 294944 | tf_op jit(solution)/shard_map/ppermute | solution.py:525
  612.6 7.0 %unpack.9 = f32[768,1536]{1,0:T(8,128)} custom-call(s32[1]{0:T(128)} %bitcast.28.me, bf16[2304,256]{1,0:T(8,128)(2,1)} %pad_maximum_fusion.2.near, bf16[2304,256]{1,0:T(8,128)(2,1)} %copy-done.22), custom_call_target="tpu_custom_call" | custom-call | bytes 7077888 | tf_op jit(solution)/shard_map/unpack/pallas_call | solution.py:505
  619.6 7.5 %broadcast_select_fusion = (f32[768,1536]{1,0:T(8,128)}, f32[768,1536]{1,0:T(8,128)}) fusion(f32[768,1536]{1,0:T(8,128)} %unpack.9, f32[768,1536]{1,0:T(8,128)S(1)} %copy-done, pred[]{:T(512)S(6)} %eq.5), kind=kLoop, calls=%fused_computation | loop fusion | flops 2359296 | bytes 18874368 | tf_op jit(solution)/shard_map/jit(_where)/select_n | solution.py:800
  663.0 6.9 %unpack.12 = f32[1024,1536]{1,0:T(8,128)} custom-call(s32[1]{0:T(128)} %bitcast.28.me, bf16[3072,256]{1,0:T(8,128)(2,1)} %pad_maximum_fusion.near, bf16[3072,256]{1,0:T(8,128)(2,1)} %collective-permute-done.80.far), custom_call_target="tpu_custom_call" | custom-call | bytes 9437184 | tf_op jit(solution)/shard_map/unpack/pallas_call | solution.py:505
  669.9 6.6 copy.68
  (427 shorter events, 282.9 us)
Async XLA Ops:
  0.6 39.4 %collective-permute-start.1 = (bf16[512,768]{1,0:T(8,128)(2,1)}, bf16[512,768]{1,0:T(8,128)(2,1)}, u32[]{:S(2)}, u32[]{:S(2)}) collective-permute-start(bf16[512,768]{1,0:T(8,128)(2,1)} %o0.3), channel_id=1, source_target_pairs={{0,1},{1,0},{2,3},{3,2},{4,5},{5,4},{6,7},{7,6},{8,9},{9,8},{10,11... | collective-permute-start | bytes 2359304 | tf_op jit(solution)/shard_map/ppermute | solution.py:521
  38.2 29.4 %collective-permute-start.2 = (bf16[768,1536]{1,0:T(8,128)(2,1)}, bf16[768,1536]{1,0:T(8,128)(2,1)}, u32[]{:S(2)}, u32[]{:S(2)}) collective-permute-start(bf16[768,1536]{1,0:T(8,128)(2,1)} %bitcast.15.u0.rest_4_), channel_id=1, source_target_pairs={{0,1},{1,0},{2,3},{3,2},{4,5},{5,4},{6,7},{7,6},{8,9},{9,8},{10,11... | collective-permute-start | bytes 7077896 | tf_op jit(solution)/shard_map/ppermute | solution.py:521
  38.3 32.1 %collective-permute-start.3 = (bf16[1536,768]{1,0:T(8,128)(2,1)}, bf16[1536,768]{1,0:T(8,128)(2,1)}, u32[]{:S(2)}, u32[]{:S(2)}) collective-permute-start(bf16[1536,768]{1,0:T(8,128)(2,1)} %bitcast.16.d0.rest_6_), channel_id=1, source_target_pairs={{0,1},{1,0},{2,3},{3,2},{4,5},{5,4},{6,7},{7,6},{8,9},{9,8},{10,11... | collective-permute-start | bytes 7077896 | tf_op jit(solution)/shard_map/ppermute | solution.py:521
  40.0 94.8 %collective-permute-start.14 = (bf16[1024,1536]{1,0:T(8,128)(2,1)S(1)}, bf16[1024,1536]{1,0:T(8,128)(2,1)}, u32[]{:S(2)}, u32[]{:S(2)}) collective-permute-start(bf16[1024,1536]{1,0:T(8,128)(2,1)S(1)} %copy-done.1), channel_id=1, source_target_pairs={{0,1},{1,0},{2,3},{3,2},{4,5},{5,4},{6,7},{7,6},{8,9},{9,8},{10,11... | collective-permute-start | bytes 9437192 | tf_op jit(solution)/shard_map/ppermute | solution.py:521
  52.5 29.2 %collective-permute-start.5 = (bf16[768,1152]{1,0:T(8,128)(2,1)}, bf16[768,1152]{1,0:T(8,128)(2,1)}, u32[]{:S(2)}, u32[]{:S(2)}) collective-permute-start(bf16[768,1152]{1,0:T(8,128)(2,1)} %copy.56.w0), channel_id=1, source_target_pairs={{0,1},{1,0},{2,3},{3,2},{4,5},{5,4},{6,7},{7,6},{8,9},{9,8},{10,11... | collective-permute-start | bytes 5308424 | tf_op jit(solution)/shard_map/ppermute | solution.py:521
  81.7 93.3 %collective-permute-start.55 = (bf16[224,1024]{1,0:T(8,128)(2,1)}, bf16[224,1024]{1,0:T(8,128)(2,1)}, u32[]{:S(2)}, u32[]{:S(2)}) collective-permute-start(bf16[224,1024]{1,0:T(8,128)(2,1)} %collective-permute-done.13.x), channel_id=1, source_target_pairs={{0,1},{1,0},{2,3},{3,2},{4,5},{5,4},{6,7},{7,6},{8,9},{9,8},{10,11... | collective-permute-start | bytes 1376264 | tf_op jit(solution)/shard_map/ppermute | solution.py:521
  105.9 56.8 %collective-permute-start.7 = (bf16[192,768]{1,0:T(8,128)(2,1)}, bf16[192,768]{1,0:T(8,128)(2,1)}, u32[]{:S(2)}, u32[]{:S(2)}) collective-permute-start(bf16[192,768]{1,0:T(8,128)(2,1)} %get-tuple-element.191), channel_id=1, source_target_pairs={{0,16},{16,0},{1,17},{17,1},{2,18},{18,2},{3,19},{19,3},{4,20},{20... | collective-permute-start | bytes 884744 | tf_op jit(solution)/shard_map/ppermute | solution.py:525
  142.5 33.0 %collective-permute-start.15 = (bf16[224,1024]{1,0:T(8,128)(2,1)}, bf16[224,1024]{1,0:T(8,128)(2,1)S(1)}, u32[]{:S(2)}, u32[]{:S(2)}) collective-permute-start(bf16[224,1024]{1,0:T(8,128)(2,1)} %get-tuple-element.214), channel_id=1, source_target_pairs={{0,16},{16,0},{1,17},{17,1},{2,18},{18,2},{3,19},{19,3},{4,20},{20... | collective-permute-start | bytes 1376264 | tf_op jit(solution)/shard_map/ppermute | solution.py:525
  162.2 23.7 %collective-permute-start.25 = (bf16[192,768]{1,0:T(8,128)(2,1)S(1)}, bf16[192,768]{1,0:T(8,128)(2,1)S(1)}, u32[]{:S(2)}, u32[]{:S(2)}) collective-permute-start(bf16[192,768]{1,0:T(8,128)(2,1)S(1)} %copy-done.76), channel_id=1, source_target_pairs={{0,1},{1,0},{2,3},{3,2},{4,5},{5,4},{6,7},{7,6},{8,9},{9,8},{10,11... | collective-permute-start | bytes 884744 | tf_op jit(solution)/shard_map/ppermute | solution.py:521
  195.2 45.3 %collective-permute-start.27 = (bf16[2304,256]{1,0:T(8,128)(2,1)}, bf16[2304,256]{1,0:T(8,128)(2,1)S(1)}, u32[]{:S(2)}, u32[]{:S(2)}) collective-permute-start(bf16[2304,256]{1,0:T(8,128)(2,1)} %get-tuple-element.245), channel_id=1, source_target_pairs={{0,2},{2,0},{4,6},{6,4},{8,10},{10,8},{12,14},{14,12},{1,3},{3,1},... | collective-permute-start | bytes 3538952 | tf_op jit(solution)/shard_map/ppermute | solution.py:530
  202.1 38.4 %collective-permute-start.32 = (bf16[2048,256]{1,0:T(8,128)(2,1)}, bf16[2048,256]{1,0:T(8,128)(2,1)S(1)}, u32[]{:S(2)}, u32[]{:S(2)}) collective-permute-start(bf16[2048,256]{1,0:T(8,128)(2,1)} %get-tuple-element.252), channel_id=1, source_target_pairs={{0,4},{2,6},{4,0},{6,2},{8,12},{10,14},{12,8},{14,10},{1,5},{3,7},... | collective-permute-start | bytes 3145736 | tf_op jit(solution)/shard_map/ppermute | solution.py:530
  210.1 24.1 %collective-permute-start.36 = (bf16[224,1024]{1,0:T(8,128)(2,1)S(1)}, bf16[224,1024]{1,0:T(8,128)(2,1)S(1)}, u32[]{:S(2)}, u32[]{:S(2)}) collective-permute-start(bf16[224,1024]{1,0:T(8,128)(2,1)S(1)} %copy-done.70), channel_id=1, source_target_pairs={{0,1},{1,0},{2,3},{3,2},{4,5},{5,4},{6,7},{7,6},{8,9},{9,8},{10,11... | collective-permute-start | bytes 1376264 | tf_op jit(solution)/shard_map/ppermute | solution.py:521
  212.5 116.2 %collective-permute-start.49 = (bf16[2304,256]{1,0:T(8,128)(2,1)}, bf16[2304,256]{1,0:T(8,128)(2,1)S(1)}, u32[]{:S(2)}, u32[]{:S(2)}) collective-permute-start(bf16[2304,256]{1,0:T(8,128)(2,1)} %get-tuple-element.292), channel_id=1, source_target_pairs={{0,2},{2,0},{4,6},{6,4},{8,10},{10,8},{12,14},{14,12},{1,3},{3,1},... | collective-permute-start | bytes 3538952 | tf_op jit(solution)/shard_map/ppermute | solution.py:530
  239.3 29.9 %collective-permute-start.39 = (bf16[1792,256]{1,0:T(8,128)(2,1)}, bf16[1792,256]{1,0:T(8,128)(2,1)S(1)}, u32[]{:S(2)}, u32[]{:S(2)}) collective-permute-start(bf16[1792,256]{1,0:T(8,128)(2,1)} %get-tuple-element.264), channel_id=1, source_target_pairs={{0,2},{2,0},{4,6},{6,4},{8,10},{10,8},{12,14},{14,12},{1,3},{3,1},... | collective-permute-start | bytes 2752520 | tf_op jit(solution)/shard_map/ppermute | solution.py:530
  240.6 28.7 %collective-permute-start.33 = (bf16[1152,256]{1,0:T(8,128)(2,1)S(1)}, bf16[1152,256]{1,0:T(8,128)(2,1)}, u32[]{:S(2)}, u32[]{:S(2)}) collective-permute-start(bf16[1152,256]{1,0:T(8,128)(2,1)S(1)} %slice_add_fusion.3), channel_id=1, source_target_pairs={{0,4},{2,6},{4,0},{6,2},{8,12},{10,14},{12,8},{14,10},{1,5},{3,7},... | collective-permute-start | bytes 1769480 | tf_op jit(solution)/shard_map/ppermute | solution.py:530
  242.0 27.3 %collective-permute-start.34 = (bf16[1024,256]{1,0:T(8,128)(2,1)}, bf16[1024,256]{1,0:T(8,128)(2,1)}, u32[]{:S(2)}, u32[]{:S(2)}) collective-permute-start(bf16[1024,256]{1,0:T(8,128)(2,1)} %slice_add_fusion.4), channel_id=1, source_target_pairs={{0,8},{2,10},{4,12},{6,14},{8,0},{10,2},{12,4},{14,6},{1,9},{3,11}... | collective-permute-start | bytes 1572872 | tf_op jit(solution)/shard_map/ppermute | solution.py:530
  250.1 44.9 %collective-permute-start.24 = (bf16[2304,256]{1,0:T(8,128)(2,1)}, bf16[2304,256]{1,0:T(8,128)(2,1)S(1)}, u32[]{:S(2)}, u32[]{:S(2)}) collective-permute-start(bf16[2304,256]{1,0:T(8,128)(2,1)} %get-tuple-element.240), channel_id=1, source_target_pairs={{0,2},{2,0},{4,6},{6,4},{8,10},{10,8},{12,14},{14,12},{1,3},{3,1},... | collective-permute-start | bytes 3538952 | tf_op jit(solution)/shard_map/ppermute | solution.py:530
  305.9 64.7 %collective-permute-start.56 = (bf16[3072,256]{1,0:T(8,128)(2,1)}, bf16[3072,256]{1,0:T(8,128)(2,1)S(1)}, u32[]{:S(2)}, u32[]{:S(2)}) collective-permute-start(bf16[3072,256]{1,0:T(8,128)(2,1)} %get-tuple-element.306), channel_id=1, source_target_pairs={{0,2},{2,0},{4,6},{6,4},{8,10},{10,8},{12,14},{14,12},{1,3},{3,1},... | collective-permute-start | bytes 4718600 | tf_op jit(solution)/shard_map/ppermute | solution.py:530
  382.3 28.1 %collective-permute-start.59 = (bf16[1536,256]{1,0:T(8,128)(2,1)S(1)}, bf16[1536,256]{1,0:T(8,128)(2,1)S(1)}, u32[]{:S(2)}, u32[]{:S(2)}) collective-permute-start(bf16[1536,256]{1,0:T(8,128)(2,1)S(1)} %slice_add_fusion), channel_id=1, source_target_pairs={{0,4},{2,6},{4,0},{6,2},{8,12},{10,14},{12,8},{14,10},{1,5},{3,7},... | collective-permute-start | bytes 2359304 | tf_op jit(solution)/shard_map/ppermute | solution.py:530
  384.1 25.4 %collective-permute-start.60 = (bf16[1024,256]{1,0:T(8,128)(2,1)S(1)}, bf16[1024,256]{1,0:T(8,128)(2,1)S(1)}, u32[]{:S(2)}, u32[]{:S(2)}) collective-permute-start(bf16[1024,256]{1,0:T(8,128)(2,1)S(1)} %pad_maximum_fusion.12), channel_id=1, source_target_pairs={{0,8},{2,10},{4,12},{6,14},{8,0},{10,2},{12,4},{14,6},{1,9},{3,11}... | collective-permute-start | bytes 1572872 | tf_op jit(solution)/shard_map/ppermute | solution.py:530
  391.2 26.0 %collective-permute-start.58 = (bf16[2304,256]{1,0:T(8,128)(2,1)S(1)}, bf16[2304,256]{1,0:T(8,128)(2,1)S(1)}, u32[]{:S(2)}, u32[]{:S(2)}) collective-permute-start(bf16[2304,256]{1,0:T(8,128)(2,1)S(1)} %pad_maximum_fusion.1.near), channel_id=1, source_target_pairs={{0,2},{2,0},{4,6},{6,4},{8,10},{10,8},{12,14},{14,12},{1,3},{3,1},... | collective-permute-start | bytes 3538952 | tf_op jit(solution)/shard_map/ppermute | solution.py:530
  410.4 24.0 %collective-permute-start.69 = (bf16[2048,256]{1,0:T(8,128)(2,1)S(1)}, bf16[2048,256]{1,0:T(8,128)(2,1)S(1)}, u32[]{:S(2)}, u32[]{:S(2)}) collective-permute-start(bf16[2048,256]{1,0:T(8,128)(2,1)S(1)} %pad_maximum_fusion.5.near), channel_id=1, source_target_pairs={{0,4},{2,6},{4,0},{6,2},{8,12},{10,14},{12,8},{14,10},{1,5},{3,7},... | collective-permute-start | bytes 3145736 | tf_op jit(solution)/shard_map/ppermute | solution.py:530
  455.6 36.9 %collective-permute-start.21 = (f32[224,1024]{1,0:T(8,128)S(1)}, f32[224,1024]{1,0:T(8,128)S(1)}, u32[]{:S(2)}, u32[]{:S(2)}) collective-permute-start(f32[224,1024]{1,0:T(8,128)S(1)} %slice.228), channel_id=1, source_target_pairs={{0,1},{1,0},{2,3},{3,2},{4,5},{5,4},{6,7},{7,6},{8,9},{9,8},{10,11... | collective-permute-start | bytes 2752520 | tf_op jit(solution)/shard_map/ppermute | solution.py:521
  472.8 27.6 %collective-permute-start.75 = (bf16[2304,256]{1,0:T(8,128)(2,1)S(1)}, bf16[2304,256]{1,0:T(8,128)(2,1)S(1)}, u32[]{:S(2)}, u32[]{:S(2)}) collective-permute-start(bf16[2304,256]{1,0:T(8,128)(2,1)S(1)} %pad_maximum_fusion.3.near), channel_id=1, source_target_pairs={{0,2},{2,0},{4,6},{6,4},{8,10},{10,8},{12,14},{14,12},{1,3},{3,1},... | collective-permute-start | bytes 3538952 | tf_op jit(solution)/shard_map/ppermute | solution.py:530
  493.3 38.8 %collective-permute-start.22 = (bf16[2,100,1024]{2,0,1:T(2,128)(2,1)S(1)}, bf16[2,100,1024]{2,0,1:T(2,128)(2,1)S(1)}, u32[]{:S(2)}, u32[]{:S(2)}) collective-permute-start(bf16[2,100,1024]{2,0,1:T(2,128)(2,1)S(1)} %copy.73), channel_id=1, source_target_pairs={{0,1},{1,0},{2,3},{3,2},{4,5},{5,4},{6,7},{7,6},{8,9},{9,8},{10,11... | collective-permute-start | bytes 1228808 | tf_op jit(solution)/shard_map/ppermute | solution.py:521
  532.1 60.3 %collective-permute-start.79 = (bf16[2304,256]{1,0:T(8,128)(2,1)S(1)}, bf16[2304,256]{1,0:T(8,128)(2,1)S(1)}, u32[]{:S(2)}, u32[]{:S(2)}) collective-permute-start(bf16[2304,256]{1,0:T(8,128)(2,1)S(1)} %pad_maximum_fusion.4.near), channel_id=1, source_target_pairs={{0,2},{2,0},{4,6},{6,4},{8,10},{10,8},{12,14},{14,12},{1,3},{3,1},... | collective-permute-start | bytes 3538952 | tf_op jit(solution)/shard_map/ppermute | solution.py:530
  533.5 49.7 %collective-permute-start.63 = (bf16[1152,256]{1,0:T(8,128)(2,1)}, bf16[1152,256]{1,0:T(8,128)(2,1)S(1)}, u32[]{:S(2)}, u32[]{:S(2)}) collective-permute-start(bf16[1152,256]{1,0:T(8,128)(2,1)} %collective-permute-done.54), channel_id=1, source_target_pairs={{0,16},{16,0},{1,17},{17,1},{2,18},{18,2},{3,19},{19,3},{4,20},{20... | collective-permute-start | bytes 1769480 | tf_op jit(solution)/shard_map/ppermute | solution.py:525
  535.6 49.7 %collective-permute-start.68 = (bf16[1792,256]{1,0:T(8,128)(2,1)}, bf16[1792,256]{1,0:T(8,128)(2,1)S(1)}, u32[]{:S(2)}, u32[]{:S(2)}) collective-permute-start(bf16[1792,256]{1,0:T(8,128)(2,1)} %collective-permute-done.57.far), channel_id=1, source_target_pairs={{0,16},{16,0},{1,17},{17,1},{2,18},{18,2},{3,19},{19,3},{4,20},{20... | collective-permute-start | bytes 2752520 | tf_op jit(solution)/shard_map/ppermute | solution.py:525
  535.7 56.8 %collective-permute-start.78 = (bf16[1536,256]{1,0:T(8,128)(2,1)S(1)}, bf16[1536,256]{1,0:T(8,128)(2,1)}, u32[]{:S(2)}, u32[]{:S(2)}) collective-permute-start(bf16[1536,256]{1,0:T(8,128)(2,1)S(1)} %pad_maximum_fusion.8), channel_id=1, source_target_pairs={{0,4},{2,6},{4,0},{6,2},{8,12},{10,14},{12,8},{14,10},{1,5},{3,7},... | collective-permute-start | bytes 2359304 | tf_op jit(solution)/shard_map/ppermute | solution.py:530
  545.5 37.3 %collective-permute-start.62 = (bf16[576,256]{1,0:T(8,128)(2,1)S(1)}, bf16[576,256]{1,0:T(8,128)(2,1)}, u32[]{:S(2)}, u32[]{:S(2)}) collective-permute-start(bf16[576,256]{1,0:T(8,128)(2,1)S(1)} %collective-permute-done.52), channel_id=1, source_target_pairs={{0,16},{16,0},{1,17},{17,1},{2,18},{18,2},{3,19},{19,3},{4,20},{20... | collective-permute-start | bytes 884744 | tf_op jit(solution)/shard_map/ppermute | solution.py:525
  582.9 28.7 %collective-permute-start.64 = (bf16[2304,256]{1,0:T(8,128)(2,1)S(1)}, bf16[2304,256]{1,0:T(8,128)(2,1)S(1)}, u32[]{:S(2)}, u32[]{:S(2)}) collective-permute-start(bf16[2304,256]{1,0:T(8,128)(2,1)S(1)} %collective-permute-done.58.far), channel_id=1, source_target_pairs={{0,16},{16,0},{1,17},{17,1},{2,18},{18,2},{3,19},{19,3},{4,20},{20... | collective-permute-start | bytes 3538952 | tf_op jit(solution)/shard_map/ppermute | solution.py:525
  595.4 67.7 %collective-permute-start.80 = (bf16[3072,256]{1,0:T(8,128)(2,1)}, bf16[3072,256]{1,0:T(8,128)(2,1)}, u32[]{:S(2)}, u32[]{:S(2)}) collective-permute-start(bf16[3072,256]{1,0:T(8,128)(2,1)} %pad_maximum_fusion.near), channel_id=1, source_target_pairs={{0,2},{2,0},{4,6},{6,4},{8,10},{10,8},{12,14},{14,12},{1,3},{3,1},... | collective-permute-start | bytes 4718600 | tf_op jit(solution)/shard_map/ppermute | solution.py:530
  (138 other events, 1933.5 us)

commit v2 on v0

v2 whole, which is shorter than its diff:
```python
import functools
import math

import jax
import jax.numpy as jnp
from jax import lax
from jax.experimental import pallas as pl
from jax.experimental.pallas import tpu as pltpu
from jax.sharding import PartitionSpec as P

D_TEXT = 768
HEADS_TEXT = 12
D_IMAGE = 1024
HEADS_IMAGE = 8
D_CO = 1024
HEADS_CO = 8

LOW = jnp.bfloat16
FULL = jnp.float32
TILE = 512
UNIT = 256
ROOM = 56 * 1024 * 1024


def times(left, right):
    return jnp.dot(left, right, preferred_element_type=FULL)


def times_back(left, right):
    return lax.dot_general(left, right, (((1,), (1,)), ((), ())), preferred_element_type=FULL)


def back_times(left, right):
    return lax.dot_general(left, right, (((0,), (0,)), ((), ())), preferred_element_type=FULL)


def norm_rows(rows):
    centre = rows - jnp.mean(rows, axis=-1, keepdims=True)
    spread = jnp.mean(centre * centre, axis=-1, keepdims=True)
    inverse = lax.rsqrt(spread + 1e-05)
    return centre * inverse, inverse


def norm_back(unit, inverse, gain, grad):
    scaled = grad * gain
    first = jnp.mean(scaled, axis=-1, keepdims=True)
    second = jnp.mean(scaled * unit, axis=-1, keepdims=True)
    dgain = jnp.sum(grad * unit, axis=0, keepdims=True)
    dshift = jnp.sum(grad, axis=0, keepdims=True)
    return inverse * (scaled - first - unit * second), dgain, dshift


def gelu_both(inputs):
    rate = 0.7978845608028654
    square = inputs * inputs
    bent = jnp.tanh(rate * inputs * (1.0 + 0.044715 * square))
    half = 0.5 * (1.0 + bent)
    slope = half + 0.5 * inputs * (1.0 - bent * bent) * rate * (1.0 + 0.134145 * square)
    return inputs * half, slope


def heads_of(query, size):
    if size == query.shape[1]:
        return [query]
    lower = lax.broadcasted_iota(jnp.int32, (1, query.shape[1]), 1) < size
    low = lower.astype(FULL).astype(LOW)
    return [query * low, query * (1 - low)]


def merged(parts, size):
    if len(parts) == 1:
        return parts[0]
    return jnp.where(lax.broadcasted_iota(jnp.int32, parts[0].shape, 1) < size, parts[0], parts[1])


def softmax_all(pairs, alloweds, size):
    scores = [times_back(query, keys) for query, keys in pairs]
    scores = [
        jnp.where(allowed, score * (1.0 / math.sqrt(size)), -1000000000.0)
        for score, allowed in zip(scores, alloweds)
    ]
    tops = [jnp.max(score, axis=-1, keepdims=True) for score in scores]
    raised = [jnp.exp(score - top) for score, top in zip(scores, tops)]
    shares = [1.0 / jnp.sum(value, axis=-1, keepdims=True) for value in raised]
    return [value * share for value, share in zip(raised, shares)]


def attend_all(units, size):
    singles = [(q, k, v, a) for query, k, v, a in units for q in heads_of(query, size)]
    weights = softmax_all([one[:2] for one in singles], [one[3] for one in singles], size)
    contexts = [times(w.astype(LOW), one[2]) for w, one in zip(weights, singles)]
    heads = len(singles) // len(units)
    return [merged(contexts[n * heads : (n + 1) * heads], size).astype(LOW) for n in range(len(units))]


def attend_back_all(units, size):
    scaling = 1.0 / math.sqrt(size)
    singles = [
        (q, k, v, a, d, query, dcontext)
        for query, k, v, a, dcontext in units
        for q, d in zip(heads_of(query, size), heads_of(dcontext, size))
    ]
    weights = softmax_all([one[:2] for one in singles], [one[3] for one in singles], size)
    dweights = [times_back(one[4], one[2]) for one in singles]
    dvalues = [back_times(w.astype(LOW), one[6]) for w, one in zip(weights, singles)]
    sums = [jnp.sum(dw * w, axis=-1, keepdims=True) for dw, w in zip(dweights, weights)]
    dscores = [(w * (dw - s)).astype(LOW) for w, dw, s in zip(weights, dweights, sums)]
    dqueries = [times(ds, one[1]) * scaling for ds, one in zip(dscores, singles)]
    dkeys = [back_times(ds, one[5]) * scaling for ds, one in zip(dscores, singles)]
    heads = len(singles) // len(units)
    return [
        [merged(grads[n * heads : (n + 1) * heads], size).astype(LOW) for grads in (dqueries, dkeys, dvalues)]
        for n in range(len(units))
    ]


def wide(column):
    return jnp.broadcast_to(column, (column.shape[0], 128))


class Late:
    def __init__(self, source, target, signal):
        self.target = target
        self.copy = pltpu.make_async_copy(source, target, signal)
        self.copy.start()
        self.here = False

    def get(self):
        if not self.here:
            self.copy.wait()
            self.here = True
        return self.target


class Here:
    def __init__(self, target):
        self.target = target

    def get(self):
        return self.target


def fetch(sources, targets, signals):
    return [Late(s, t, signals.at[n]) for n, (s, t) in enumerate(zip(sources, targets))]


def pass_through(sources, targets, signals):
    copies = [
        pltpu.make_async_copy(s, t, signals.at[n]) for n, (s, t) in enumerate(zip(sources, targets))
    ]
    for copy in copies:
        copy.start()
    for copy in copies:
        copy.wait()


def tail_forward(residual, contexts, out_w, gain, shift, up_w, down_w, kept, mixed):
    normed_ref, hidden, slopes, unit1, inv1, unit2, inv2 = kept
    branch = times(contexts[0], out_w[0].get()[...]) + times(contexts[1], out_w[1].get()[...])
    unit, inverse = norm_rows(residual.astype(FULL) + branch)
    unit1[...] = unit
    inv1[...] = wide(inverse)
    normed = unit * gain[0:1, :] + shift[0:1, :]
    normed_ref[...] = normed.astype(LOW)
    mixed[...] = normed
    for half in range(2):
        up, down = up_w[half].get(), down_w[half].get()
        for start in range(0, up.shape[1], TILE):
            span = pl.ds(start, TILE)
            value, slope = gelu_both(times(normed_ref[...], up[:, span]))
            hidden[half][:, span] = value.astype(LOW)
            slopes[half][:, span] = slope
            mixed[...] += times(hidden[half][:, span], down[span, :])
    unit, inverse = norm_rows(mixed[...])
    unit2[...] = unit
    inv2[...] = wide(inverse)
    return unit * gain[1:2, :] + shift[1:2, :]


def tail_backward(seed, kept, out_w, gain, up_w, down_w, grads, total):
    slopes, unit1, inv1, unit2, inv2 = kept
    df, du, da, dgain, dshift = grads
    dsecond, dgain1, dshift1 = norm_back(
        unit2.get()[...], inv2.get()[:, 0:1], gain[1:2, :], seed
    )
    total[...] = dsecond
    df[...] = dsecond.astype(LOW)
    for half in range(2):
        up, down, slope = up_w[half].get(), down_w[half].get(), slopes[half].get()
        for start in range(0, up.shape[1], TILE):
            span = pl.ds(start, TILE)
            dhidden = times_back(df[...], down[span, :])
            du[half][:, span] = (dhidden * slope[:, span]).astype(LOW)
            total[...] += times_back(du[half][:, span], up[:, span])
    dfirst, dgain0, dshift0 = norm_back(
        unit1.get()[...], inv1.get()[:, 0:1], gain[0:1, :], total[...]
    )
    dgain[...] = jnp.concatenate([dgain0, dgain1], axis=0)
    dshift[...] = jnp.concatenate([dshift0, dshift1], axis=0)
    total[...] = dfirst
    da[...] = dfirst.astype(LOW)
    return [times_back(da[...], w.get()[...]).astype(LOW) for w in out_w]


def shape_of(rows, columns, kind=LOW):
    return jax.ShapeDtypeStruct((rows, columns), kind)


def launch(body, outputs, args, far=(), scratch=(), flag=None, work=0, name=None):
    whole = pl.BlockSpec(memory_space=pltpu.VMEM)
    moved = sum(
        math.prod(v.shape) * v.dtype.itemsize for v in tuple(args) + tuple(far) + tuple(outputs)
    )
    specs = [pl.BlockSpec(memory_space=pltpu.SMEM)] + [whole] * len(args)
    specs += [pl.BlockSpec(memory_space=pl.ANY)] * len(far)
    return pl.pallas_call(
        body,
        out_shape=tuple(outputs),
        in_specs=specs,
        out_specs=tuple([whole] * len(outputs)),
        scratch_shapes=list(scratch),
        compiler_params=pltpu.CompilerParams(vmem_limit_bytes=ROOM),
        cost_estimate=pl.CostEstimate(flops=work, bytes_accessed=moved, transcendentals=0),
        name=name,
    )(flag, *args, *far)


def buffers_for(far):
    return [pltpu.VMEM(v.shape, v.dtype) for v in far] + [pltpu.SemaphoreType.DMA((len(far),))]


def rows_at(pair, rows):
    return pl.ds(pl.multiple_of(pair * rows, 16), rows)


def slab(index):
    return pl.ds(index * 128, 128)


def cross_forward(
    pairs, rows_t, rows_i, real_t, info, x_t, x_i, keep, far_t, far_i,
    xt_own, xt_other, xi_own, xi_other, tp, ip, ct_own, ct_other, ci_own, ci_other, xt, xi, wt, wi, signals,
):
    half = pairs // 2
    for place in range(pairs):
        pair = lax.rem(place + half * info[1], pairs)
        text, image = x_t[rows_at(pair, rows_t), :], x_i[rows_at(pair, rows_i), :]
        xt[place * rows_t : (place + 1) * rows_t, :] = text
        xi[place * rows_i : (place + 1) * rows_i, :] = image
        inside = place % half
        (xt_own, xt_other)[place // half][inside * rows_t : (inside + 1) * rows_t, :] = text
        (xi_own, xi_other)[place // half][inside * rows_i : (inside + 1) * rows_i, :] = image

    @pl.when(info[0] == 1)
    def work():
        width = ct_own.shape[1]
        weights = fetch((far_t, far_i), (wt, wi), signals)
        for late, x, p in ((weights[0], xt, tp), (weights[1], xi, ip)):
            for slot in range(3):
                p[:, pl.ds(slot * width, width)] = times(x[...], late.get()[slot]).astype(LOW)
        text_keys = lax.broadcasted_iota(jnp.int32, (1, rows_t), 1) < real_t
        slabs = width // 128

        def each(pair, carry):
            at_t, at_i = rows_at(pair, rows_t), rows_at(pair, rows_i)
            for group, ct, ci in ((0, ct_own, ci_own), (half, ct_other, ci_other)):
                from_t, from_i = rows_at(pair + group, rows_t), rows_at(pair + group, rows_i)
                kept = keep[lax.rem(pair + group + half * info[1], pairs)] > 0
                texts, images = [], []
                for n in range(slabs):
                    first, second, third = slab(n), slab(slabs + n), slab(2 * slabs + n)
                    texts.append((tp[from_t, first], ip[from_i, second], ip[from_i, third], kept))
                    images.append((ip[from_i, first], tp[from_t, second], tp[from_t, third], text_keys))
                results = zip(attend_all(texts, 128), attend_all(images, 128))
                for n, (text, image) in enumerate(results):
                    ct[at_t, slab(n)] = text
                    ci[at_i, slab(n)] = image
            return carry

        lax.fori_loop(0, half, each, 0)


def first_tail(
    info, x, c0, c1, gain, shift, *refs
):
    far, refs = refs[:6], refs[6:]
    out, y, h0, h1, s0, s1, n1, i1, n2, i2, mixed = refs[:11]
    near, signals = refs[11:17], refs[17]

    @pl.when(info[0] == 1)
    def work():
        o0, o1, u0, d0, u1, d1 = fetch(far, near, signals)
        kept = (y, (h0, h1), (s0, s1), n1, i1, n2, i2)
        out[...] = tail_forward(
            x[...], (c0[...], c1[...]), (o0, o1), gain, shift, (u0, u1), (d0, d1), kept, mixed
        ).astype(LOW)


def self_layer(
    masked, half, rows, real, size, stride, info, x, seed, gain, shift, keep, *refs
):
    far, refs = refs[:12], refs[12:]
    (out, dx, c0, p0, da, df, du0, du1, y, h0, dgain, dshift, give) = refs[:13]
    (q0, q1, s0, s1, n1, i1, n2, i2, mixed, dc0, dc1, h1, c1, p1) = refs[13:27]
    near, signals = refs[27:35], refs[35]
    width = q0.shape[1] // 3
    wide_x, wide_h, wide_c = x.shape[1], h1.shape[1], c1.shape[1]
    spans = []
    for columns in (wide_x, wide_h, wide_c, p1.shape[1], wide_x):
        spans.append(pl.ds(sum(span.size for span in spans), columns))

    @pl.when(info[0] == 1)
    def pass_on():
        targets = (y, h0, c0, give.at[:, spans[0]], give.at[:, spans[1]])
        pass_through((far[8], far[9], far[11], far[8], far[10]), targets, signals)

    @pl.when(info[0] == 0)
    def work():
        w0, w1, o0, o1, u0, d0, u1, d1 = fetch(far[:8], near, signals)
        slabs = width // 128
        if c0.shape[1] != width:
            rest = pl.ds(width, c0.shape[1] - width)
            c0[:, rest] = jnp.zeros((c0.shape[0], c0.shape[1] - width), LOW)
            c1[:, rest] = jnp.zeros((c0.shape[0], c0.shape[1] - width), LOW)
            for slot in range(3):
                rest = pl.ds(slot * stride + width, stride - width)
                p0[:, rest] = jnp.zeros((p0.shape[0], stride - width), LOW)
                p1[:, rest] = jnp.zeros((p0.shape[0], stride - width), LOW)
        for w, q in ((w0, q0), (w1, q1)):
            for slot in range(3):
                q[:, pl.ds(slot * width, width)] = times(x[...], w.get()[slot]).astype(LOW)

        def allowed(pair):
            if not masked:
                return lax.broadcasted_iota(jnp.int32, (1, rows), 1) < real
            return keep[pair + half * info[1]] > 0

        def forward(pair, carry):
            at = rows_at(pair, rows)
            kept = allowed(pair)
            units = [
                (q[at, slab(n)], q[at, slab(slabs + n)], q[at, slab(2 * slabs + n)], kept)
                for q in (q0, q1)
                for n in range(slabs)
            ]
            results = attend_all(units, size)
            for n, value in enumerate(results):
                (c0, c1)[n // slabs][at, slab(n % slabs)] = value
            return carry

        lax.fori_loop(0, half, forward, 0)
        used = pl.ds(0, width)
        kept = (y, (h0, h1), (s0, s1), n1, i1, n2, i2)
        out[...] = tail_forward(
            x[...], (c0[:, used], c1[:, used]), (o0, o1), gain, shift, (u0, u1), (d0, d1), kept, mixed
        ).astype(LOW)
        held = ((Here(s0), Here(s1)), Here(n1), Here(i1), Here(n2), Here(i2))
        dcs = tail_backward(
            seed[...].astype(FULL),
            held,
            (o0, o1),
            gain,
            (u0, u1),
            (d0, d1),
            (df, (du0, du1), da, dgain, dshift),
            mixed,
        )
        dc0[...] = dcs[0]
        dc1[...] = dcs[1]

        def backward(pair, carry):
            at = rows_at(pair, rows)
            kept = allowed(pair)
            units = [
                (q[at, slab(n)], q[at, slab(slabs + n)], q[at, slab(2 * slabs + n)], kept, dc[at, slab(n)])
                for q, dc in ((q0, dc0), (q1, dc1))
                for n in range(slabs)
            ]
            results = attend_back_all(units, size)
            for n, grads in enumerate(results):
                for slot in range(3):
                    column = slot * stride + (n % slabs) * 128
                    (p0, p1)[n // slabs][at, pl.ds(column, 128)] = grads[slot]
            return carry

        lax.fori_loop(0, half, backward, 0)
        for w, p in ((w0, p0), (w1, p1)):
            for slot in range(3):
                mixed[...] += times_back(p[:, pl.ds(slot * stride, width)], w.get()[slot])
        dx[...] = mixed[...].astype(LOW)
        for span, value in zip(spans, (y, h1, c1, p1, x)):
            give[:, span] = value[...]


def first_tail_back(info, seed, gain, *refs):
    far, refs = refs[:18], refs[18:]
    df, du0, da, dgain, dshift, dres, dc0, give = refs[:8]
    du1, near, signals = refs[8], refs[9:21], refs[21]
    spans = []
    for columns in (df.shape[1], du1.shape[1], da.shape[1], dc0.shape[1]):
        spans.append(pl.ds(sum(span.size for span in spans), columns))

    @pl.when(info[0] == 0)
    def pass_on():
        df_in, du0_in, du1_in, da_in, dgain_in, dshift_in = far[12:]
        pass_through(
            (df_in, du0_in, da_in, dgain_in, dshift_in, df_in, du1_in, da_in),
            (df, du0, da, dgain, dshift) + tuple(give.at[:, span] for span in spans[:3]),
            signals,
        )

    @pl.when(info[0] == 1)
    def work():
        n2, i2, d0, s0, u0, d1, s1, u1, n1, i1, o0, o1 = fetch(far[:12], near, signals)
        dcs = tail_backward(
            seed[...].astype(FULL),
            ((s0, s1), n1, i1, n2, i2),
            (o0, o1),
            gain,
            (u0, u1),
            (d0, d1),
            (df, (du0, du1), da, dgain, dshift),
            dres,
        )
        dc0[...] = dcs[0]
        for span, value in zip(spans, (df[...], du1[...], da[...], dcs[1])):
            give[:, span] = value


def cross_backward(
    wides, pairs, rows_t, rows_i, real_t, info,
    tp, ip, dct_own, dci_own, keep, *refs
):
    far, refs = refs[:8], refs[8:]
    dtp_own, dtp_other, dip_own, dip_other, dxt_own, dxt_other, dxi_own, dxi_other = refs[:8]
    wt, wi, dct_other, dci_other, signals = refs[8:]
    width = dct_own.shape[1]
    slabs = width // 128
    half = pairs // 2

    @pl.when(info[0] == 0)
    def pass_on():
        sources = []
        for mine, got in ((far[4], far[5]), (far[6], far[7])):
            start = got.shape[1] - wides[len(sources) // 2] - mine.shape[1]
            sources += [mine, got.at[:, pl.ds(start, mine.shape[1])]]
        pass_through(sources, (dtp_own, dtp_other, dip_own, dip_other), signals)

    @pl.when(info[0] == 1)
    def work():
        got = [far[n].at[:, pl.ds(far[n].shape[1] - width, width)] for n in (2, 3)]
        weights = fetch(
            (got[0], got[1], far[0], far[1]), (dct_other, dci_other, wt, wi), signals
        )
        weights[0].get()
        weights[1].get()
        weights = weights[2:]
        text_keys = lax.broadcasted_iota(jnp.int32, (1, rows_t), 1) < real_t

        def each(pair, carry):
            at_t, at_i = rows_at(pair, rows_t), rows_at(pair, rows_i)
            for group, dct, dci, dtp, dip in (
                (0, dct_own, dci_own, dtp_own, dip_own),
                (half, dct_other, dci_other, dtp_other, dip_other),
            ):
                from_t, from_i = rows_at(pair + group, rows_t), rows_at(pair + group, rows_i)
                kept = keep[lax.rem(pair + group + half * info[1], pairs)] > 0
                texts, images = [], []
                for n in range(slabs):
                    first, second, third = slab(n), slab(slabs + n), slab(2 * slabs + n)
                    texts.append((tp[from_t, first], ip[from_i, second], ip[from_i, third], kept, dct[at_t, first]))
                    images.append((ip[from_i, first], tp[from_t, second], tp[from_t, third], text_keys, dci[at_i, first]))
                results = zip(attend_back_all(texts, 128), attend_back_all(images, 128))
                for n, (text, image) in enumerate(results):
                    first, second, third = slab(n), slab(slabs + n), slab(2 * slabs + n)
                    dtp[at_t, first], dip[at_i, second], dip[at_i, third] = text
                    dip[at_i, first], dtp[at_t, second], dtp[at_t, third] = image
            return carry

        lax.fori_loop(0, half, each, 0)
        for late, triples in (
            (weights[0], ((dtp_own, dxt_own), (dtp_other, dxt_other))),
            (weights[1], ((dip_own, dxi_own), (dip_other, dxi_other))),
        ):
            for dp, dx in triples:
                total = times_back(dp[:, pl.ds(0, width)], late.get()[0])
                for slot in range(1, 3):
                    total += times_back(dp[:, pl.ds(slot * width, width)], late.get()[slot])
                dx[...] = total


def round_up(value, step):
    return -(-value // step) * step


class Layout:
    def __init__(self, blocks, weights):
        self.blocks, self.weights = blocks, weights
        self.sizes = [0, 0]
        self.units = []
        self.after = {}
        for index, (name, depth, width) in enumerate(weights):
            real = depth // blocks
            for unit in range(width // UNIT):
                way = 0 if self.sizes[0] <= self.sizes[1] else 1
                self.units.append((index, unit, way, self.sizes[way], real))
                self.sizes[way] += round_up(real, 16)
            self.after[name] = list(self.sizes)


def pack_body(layout, chosen, kinds, later, info, *refs):
    blocks, weights = layout.blocks, layout.weights
    place = info[2]
    arrays = 1 + max(max(k[0], k[2] or 0) for k in kinds)
    sources, refs = refs[:arrays], refs[arrays + later :]
    targets, refs = refs[: 2 * blocks], refs[2 * blocks :]
    buffers, refs = refs[: len(kinds)], refs[len(kinds) :]
    outs, (total, signals, out_signals) = refs[: 2 * blocks], refs[2 * blocks :]
    waits = []
    for number, (first, column, second, other) in enumerate(kinds):
        buffer = buffers[number]

        def copy(source, start):
            view = sources[source].at[:, pl.ds(start, buffer.shape[1])]
            return pltpu.make_async_copy(view, buffer, signals.at[number])

        if second is None:
            copy(first, column).start()
        else:
            pl.when(info[0] == 1)(copy(first, column).start)
            pl.when(info[0] == 0)(copy(second, other).start)
        waits.append(copy(first, column))
    position, copies = 0, []
    for index, (name, depth, width) in enumerate(weights):
        if name not in chosen:
            continue
        mine = buffers[position : position + chosen[name]]
        for wait in waits[position : position + chosen[name]]:
            wait.wait()
        position += chosen[name]
        span = TILE if width % TILE == 0 else UNIT
        units = [unit for unit in layout.units if unit[0] == index]
        for column in range(0, width, span):
            area = pl.ds(column, span)
            if chosen[name] == 1:
                total[0:depth, 0:span] = mine[0][:, area]
            else:
                x0, x1, y0, y1 = mine
                total[0:depth, 0:span] = back_times(x0[...], y0[:, area]) + back_times(
                    x1[...], y1[:, area]
                )
            for unused, unit, way, row, real in units:
                inside = unit * UNIT - column
                if not 0 <= inside < span:
                    continue
                rows = round_up(real, 16)
                for hop in range(blocks):
                    block = lax.rem(place + (blocks - hop if way == 0 else hop), blocks)
                    source = pl.ds(pl.multiple_of(block * real, 8), rows)
                    outs[way * blocks + hop][row : row + rows, :] = total[
                        source, inside : inside + UNIT
                    ].astype(LOW)
        for way in range(2):
            rows = [(unit[3], unit[3] + round_up(unit[4], 16)) for unit in units if unit[2] == way]
            if not rows:
                continue
            part = pl.ds(rows[0][0], rows[-1][1] - rows[0][0])
            for hop in range(blocks):
                number = way * blocks + hop
                out = pltpu.make_async_copy(
                    outs[number].at[part], targets[number].at[part], out_signals.at[len(copies)]
                )
                out.start()
                copies.append(out)
    for out in copies:
        out.wait()


def pack(layout, factors, info, name, former=None):
    blocks = layout.blocks
    outputs = [shape_of(layout.sizes[way], UNIT) for way in range(2) for hop in range(blocks)]
    deepest = max(weight[1] for weight in layout.weights) + 32
    arrays, kinds, buffers, work = [], [], [], 0

    def number_of(array):
        for number, one in enumerate(arrays):
            if one is array:
                return number
        arrays.append(array)
        return len(arrays) - 1

    for weight in layout.weights:
        for first, second, columns in factors.get(weight[0], ()):
            if isinstance(first, tuple):
                kind = (number_of(first[0]), first[1], number_of(second[0]), second[1])
                array = first[0]
            else:
                kind = (number_of(first), second, None, None)
                array = first
            kinds.append(kind)
            buffers.append(pltpu.VMEM((array.shape[0], columns), array.dtype))
        if weight[0] in factors:
            work += 4 * factors[weight[0]][0][0].shape[0] * weight[1] * weight[2] if len(factors[weight[0]]) > 1 and not isinstance(factors[weight[0]][0][0], tuple) else 800 * weight[1] * weight[2]
    chosen = {name: len(value) for name, value in factors.items()}
    former = tuple(former[0]) + tuple(former[1]) if former else ()
    anywhere = pl.BlockSpec(memory_space=pl.ANY)
    moved = sum(math.prod(v.shape) * 2 for v in outputs) * 2
    outs = pl.pallas_call(
        functools.partial(pack_body, layout, chosen, kinds, len(former)),
        out_shape=tuple(outputs),
        in_specs=[pl.BlockSpec(memory_space=pltpu.SMEM)] + [anywhere] * (len(arrays) + len(former)),
        out_specs=tuple([anywhere] * len(outputs)),
        scratch_shapes=buffers
        + [pltpu.VMEM(v.shape, v.dtype) for v in outputs]
        + [
            pltpu.VMEM((deepest, TILE), FULL),
            pltpu.SemaphoreType.DMA((len(buffers),)),
            pltpu.SemaphoreType.DMA((2 * blocks * len(chosen),)),
        ],
        input_output_aliases={1 + len(arrays) + n: n for n in range(len(former))},
        compiler_params=pltpu.CompilerParams(vmem_limit_bytes=ROOM),
        cost_estimate=pl.CostEstimate(flops=work, bytes_accessed=moved, transcendentals=0),
        name=name,
    )(info, *arrays, *former)
    return [list(outs[:blocks]), list(outs[blocks:])]


def unpack_body(moves, shapes, blocks, later, info, *refs):
    sources = len(shapes)
    inputs, refs = refs[:sources], refs[sources:]
    if later:
        refs = refs[later:]
    count = len(refs) - sources - 1
    outs, wide_refs, signals = refs[:count], refs[count : count + sources], refs[-1]
    place = info[2]
    copies = []
    for source, wide_ref in zip(inputs, wide_refs):
        wide_ref[...] = source[...].astype(FULL)
    for number, (source, way, hop, row, real, target, slot, column, columns, mark) in enumerate(moves):
        block = lax.rem(place + (blocks - hop if way == 0 else hop), blocks)
        rows = pl.ds(pl.multiple_of(block * real, 8), real)
        area = pl.ds(column, columns)
        out = outs[target]
        view = out.at[rows, area] if slot is None else out.at[slot, rows, area]
        copy = pltpu.make_async_copy(
            wide_refs[source].at[pl.ds(row, real), pl.ds(0, columns)], view, signals.at[number]
        )
        wanted = None
        if mark:
            wanted = info[0] == (1 if mark == 1 else 0)
        depth = out.shape[-2]
        if depth < blocks * real:
            inside = block * real < depth
            wanted = inside if wanted is None else jnp.logical_and(wanted, inside)
        copies.append((copy, wanted))
    for step in ("start", "wait"):
        for copy, wanted in copies:
            if wanted is None:
                getattr(copy, step)()
            else:
                pl.when(wanted)(getattr(copy, step))


def unpack(moves, inputs, outputs, former, blocks, info):
    spec = pl.BlockSpec(memory_space=pl.ANY)
    whole = pl.BlockSpec(memory_space=pltpu.VMEM)
    former = tuple(former or ())
    inputs = tuple(inputs)
    rows = [value.shape[0] for value in inputs]
    return pl.pallas_call(
        functools.partial(unpack_body, moves, rows, blocks, len(former)),
        out_shape=tuple(jax.ShapeDtypeStruct(shape, FULL) for shape in outputs),
        in_specs=[pl.BlockSpec(memory_space=pltpu.SMEM)] + [whole] * len(inputs) + [spec] * len(former),
        out_specs=tuple([spec] * len(outputs)),
        scratch_shapes=[pltpu.VMEM((count, UNIT), FULL) for count in rows]
        + [pltpu.SemaphoreType.DMA((len(moves),))],
        input_output_aliases={1 + len(inputs) + n: n for n in range(len(former))},
        compiler_params=pltpu.CompilerParams(vmem_limit_bytes=ROOM),
        cost_estimate=pl.CostEstimate(flops=0, bytes_accessed=6 * sum(rows) * UNIT, transcendentals=0),
        name="unpack",
    )(info, *inputs, *former)


CORES = [(0, 1), (1, 0)]


def to_other_core(values):
    return lax.ppermute(values, "tensor", CORES)


def to_other_section(values):
    return lax.ppermute(values, "section", CORES)


def to_layer(values, layer):
    return lax.ppermute(values, "section", [(1 - layer, layer)])


def ring_order():
    places = list(range(lax.axis_size("dp")))
    return places[0::2] + places[1::2][::-1]


def ring_place():
    place, count = lax.axis_index("dp"), lax.axis_size("dp")
    return jnp.where(place % 2 == 0, place // 2, count - 1 - place // 2)


def to_next(values, way):
    order = ring_order()
    route = list(zip(order, order[1:] + order[:1]))
    if way == 1:
        route = [(there, here) for here, there in route]
    return lax.ppermute(values, "dp", route)


def after(values, token):
    if token is None:
        return values
    return lax.optimization_barrier((values, token))[0]


class Ring:
    def __init__(self, parts):
        self.parts = parts
        self.count = len(parts[0])
        self.pieces = [[None] * self.count, [None] * self.count]
        self.step = 0
        self.last = 2 * (self.count - 1)
        self.flying = [to_next(parts[way][1], way) for way in range(2)]

    def advance(self, token):
        got = [after(self.flying[0], token), after(self.flying[1], token)]
        turn, count = self.step, self.count
        self.step += 1
        if turn < count - 1:
            got = [got[way] + self.parts[way][(turn + 2) % count] for way in range(2)]
        hop = max(turn - (count - 2), 0)
        if turn >= count - 2:
            for way in range(2):
                self.pieces[way][hop] = got[way]
        if self.step < self.last:
            self.flying = [to_next(got[way], way) for way in range(2)]
        return tuple(got), (hop if turn >= count - 2 else None)


def shards(
    text_stream,
    image_stream,
    region_mask,
    co_text_in,
    co_text_out,
    self_text_in,
    self_text_out,
    image_attn_in,
    image_attn_out,
    text_up,
    text_down,
    image_up,
    image_down,
    text_gain,
    text_shift,
    image_gain,
    image_shift,
):
    front = lax.axis_index("section") == 0
    core = lax.axis_index("tensor")
    blocks = lax.axis_size("dp")
    in_ring = blocks == 8
    place = ring_place() if in_ring else 0 * core
    info = jnp.stack([front.astype(jnp.int32), core.astype(jnp.int32), place.astype(jnp.int32)])
    pairs = text_stream.shape[1]
    half = pairs // 2
    real_t, real_i = text_stream.shape[2], image_stream.shape[2]
    rows_t, rows_i = round_up(real_t, 16), round_up(real_i, 16)
    wide_t, wide_i = text_stream.shape[3], image_stream.shape[3]
    text_size = D_TEXT // HEADS_TEXT
    image_size = D_IMAGE // HEADS_IMAGE

    def flat_rows(values, rows):
        grown = jnp.pad(values, ((0, 0), (0, rows - values.shape[1]), (0, 0)))
        return grown.reshape(values.shape[0] * rows, values.shape[2])

    def by_slot(weight):
        return jnp.transpose(weight, (1, 0, 2))

    own_t, own_i = half * rows_t, half * rows_i
    all_t, all_i = pairs * rows_t, pairs * rows_i
    keep = jnp.pad(region_mask, ((0, 0), (0, rows_i - real_i))).reshape(pairs, 1, rows_i)
    gain_t, shift_t, gain_i, shift_i = text_gain[0], text_shift[0], image_gain[0], image_shift[0]
    cross_in, image_in, single_in = by_slot(co_text_in), by_slot(image_attn_in[0]), by_slot(self_text_in)
    image_out, up_i, down_i = image_attn_out[0], image_up[0], image_down[0]
    up_t, down_t = text_up[0], text_down[0]
    image_out_2, cross_out_2 = to_other_core(image_out), to_other_core(co_text_out)
    up_i_2, down_i_2 = to_other_core(up_i), to_other_core(down_i)
    up_t_2, down_t_2 = to_other_core(up_t), to_other_core(down_t)
    cross = cross_in.shape[2]
    single = single_in.shape[2]
    ff_t, ff_i = up_t.shape[1], up_i.shape[1]
    tail_t = (up_t, down_t, up_t_2, down_t_2)
    tail_i = (up_i, down_i, up_i_2, down_i_2)

    far = (cross_in, image_in)
    xt_own, xt_other, xi_own, xi_other, tp, ip, ct_own, ct_give, ci_own, ci_give = launch(
        functools.partial(cross_forward, pairs, rows_t, rows_i, real_t),
        [shape_of(own_t, wide_t)] * 2
        + [shape_of(own_i, wide_i)] * 2
        + [shape_of(all_t, 3 * cross), shape_of(all_i, 3 * cross)]
        + [shape_of(own_t, cross)] * 2
        + [shape_of(own_i, cross)] * 2,
        (flat_rows(text_stream[0], rows_t), flat_rows(image_stream[0], rows_i), keep),
        far=far,
        scratch=[pltpu.VMEM((all_t, wide_t), LOW), pltpu.VMEM((all_i, wide_i), LOW)] + buffers_for(far),
        flag=info,
        work=6 * cross * (all_t * wide_t + all_i * wide_i),
        name="cross_forward",
    )
    ct_other, ci_other = ct_give, ci_give
    ci_2 = to_other_core(ci_give)
    ct_2 = to_other_core(ct_give)

    def run_first_tail(x, c0, c1, o0, o1, gain, shift, ff, rows, width, hidden, name):
        low_w, low_h = shape_of(rows, width), shape_of(rows, hidden)
        far = (o0, o1) + ff
        return launch(
            first_tail,
            [low_w, low_w, low_h, low_h]
            + [shape_of(rows, hidden, FULL)] * 2
            + [shape_of(rows, width, FULL), shape_of(rows, 128, FULL)] * 2,
            (x, c0, c1, gain, shift),
            far=far,
            scratch=[pltpu.VMEM((rows, width), FULL)] + buffers_for(far),
            flag=info,
            work=4 * rows * width * (o0.shape[0] + 2 * hidden),
            name=name,
        )

    bi, yi, hi0, hi1, si0, si1, ni1, ii1, ni2, ii2 = run_first_tail(
        after(xi_own, (up_t_2, down_t_2, cross_out_2, ct_2)), ci_own, ci_2, image_out, image_out_2, gain_i, shift_i,
        tail_i, own_i, wide_i, ff_i, "tail_i"
    )
    image_in_2, single_in_2, single_out_2 = [
        to_other_core(after(value, bi)) for value in (image_in, single_in, self_text_out)
    ]
    bi_here, bi = bi, to_layer(bi, 1)
    bt, yt, ht0, ht1, st0, st1, nt1, it1, nt2, it2 = run_first_tail(
        after(xt_own, bi_here), ct_own, ct_2, co_text_out, cross_out_2, gain_t, shift_t, tail_t, own_t, wide_t, ff_t, "tail_t"
    )

    def run_self(rows, real, size, width, hidden, x, w0, w1, masked, o0, o1, gain, shift, ff, seed, y, h0, h1, c, name):
        count = half * rows
        inner = w0.shape[2]
        low_w, low_h = shape_of(count, width), shape_of(count, hidden)
        outputs = [low_w, low_w, shape_of(count, cross), shape_of(count, 3 * cross)]
        outputs += [low_w, low_w, low_h, low_h, low_w, low_h] + [shape_of(2, width, FULL)] * 2
        outputs += [shape_of(count, 2 * width + hidden + 4 * cross)]
        scratch = [pltpu.VMEM((count, 3 * inner), LOW)] * 2
        scratch += [pltpu.VMEM((count, hidden), FULL)] * 2
        scratch += [pltpu.VMEM((count, width), FULL), pltpu.VMEM((count, 128), FULL)] * 2
        scratch += [pltpu.VMEM((count, width), FULL)] + [pltpu.VMEM((count, inner), LOW)] * 2
        scratch += [pltpu.VMEM((count, columns), LOW) for columns in (hidden, cross, 3 * cross)]
        weights = (w0, w1, o0, o1) + ff
        return launch(
            functools.partial(self_layer, masked, half, rows, real, size, cross),
            outputs,
            (x, seed, gain, shift, keep),
            far=weights + (y, h0, h1, c),
            scratch=scratch + buffers_for(weights),
            flag=info,
            work=8 * count * width * (4 * inner + 2 * hidden),
            name=name,
        )

    i2 = run_self(
        rows_i, real_i, image_size, wide_i, ff_i, bi, image_in, image_in_2, True, image_out, image_out_2,
        gain_i, shift_i, tail_i, xi_own, yi, hi0, hi1, ci_own, "self_i",
    )
    seed_i = to_layer(i2[1], 0)
    bt = to_layer(bt, 1)
    t2 = run_self(
        rows_t, real_t, text_size, wide_t, ff_t, after(bt, i2[1]), single_in, single_in_2, False,
        self_text_out, single_out_2, gain_t, shift_t, tail_t, xt_own, yt, ht0, ht1, ct_own, "self_t",
    )
    seed_t = to_layer(t2[1], 0)
    (oi, unused, ci_own, pi_own, dai, dfi, dui0, dui1, yi, hi0, dgi, dsi, give_i) = i2
    (ot, unused, ct_own, pt_own, dat, dft, dut0, dut1, yt, ht0, dgt, dst, give_t) = t2
    left_t, left_i = to_other_core(give_t), to_other_core(give_i)

    def run_tail_back(seed, kept, o0, o1, gain, ff, given, rows, width, hidden, name):
        low_w, low_h = shape_of(rows, width), shape_of(rows, hidden)
        outputs = [low_w, low_h, low_w] + [shape_of(2, width, FULL)] * 2
        outputs += [shape_of(rows, width, FULL), shape_of(rows, cross)]
        outputs += [shape_of(rows, 2 * width + hidden + cross)]
        s0, s1, n1, i1, n2, i2 = kept
        u0, d0, u1, d1 = ff
        late = (n2, i2, d0, s0, u0, d1, s1, u1, n1, i1, o0, o1)
        return launch(
            first_tail_back,
            outputs,
            (seed, gain),
            far=late + given,
            scratch=[pltpu.VMEM((rows, hidden), LOW)] + buffers_for(late),
            flag=info,
            work=4 * rows * width * (cross + 2 * hidden),
            name=name,
        )


    def choose(first, second):
        return jnp.where(front, first, second)

    ff_layout = Layout(
        blocks,
        [
            ("down_t", ff_t, wide_t),
            ("up_t", wide_t, ff_t),
            ("up_i", wide_i, ff_i),
            ("down_i", ff_i, wide_i),
        ],
    )
    attn_layout = Layout(
        blocks,
        [
            ("in_t", wide_t, 3 * cross),
            ("out_t", cross, wide_t),
            ("in_i", wide_i, 3 * cross),
            ("out_i", cross, wide_i),
            ("small", blocks * 16, UNIT),
        ],
    )
    text_rows = attn_layout.after["out_t"]

    out = run_tail_back(
        seed_i, (si0, si1, ni1, ii1, ni2, ii2), image_out, image_out_2, gain_i, tail_i,
        (dfi, dui0, dui1, dai, dgi, dsi), own_i, wide_i, ff_i, "tail_back_i",
    )
    dfi, dui0, dai, dgi, dsi, dri, dci_own, give_i = out
    right_i = to_other_core(give_i)
    out = run_tail_back(
        after(seed_t, dci_own), (st0, st1, nt1, it1, nt2, it2), co_text_out, cross_out_2, gain_t, tail_t,
        (dft, dut0, dut1, dat, dgt, dst), own_t, wide_t, ff_t, "tail_back_t",
    )
    dft, dut0, dat, dgt, dst, drt, dct_own, give_t = out
    right_t = to_other_core(give_t)
    small = jnp.concatenate([dgt, dst, dgi, dsi], axis=1)
    small = small + to_other_core(small)
    small_rows = round_up(-(-small.size // UNIT), blocks) // blocks
    small = jnp.pad(small.reshape(-1), (0, blocks * small_rows * UNIT - small.size))
    small = small.reshape(blocks, small_rows, UNIT)
    small = jnp.pad(small, ((0, 0), (0, 16 - small_rows), (0, 0))).reshape(blocks * 16, UNIT)
    ff_parts = pack(
        ff_layout,
        {
            "down_t": ((ht0, 0, ff_t), (left_t, wide_t, ff_t), (after(dft, small), 0, wide_t), (right_t, 0, wide_t)),
            "up_t": ((yt, 0, wide_t), (left_t, 0, wide_t), (dut0, 0, ff_t), (right_t, wide_t, ff_t)),
            "up_i": ((yi, 0, wide_i), (left_i, 0, wide_i), (dui0, 0, ff_i), (right_i, wide_i, ff_i)),
            "down_i": ((hi0, 0, ff_i), (left_i, wide_i, ff_i), (dfi, 0, wide_i), (right_i, 0, wide_i)),
        },
        info,
        "pack_ff",
    )
    token = ff_parts[0][1]
    ff = Ring(ff_parts) if in_ring else None
    far = (cross_in, image_in)
    out = launch(
        functools.partial(cross_backward, (wide_t, wide_i), pairs, rows_t, rows_i, real_t),
        [shape_of(own_t, 3 * cross)] * 2
        + [shape_of(own_i, 3 * cross)] * 2
        + [shape_of(own_t, wide_t, FULL)] * 2
        + [shape_of(own_i, wide_i, FULL)] * 2,
        (after(tp, token), ip, dct_own, dci_own, keep),
        far=far + (right_t, right_i, pt_own, left_t, pi_own, left_i),
        scratch=[pltpu.VMEM(v.shape, v.dtype) for v in far]
        + [pltpu.VMEM((own_t, cross), LOW), pltpu.VMEM((own_i, cross), LOW), pltpu.SemaphoreType.DMA((4,))],
        flag=info,
        work=6 * cross * (all_t * wide_t + all_i * wide_i),
        name="cross_backward",
    )
    dtp_own, dtp_other, dip_own, dip_other, dxt_own, dxt_give, dxi_own, dxi_give = out
    token = dtp_own
    if in_ring:
        token, unused = ff.advance(token)

    def columns(part, wide, hidden):
        starts = {"c": wide + hidden, "x": wide + hidden + 4 * cross}
        return starts[part]

    ct_column, xt_column = columns("c", wide_t, ff_t), columns("x", wide_t, ff_t)
    ci_column, xi_column = columns("c", wide_i, ff_i), columns("x", wide_i, ff_i)
    attn_parts = pack(
        attn_layout,
        {
            "in_t": (
                ((xt_own, 0), (bt, 0), wide_t),
                ((xt_other, 0), (left_t, xt_column), wide_t),
                (after(dtp_own, token), 0, 3 * cross),
                (dtp_other, 0, 3 * cross),
            ),
            "out_t": (
                (ct_own, 0, cross),
                ((ct_give, 0), (left_t, ct_column), cross),
                (dat, 0, wide_t),
                (right_t, wide_t + ff_t, wide_t),
            ),
            "in_i": (
                ((xi_own, 0), (bi, 0), wide_i),
                ((xi_other, 0), (left_i, xi_column), wide_i),
                (dip_own, 0, 3 * cross),
                (dip_other, 0, 3 * cross),
            ),
            "out_i": (
                (ci_own, 0, cross),
                ((ci_give, 0), (left_i, ci_column), cross),
                (dai, 0, wide_i),
                (right_i, wide_i + ff_i, wide_i),
            ),
            "small": ((small, 0, UNIT),),
        },
        info,
        "pack_attention",
    )

    def choose(first, second):
        return jnp.where(front, first, second)

    def result(rest, partial, other, output, rows, real, token):
        mine = choose(rest + partial + to_other_core(after(other, token)), output.astype(FULL))
        mine = mine.astype(LOW).reshape(half, rows, -1)[:, :real]
        got = to_other_core(mine)
        return jnp.concatenate(
            [jnp.where(core == 0, mine, got), jnp.where(core == 0, got, mine)], axis=0
        )[None]

    main_shapes = [
        (ff_t, wide_t),
        (wide_t, ff_t),
        (wide_i, ff_i),
        (ff_i, wide_i),
        (3, wide_i, cross),
        (cross, wide_i),
        (blocks * 16, UNIT),
    ]
    text_shapes = [(3, wide_t, cross), (cross, wide_t), (3, wide_t, single), (self_text_out.shape[0], wide_t)]
    main_moves, text_moves = [], []

    def move(target, source, way, row, real, unit, output, shape, mark=0):
        slot, column, columns = None, unit * UNIT, UNIT
        if len(shape) == 3:
            slot, column = column // cross, column % cross
            columns = min(UNIT, shape[2] - column)
        if columns > 0:
            target.append((source, way, row, real, output, slot, column, columns, mark))

    for index, unit, way, row, real in ff_layout.units:
        move(main_moves, way, way, row, real, unit, index, main_shapes[index])
    for index, unit, way, row, real in attn_layout.units:
        if index >= 2:
            move(main_moves, 2 + way, way, row, real, unit, index + 2, main_shapes[index + 2])
        else:
            for mark in (1, 2):
                move(text_moves, way + 2 * (mark - 1), way, row, real, unit, index, text_shapes[index], mark)
                move(text_moves, way + 4 - 2 * mark, way, row, real, unit, index + 2, text_shapes[index + 2], mark)

    main, text = None, None

    def shifted(moves, hop, source_shift, row_shift):
        result = []
        for source, way, row, *rest in moves:
            result.append((source_shift(source), way, hop, row + row_shift(source), *rest))
        return result

    def spread_main(hops, ff, attn, main):
        inputs, moves = [], []
        for number, hop in enumerate(hops):
            inputs += [ff[0][hop], ff[1][hop], attn[0][hop], attn[1][hop]]
            moves += shifted(main_moves, hop, lambda source: source + 4 * number, lambda source: 0)
        return unpack(moves, inputs, main_shapes, main, blocks, info)

    def spread_text(hops, attn, crossed, text):
        inputs, moves, both = [], [], text_rows[0] + text_rows[1]
        for hop in hops:
            inputs += [attn[0][hop], attn[1][hop]]
        places = []
        for array in crossed:
            places += [(len(inputs), row) for row in range(0, array.shape[0], both)]
            inputs.append(array)
        for number, hop in enumerate(hops):
            moves += shifted(
                text_moves,
                hop,
                lambda source: source + 2 * number if source < 2 else places[number][0],
                lambda source: 0 if source < 2 else places[number][1] + (source - 2) * text_rows[0],
            )
        return unpack(moves, inputs, text_shapes, text, blocks, info)

    def cross_over(attn, hops):
        return to_other_section(
            jnp.concatenate([attn[way][hop][: text_rows[way]] for hop in hops for way in range(2)], axis=0)
        )

    if in_ring:
        attn = Ring(attn_parts)
        token = attn_parts[0][1]
        results = (
            result(drt, dxt_own, dxt_give, ot, rows_t, real_t, token),
            result(dri, dxi_own, dxi_give, oi, rows_i, real_i, token),
        )
        token = (token, results)
        groups = [(0, 1), (2, 3), (4, 5), (6,), (7,)]
        crossed = [None] * len(groups)
        while attn.step < attn.last:
            if ff.step < ff.last:
                token, unused = ff.advance(token)
            token, hop = attn.advance(token)
            if hop is None:
                continue
            if hop == 2:
                first = after(crossed[0], token)
                relay = [to_next(first[: text_rows[0]], 1), to_next(first[text_rows[0] : sum(text_rows)], 0)]
            if hop == 4:
                crossed[-1] = jnp.concatenate([after(value, token) for value in relay], axis=0)
                token = (token, crossed[-1])
            for number, group in enumerate(groups):
                if hop == group[-1]:
                    if number < len(groups) - 1:
                        crossed[number] = cross_over(attn.pieces, group)
                    main = spread_main(group, ff.pieces, attn.pieces, main)
                    token = (token, main)
                elif number and hop == group[0] and len(group) > 1:
                    text = spread_text(groups[number - 1], attn.pieces, [crossed[number - 1]], text)
                    token = (token, text)
        text = spread_text(groups[-3], attn.pieces, crossed[-3:-2], text)
        text = spread_text((6, 7), attn.pieces, crossed[-2:], text)
    else:
        results = (
            result(drt, dxt_own, dxt_give, ot, rows_t, real_t, token),
            result(dri, dxi_own, dxi_give, oi, rows_i, real_i, token),
        )
        ff, attn = lax.psum((ff_parts, attn_parts), "dp")
        for hop in range(0, blocks, 2):
            main = spread_main((hop, hop + 1), ff, attn, main)
            text = spread_text((hop, hop + 1), attn, [cross_over(attn, (hop, hop + 1))], text)
    down_t_grad, up_t_grad, up_i_grad, down_i_grad, in_i_grad, out_i_grad, small = main
    co_in_grad, co_out_grad, self_in_grad, self_out_grad = text
    small = small.reshape(blocks, 16, UNIT)[:, :small_rows].reshape(-1)[: 4 * (wide_t + wide_i)]
    small = small.reshape(2, 2 * (wide_t + wide_i))
    small = jnp.split(small, [wide_t, 2 * wide_t, 2 * wide_t + wide_i], axis=1)

    return (
        results[0],
        results[1],
        by_slot(co_in_grad),
        co_out_grad,
        by_slot(self_in_grad),
        self_out_grad,
        by_slot(in_i_grad)[None],
        out_i_grad[None],
        up_t_grad[None],
        down_t_grad[None],
        up_i_grad[None],
        down_i_grad[None],
        small[0][None],
        small[1][None],
        small[2][None],
        small[3][None],
    )


def solution(mesh):
    in_specs = (
        P("section", "dp", None, None),
        P("section", "dp", None, None),
        P("dp", None),
        P(None, None, "tensor"),
        P("tensor", None),
        P(None, None, "tensor"),
        P("tensor", None),
        P("section", None, None, "tensor"),
        P("section", "tensor", None),
        P("section", None, "tensor"),
        P("section", "tensor", None),
        P("section", None, "tensor"),
        P("section", "tensor", None),
        P("section", None, None),
        P("section", None, None),
        P("section", None, None),
        P("section", None, None),
    )
    out_specs = (
        P("section", "dp", None, None),
        P("section", "dp", None, None),
        P(None, None, "tensor"),
        P("tensor", None),
        P(None, None, "tensor"),
        P("tensor", None),
        P("section", None, None, "tensor"),
        P("section", "tensor", None),
        P("section", None, "tensor"),
        P("section", "tensor", None),
        P("section", None, "tensor"),
        P("section", "tensor", None),
        P("section", None, None),
        P("section", None, None),
        P("section", None, None),
        P("section", None, None),
    )
    return jax.shard_map(shards, mesh=mesh, in_specs=in_specs, out_specs=out_specs, check_vma=False)
```

time: 843 us -> 468 us (0.56)
  matrix products: 211 us -> 0 us
  Pallas kernels: 0 us -> 131 us
  waiting for transfers between devices: 342 us -> 221 us
  local copies, waits for them, and re-layouts: 104 us -> 22.2 us
  other arithmetic: 60.6 us -> 9.05 us
  starting transfers between devices: 108 us -> 73 us
    dot_general x116 -> x0, matrix products: 204 us -> none  [dot(): return jnp.einsum(spec, left, right, preferred_element_type=FULL)]
    pallas_call x0 -> x19, Pallas kernels: none -> 131 us  [the longest x8 74.9 us: launch(): pl.pallas_call(body, out_shape=tuple(outputs), in_specs=specs, out_specs=...]
    ppermute x86, waiting for transfers between devices: 342 us -> 221 us  [the longest x58 182 us: to_next(): return lax.ppermute(values, 'dp', route)]
    convert_element_type x58 -> x0, local copies, waits for them, and re-layouts: 51 us -> none  [the longest x14 14.6 us: attend_back(): dkeys.reshape(keys.shape).astype(LOW)]
    ppermute x86, starting transfers between devices: 108 us -> 73 us  [the longest x58 61.8 us: to_next(): return lax.ppermute(values, 'dp', route)]
    convert_element_type x48 -> x2, other arithmetic: 28.2 us -> 0.49 us  [result(): mine = mine.astype(LOW).reshape(half, rows, -1)[:, :real]]
    select_n x38 -> x2, other arithmetic: 16.4 us -> 1.37 us  [result(): jnp.where(core == 0, mine, got)]
    another operation x26 -> x0, local copies, waits for them, and re-layouts: 10.9 us -> none  [the longest x18 8.5 us: heads_of(): values.reshape(values.shape[0], values.shape[1], values.shape[2] // size,...]
  transfers between devices with their start and end apart: 86 -> 86, of which waited for: 31 -> 38; matrix products, arithmetic and copies ran while one was open for 43% -> 4% of each run, Pallas kernels for 0% -> 22%
where the time goes in v2:
time: 468 us; the launch traced here: 459 us
  waiting for transfers between devices  221 us (47%)
  Pallas kernels  131 us (28%)
  starting transfers between devices  73 us (16%)
  local copies, waits for them, and re-layouts  22.2 us (5%)
  other arithmetic  9.05 us (2%)
    ppermute x58, waiting for transfers between devices, to_next(): return lax.ppermute(values, 'dp', route)  182 us
    pallas_call x8, Pallas kernels, launch(): pl.pallas_call(body, out_shape=tuple(outputs), in_specs=specs, out_specs=...  74.9 us
    ppermute x58, starting transfers between devices, to_next(): return lax.ppermute(values, 'dp', route)  61.8 us
    pallas_call x9, Pallas kernels, unpack(): pl.pallas_call(functools.partial(unpack_body, moves, rows, blocks, len(fo...  37.1 us
    ppermute x4, waiting for transfers between devices, to_layer(): return lax.ppermute(values, 'section', [(1 - layer, layer)])  28.5 us
    pallas_call x2, Pallas kernels, pack(): pl.pallas_call(functools.partial(pack_body, layout, chosen, kinds, len(fo...  19.3 us
    unnamed x196, local copies, waits for them, and re-layouts  15.1 us
    ppermute x20, waiting for transfers between devices, to_other_core(): return lax.ppermute(values, 'tensor', CORES)  10.6 us
  transfers between devices with their start and end apart: 86, of which 38 were waited for; matrix products, arithmetic and copies ran while one was open for 4% of the time, Pallas kernels for 22%

profile of v2, /device:TPU:0, one launch (start us, length us, event | category | flops | bytes accessed | tf_op | source)
XLA Modules:
  0.0 459.4 jit_solution(11493387472936424428)
XLA Ops:
  6.9 11.5 %cross_forward.1 = (bf16[192,768]{1,0:T(8,128)(2,1)}, bf16[192,768]{1,0:T(8,128)(2,1)}, bf16[224,1024]{1,0:T(8,128)(2,1)}, bf16[224,1024]{1,0:T(8,128)(2,1)}, bf...) custom-call(s32[3]{0:T(128)} %pad_add_fusion.info, ...), custom_call_target="tpu_custom_call" | custom-call | flops 2315255808 | bytes 11929344 | tf_op jit(solution)/shard_map/cross_forward/pallas_call | solution.py:216
  25.7 8.1 %tail_i.1 = (bf16[224,1024]{1,0:T(8,128)(2,1)}, bf16[224,1024]{1,0:T(8,128)(2,1)}, bf16[224,512]{1,0:T(8,128)(2,1)}, bf16[224,512]{1,0:T(8,128)(2,1)}, f32[224,5...) custom-call(s32[3]{0:T(128)} %pad_add_fusion.info, ...), custom_call_target="tpu_custom_call" | custom-call | flops 1409286144 | bytes 11583488 | tf_op jit(solution)/shard_map/tail_i/pallas_call | solution.py:216
  36.0 10.1 %tail_t.1 = (bf16[192,768]{1,0:T(8,128)(2,1)}, bf16[192,768]{1,0:T(8,128)(2,1)}, bf16[192,1536]{1,0:T(8,128)(2,1)}, bf16[192,1536]{1,0:T(8,128)(2,1)}, f32[192,1...) custom-call(s32[3]{0:T(128)} %pad_add_fusion.info, ...), custom_call_target="tpu_custom_call" | custom-call | flops 2113929216 | bytes 17215488 | tf_op jit(solution)/shard_map/tail_t/pallas_call | solution.py:216
  49.3 5.4 %self_i.1 = (bf16[224,1024]{1,0:T(8,128)(2,1)}, bf16[224,1024]{1,0:T(8,128)(2,1)}, bf16[224,512]{1,0:T(8,128)(2,1)}, bf16[224,1536]{1,0:T(8,128)(2,1)}, bf16[224...) custom-call(s32[3]{0:T(128)} %pad_add_fusion.info, ...), custom_call_target="tpu_custom_call" | custom-call | flops 5637144576 | bytes 20645632 | tf_op jit(solution)/shard_map/self_i/pallas_call | solution.py:216
  56.8 5.6 %self_t.1 = (bf16[192,768]{1,0:T(8,128)(2,1)}, bf16[192,768]{1,0:T(8,128)(2,1)}, bf16[192,512]{1,0:T(8,128)(2,1)}, bf16[192,1536]{1,0:T(8,128)(2,1)}, bf16[192,7...) custom-call(s32[3]{0:T(128)} %pad_add_fusion.info, ...), custom_call_target="tpu_custom_call" | custom-call | flops 5435817984 | bytes 22439680 | tf_op jit(solution)/shard_map/self_t/pallas_call | solution.py:216
  64.1 17.5 %collective-permute-done.14.seed = bf16[224,1024]{1,0:T(8,128)(2,1)S(1)} collective-permute-done((bf16[224,1024]{1,0:T(8,128)(2,1)}, bf16[224,1024]{1,0:T(8,128)(2,1)S(1)}, u32[]{:S(2)}, u32[]{:S(2)}) %collective-permute-start.14) | collective-permute-done | bytes 458784 | tf_op jit(solution)/shard_map/ppermute | solution.py:696
  82.4 8.5 %tail_back_i.1 = (bf16[224,1024]{1,0:T(8,128)(2,1)}, bf16[224,512]{1,0:T(8,128)(2,1)}, bf16[224,1024]{1,0:T(8,128)(2,1)}, f32[2,1024]{1,0:T(2,128)}, f32[2,1024]...) custom-call(s32[3]{0:T(128)} %pad_add_fusion.info, ...), custom_call_target="tpu_custom_call" | custom-call | flops 1409286144 | bytes 14819328 | tf_op jit(solution)/shard_map/tail_back_i/pallas_call | solution.py:216
  90.9 11.0 %collective-permute-done.13.seed = bf16[192,768]{1,0:T(8,128)(2,1)S(1)} collective-permute-done((bf16[192,768]{1,0:T(8,128)(2,1)}, bf16[192,768]{1,0:T(8,128)(2,1)S(1)}, u32[]{:S(2)}, u32[]{:S(2)}) %collective-permute-start.13) | collective-permute-done | bytes 294944 | tf_op jit(solution)/shard_map/ppermute | solution.py:696
  102.6 10.9 %tail_back_t.1 = (bf16[192,768]{1,0:T(8,128)(2,1)}, bf16[192,1536]{1,0:T(8,128)(2,1)}, bf16[192,768]{1,0:T(8,128)(2,1)}, f32[2,768]{1,0:T(2,128)}, f32[2,768]{1,...) custom-call(s32[3]{0:T(128)} %pad_add_fusion.info, ...), custom_call_target="tpu_custom_call" | custom-call | flops 2113929216 | bytes 20183040 | tf_op jit(solution)/shard_map/tail_back_t/pallas_call | solution.py:216
  120.8 9.7 %pack_ff.1 = (bf16[832,256]{1,0:T(8,128)(2,1)}, bf16[832,256]{1,0:T(8,128)(2,1)}, bf16[832,256]{1,0:T(8,128)(2,1)}, bf16[832,256]{1,0:T(8,128)(2,1)}, bf16[832,2...) custom-call(s32[3]{0:T(128)} %pad_add_fusion.info, ...), custom_call_target="tpu_custom_call" | custom-call | flops 2751463424 | bytes 13631488 | tf_op jit(solution)/shard_map/pack_ff/pallas_call | solution.py:608
  133.5 14.6 %cross_backward.1 = (bf16[192,1536]{1,0:T(8,128)(2,1)}, bf16[192,1536]{1,0:T(8,128)(2,1)}, bf16[224,1536]{1,0:T(8,128)(2,1)}, bf16[224,1536]{1,0:T(8,128)(2,1)},...) custom-call(s32[3]{0:T(128)} %pad_add_fusion.info, ...), custom_call_target="tpu_custom_call" | custom-call | flops 2315255808 | bytes 22120192 | tf_op jit(solution)/shard_map/cross_backward/pallas_call | solution.py:216
  148.5 9.6 %pack_attention.1 = (bf16[928,256]{1,0:T(8,128)(2,1)}, bf16[928,256]{1,0:T(8,128)(2,1)}, bf16[928,256]{1,0:T(8,128)(2,1)}, bf16[928,256]{1,0:T(8,128)(2,1)}, bf1...) custom-call(s32[3]{0:T(128)} %pad_add_fusion.info, ...), custom_call_target="tpu_custom_call" | custom-call | flops 2999975936 | bytes 14811136 | tf_op jit(solution)/shard_map/pack_attention/pallas_call | solution.py:608
  178.4 8.8 %collective-permute-done.26 = bf16[928,256]{1,0:T(8,128)(2,1)S(1)} collective-permute-done((bf16[928,256]{1,0:T(8,128)(2,1)S(1)}, bf16[928,256]{1,0:T(8,128)(2,1)S(1)}, u32[]{:S(2)}, u32[]{:S(2)}) %collective-permute-start.26) | collective-permute-done | bytes 475168 | tf_op jit(solution)/shard_map/ppermute | solution.py:714
  191.6 8.8 %collective-permute-done.32 = bf16[832,256]{1,0:T(8,128)(2,1)S(1)} collective-permute-done((bf16[832,256]{1,0:T(8,128)(2,1)S(1)}, bf16[832,256]{1,0:T(8,128)(2,1)S(1)}, u32[]{:S(2)}, u32[]{:S(2)}) %collective-permute-start.32) | collective-permute-done | bytes 426016 | tf_op jit(solution)/shard_map/ppermute | solution.py:714
  200.4 7.8 %collective-permute-done.30 = bf16[832,256]{1,0:T(8,128)(2,1)S(1)} collective-permute-done((bf16[832,256]{1,0:T(8,128)(2,1)S(1)}, bf16[832,256]{1,0:T(8,128)(2,1)S(1)}, u32[]{:S(2)}, u32[]{:S(2)}) %collective-permute-start.30) | collective-permute-done | bytes 426016 | tf_op jit(solution)/shard_map/ppermute | solution.py:714
  213.1 9.1 %collective-permute-done.36 = bf16[832,256]{1,0:T(8,128)(2,1)S(1)} collective-permute-done((bf16[832,256]{1,0:T(8,128)(2,1)S(1)}, bf16[832,256]{1,0:T(8,128)(2,1)S(1)}, u32[]{:S(2)}, u32[]{:S(2)}) %collective-permute-start.36) | collective-permute-done | bytes 426016 | tf_op jit(solution)/shard_map/ppermute | solution.py:714
  222.2 6.6 %collective-permute-done.34 = bf16[832,256]{1,0:T(8,128)(2,1)S(1)} collective-permute-done((bf16[832,256]{1,0:T(8,128)(2,1)S(1)}, bf16[832,256]{1,0:T(8,128)(2,1)S(1)}, u32[]{:S(2)}, u32[]{:S(2)}) %collective-permute-start.34) | collective-permute-done | bytes 426016 | tf_op jit(solution)/shard_map/ppermute | solution.py:714
  233.5 9.3 %collective-permute-done.40 = bf16[832,256]{1,0:T(8,128)(2,1)S(1)} collective-permute-done((bf16[832,256]{1,0:T(8,128)(2,1)S(1)}, bf16[832,256]{1,0:T(8,128)(2,1)S(1)}, u32[]{:S(2)}, u32[]{:S(2)}) %collective-permute-start.40) | collective-permute-done | bytes 426016 | tf_op jit(solution)/shard_map/ppermute | solution.py:714
  242.9 6.1 %collective-permute-done.38 = bf16[832,256]{1,0:T(8,128)(2,1)S(1)} collective-permute-done((bf16[832,256]{1,0:T(8,128)(2,1)S(1)}, bf16[832,256]{1,0:T(8,128)(2,1)S(1)}, u32[]{:S(2)}, u32[]{:S(2)}) %collective-permute-start.38) | collective-permute-done | bytes 426016 | tf_op jit(solution)/shard_map/ppermute | solution.py:714
  253.7 8.9 %collective-permute-done.44 = bf16[832,256]{1,0:T(8,128)(2,1)S(1)} collective-permute-done((bf16[832,256]{1,0:T(8,128)(2,1)S(1)}, bf16[832,256]{1,0:T(8,128)(2,1)S(1)}, u32[]{:S(2)}, u32[]{:S(2)}) %collective-permute-start.44) | collective-permute-done | bytes 426016 | tf_op jit(solution)/shard_map/ppermute | solution.py:714
  262.6 6.6 %collective-permute-done.42 = bf16[832,256]{1,0:T(8,128)(2,1)S(1)} collective-permute-done((bf16[832,256]{1,0:T(8,128)(2,1)S(1)}, bf16[832,256]{1,0:T(8,128)(2,1)S(1)}, u32[]{:S(2)}, u32[]{:S(2)}) %collective-permute-start.42) | collective-permute-done | bytes 426016 | tf_op jit(solution)/shard_map/ppermute | solution.py:714
  273.9 7.5 %collective-permute-done.48 = bf16[832,256]{1,0:T(8,128)(2,1)S(1)} collective-permute-done((bf16[832,256]{1,0:T(8,128)(2,1)S(1)}, bf16[832,256]{1,0:T(8,128)(2,1)S(1)}, u32[]{:S(2)}, u32[]{:S(2)}) %collective-permute-start.48) | collective-permute-done | bytes 426016 | tf_op jit(solution)/shard_map/ppermute | solution.py:714
  281.3 7.9 %collective-permute-done.46 = bf16[832,256]{1,0:T(8,128)(2,1)S(1)} collective-permute-done((bf16[832,256]{1,0:T(8,128)(2,1)S(1)}, bf16[832,256]{1,0:T(8,128)(2,1)S(1)}, u32[]{:S(2)}, u32[]{:S(2)}) %collective-permute-start.46) | collective-permute-done | bytes 426016 | tf_op jit(solution)/shard_map/ppermute | solution.py:714
  294.1 6.1 %collective-permute-done.52.refs_5_ = bf16[832,256]{1,0:T(8,128)(2,1)S(1)} collective-permute-done((bf16[832,256]{1,0:T(8,128)(2,1)S(1)}, bf16[832,256]{1,0:T(8,128)(2,1)S(1)}, u32[]{:S(2)}, u32[]{:S(2)}) %collective-permute-start.52) | collective-permute-done | bytes 426016 | tf_op jit(solution)/shard_map/ppermute | solution.py:714
  300.1 9.6 %collective-permute-done.50.refs_4_ = bf16[832,256]{1,0:T(8,128)(2,1)S(1)} collective-permute-done((bf16[832,256]{1,0:T(8,128)(2,1)S(1)}, bf16[832,256]{1,0:T(8,128)(2,1)S(1)}, u32[]{:S(2)}, u32[]{:S(2)}) %collective-permute-start.50) | collective-permute-done | bytes 426016 | tf_op jit(solution)/shard_map/ppermute | solution.py:714
  314.2 12.5 %collective-permute-done.56.refs_1_ = bf16[832,256]{1,0:T(8,128)(2,1)S(1)} collective-permute-done((bf16[832,256]{1,0:T(8,128)(2,1)S(1)}, bf16[832,256]{1,0:T(8,128)(2,1)S(1)}, u32[]{:S(2)}, u32[]{:S(2)}) %collective-permute-start.56) | collective-permute-done | bytes 426016 | tf_op jit(solution)/shard_map/ppermute | solution.py:714
  340.4 10.2 %collective-permute-done.57.refs_2_.refs_0_ = bf16[928,256]{1,0:T(8,128)(2,1)S(1)} collective-permute-done((bf16[928,256]{1,0:T(8,128)(2,1)S(1)}, bf16[928,256]{1,0:T(8,128)(2,1)S(1)}, u32[]{:S(2)}, u32[]{:S(2)}) %collective-permute-start.57) | collective-permute-done | bytes 475168 | tf_op jit(solution)/shard_map/ppermute | solution.py:714
  365.6 5.3 %collective-permute-done.62.refs_0_ = bf16[832,256]{1,0:T(8,128)(2,1)S(1)} collective-permute-done((bf16[832,256]{1,0:T(8,128)(2,1)S(1)}, bf16[832,256]{1,0:T(8,128)(2,1)S(1)}, u32[]{:S(2)}, u32[]{:S(2)}) %collective-permute-start.62) | collective-permute-done | bytes 426016 | tf_op jit(solution)/shard_map/ppermute | solution.py:714
  384.0 4.9 %unpack.11 = (f32[1536,768]{1,0:T(8,128)}, f32[768,1536]{1,0:T(8,128)}, f32[1024,512]{1,0:T(8,128)}, f32[512,1024]{1,0:T(8,128)}, f32[3,1024,512]{2,1,0:T(8,128)...) custom-call(s32[3]{0:T(128)} %pad_add_fusion.info, ...), custom_call_target="tpu_custom_call", output_to_operand_aliasing={{0}: (9, {}), {1}: (10, {}), {2}: (11, {}), {3}: (12, {}), ... | custom-call | bytes 10665984 | tf_op jit(solution)/shard_map/unpack/pallas_call | solution.py:670
  388.9 5.1 %collective-permute-done.66.refs_2_.refs_0_ = bf16[928,256]{1,0:T(8,128)(2,1)S(1)} collective-permute-done((bf16[928,256]{1,0:T(8,128)(2,1)S(1)}, bf16[928,256]{1,0:T(8,128)(2,1)S(1)}, u32[]{:S(2)}, u32[]{:S(2)}) %collective-permute-start.66) | collective-permute-done | bytes 475168 | tf_op jit(solution)/shard_map/ppermute | solution.py:714
  404.1 11.3 %collective-permute-done.76.refs_1_ = bf16[832,256]{1,0:T(8,128)(2,1)S(1)} collective-permute-done((bf16[832,256]{1,0:T(8,128)(2,1)S(1)}, bf16[832,256]{1,0:T(8,128)(2,1)S(1)}, u32[]{:S(2)}, u32[]{:S(2)}) %collective-permute-start.76) | collective-permute-done | bytes 426016 | tf_op jit(solution)/shard_map/ppermute | solution.py:714
  429.6 5.2 %collective-permute-done.77.refs_2_.refs_0_ = bf16[928,256]{1,0:T(8,128)(2,1)} collective-permute-done((bf16[928,256]{1,0:T(8,128)(2,1)S(1)}, bf16[928,256]{1,0:T(8,128)(2,1)}, u32[]{:S(2)}, u32[]{:S(2)}) %collective-permute-start.77) | collective-permute-done | bytes 475168 | tf_op jit(solution)/shard_map/ppermute | solution.py:714
  (425 shorter events, 176.6 us)
Async XLA Ops:
  0.7 20.0 %collective-permute-start = (bf16[768,1536]{1,0:T(8,128)(2,1)}, bf16[768,1536]{1,0:T(8,128)(2,1)S(1)}, u32[]{:S(2)}, u32[]{:S(2)}) collective-permute-start(bf16[768,1536]{1,0:T(8,128)(2,1)} %bitcast.57), channel_id=1, source_target_pairs={{0,1},{1,0},{2,3},{3,2},{4,5},{5,4},{6,7},{7,6},{8,9},{9,8},{10,11... | collective-permute-start | bytes 7077896 | tf_op jit(solution)/shard_map/ppermute | solution.py:688
  1.2 19.6 %collective-permute-start.1 = (bf16[1536,768]{1,0:T(8,128)(2,1)}, bf16[1536,768]{1,0:T(8,128)(2,1)}, u32[]{:S(2)}, u32[]{:S(2)}) collective-permute-start(bf16[1536,768]{1,0:T(8,128)(2,1)} %bitcast.61), channel_id=1, source_target_pairs={{0,1},{1,0},{2,3},{3,2},{4,5},{5,4},{6,7},{7,6},{8,9},{9,8},{10,11... | collective-permute-start | bytes 7077896 | tf_op jit(solution)/shard_map/ppermute | solution.py:688
  34.1 22.3 %collective-permute-start.11 = (bf16[3,768,384]{2,1,0:T(8,128)(2,1)}, bf16[3,768,384]{2,1,0:T(8,128)(2,1)}, u32[]{:S(2)}, u32[]{:S(2)}) collective-permute-start(bf16[3,768,384]{2,1,0:T(8,128)(2,1)} %bitcast.106), channel_id=1, source_target_pairs={{0,1},{1,0},{2,3},{3,2},{4,5},{5,4},{6,7},{7,6},{8,9},{9,8},{10,11... | collective-permute-start | bytes 5308424 | tf_op jit(solution)/shard_map/ppermute | solution.py:688
  35.7 20.7 %collective-permute-start.12 = (bf16[384,768]{1,0:T(8,128)(2,1)}, bf16[384,768]{1,0:T(8,128)(2,1)}, u32[]{:S(2)}, u32[]{:S(2)}) collective-permute-start(bf16[384,768]{1,0:T(8,128)(2,1)} %refs_2_.1), channel_id=1, source_target_pairs={{0,1},{1,0},{2,3},{3,2},{4,5},{5,4},{6,7},{7,6},{8,9},{9,8},{10,11... | collective-permute-start | bytes 1769480 | tf_op jit(solution)/shard_map/ppermute | solution.py:688
  54.8 26.8 %collective-permute-start.14 = (bf16[224,1024]{1,0:T(8,128)(2,1)}, bf16[224,1024]{1,0:T(8,128)(2,1)S(1)}, u32[]{:S(2)}, u32[]{:S(2)}) collective-permute-start(bf16[224,1024]{1,0:T(8,128)(2,1)} %get-tuple-element.264), channel_id=1, source_target_pairs={{16,0},{17,1},{18,2},{19,3},{20,4},{21,5},{22,6},{23,7},{24,8},{25... | collective-permute-start | bytes 1376264 | tf_op jit(solution)/shard_map/ppermute | solution.py:696
  56.1 63.0 %collective-permute-start.18 = (bf16[224,4608]{1,0:T(8,128)(2,1)}, bf16[224,4608]{1,0:T(8,128)(2,1)S(1)}, u32[]{:S(2)}, u32[]{:S(2)}) collective-permute-start(bf16[224,4608]{1,0:T(8,128)(2,1)} %get-tuple-element.312), channel_id=1, source_target_pairs={{0,1},{1,0},{2,3},{3,2},{4,5},{5,4},{6,7},{7,6},{8,9},{9,8},{10,11... | collective-permute-start | bytes 6193160 | tf_op jit(solution)/shard_map/ppermute | solution.py:688
  62.4 56.6 %collective-permute-start.15 = (bf16[192,5120]{1,0:T(8,128)(2,1)}, bf16[192,5120]{1,0:T(8,128)(2,1)}, u32[]{:S(2)}, u32[]{:S(2)}) collective-permute-start(bf16[192,5120]{1,0:T(8,128)(2,1)} %get-tuple-element.301), channel_id=1, source_target_pairs={{0,1},{1,0},{2,3},{3,2},{4,5},{5,4},{6,7},{7,6},{8,9},{9,8},{10,11... | collective-permute-start | bytes 5898248 | tf_op jit(solution)/shard_map/ppermute | solution.py:688
  62.8 39.1 %collective-permute-start.13 = (bf16[192,768]{1,0:T(8,128)(2,1)}, bf16[192,768]{1,0:T(8,128)(2,1)S(1)}, u32[]{:S(2)}, u32[]{:S(2)}) collective-permute-start(bf16[192,768]{1,0:T(8,128)(2,1)} %get-tuple-element.271), channel_id=1, source_target_pairs={{16,0},{17,1},{18,2},{19,3},{20,4},{21,5},{22,6},{23,7},{24,8},{25... | collective-permute-start | bytes 884744 | tf_op jit(solution)/shard_map/ppermute | solution.py:696
  165.5 21.6 %collective-permute-start.26 = (bf16[928,256]{1,0:T(8,128)(2,1)S(1)}, bf16[928,256]{1,0:T(8,128)(2,1)S(1)}, u32[]{:S(2)}, u32[]{:S(2)}) collective-permute-start(bf16[928,256]{1,0:T(8,128)(2,1)S(1)} %copy-done.93), channel_id=1, source_target_pairs={{0,4},{4,8},{8,12},{12,14},{14,10},{10,6},{6,2},{2,0},{1,5},{5,9},... | collective-permute-start | bytes 1425416 | tf_op jit(solution)/shard_map/ppermute | solution.py:714
  167.5 22.2 %collective-permute-start.31 = (bf16[880,256]{1,0:T(8,128)(2,1)}, bf16[880,256]{1,0:T(8,128)(2,1)S(1)}, u32[]{:S(2)}, u32[]{:S(2)}) collective-permute-start(bf16[880,256]{1,0:T(8,128)(2,1)} %get-tuple-element.355), channel_id=1, source_target_pairs={{4,0},{8,4},{12,8},{14,12},{10,14},{6,10},{2,6},{0,2},{5,1},{9,5},... | collective-permute-start | bytes 1351688 | tf_op jit(solution)/shard_map/ppermute | solution.py:714
  187.3 21.2 %collective-permute-start.29 = (bf16[928,256]{1,0:T(8,128)(2,1)S(1)}, bf16[928,256]{1,0:T(8,128)(2,1)S(1)}, u32[]{:S(2)}, u32[]{:S(2)}) collective-permute-start(bf16[928,256]{1,0:T(8,128)(2,1)S(1)} %add.124), channel_id=1, source_target_pairs={{0,4},{4,8},{8,12},{12,14},{14,10},{10,6},{6,2},{2,0},{1,5},{5,9},... | collective-permute-start | bytes 1425416 | tf_op jit(solution)/shard_map/ppermute | solution.py:714
  189.8 21.6 %collective-permute-start.35 = (bf16[880,256]{1,0:T(8,128)(2,1)S(1)}, bf16[880,256]{1,0:T(8,128)(2,1)S(1)}, u32[]{:S(2)}, u32[]{:S(2)}) collective-permute-start(bf16[880,256]{1,0:T(8,128)(2,1)S(1)} %add.125), channel_id=1, source_target_pairs={{4,0},{8,4},{12,8},{14,12},{10,14},{6,10},{2,6},{0,2},{5,1},{9,5},... | collective-permute-start | bytes 1351688 | tf_op jit(solution)/shard_map/ppermute | solution.py:714
  208.6 20.4 %collective-permute-start.33 = (bf16[928,256]{1,0:T(8,128)(2,1)S(1)}, bf16[928,256]{1,0:T(8,128)(2,1)S(1)}, u32[]{:S(2)}, u32[]{:S(2)}) collective-permute-start(bf16[928,256]{1,0:T(8,128)(2,1)S(1)} %add.128), channel_id=1, source_target_pairs={{0,4},{4,8},{8,12},{12,14},{14,10},{10,6},{6,2},{2,0},{1,5},{5,9},... | collective-permute-start | bytes 1425416 | tf_op jit(solution)/shard_map/ppermute | solution.py:714
  211.6 20.5 %collective-permute-start.39 = (bf16[880,256]{1,0:T(8,128)(2,1)S(1)}, bf16[880,256]{1,0:T(8,128)(2,1)S(1)}, u32[]{:S(2)}, u32[]{:S(2)}) collective-permute-start(bf16[880,256]{1,0:T(8,128)(2,1)S(1)} %add.129), channel_id=1, source_target_pairs={{4,0},{8,4},{12,8},{14,12},{10,14},{6,10},{2,6},{0,2},{5,1},{9,5},... | collective-permute-start | bytes 1351688 | tf_op jit(solution)/shard_map/ppermute | solution.py:714
  229.3 20.0 %collective-permute-start.37 = (bf16[928,256]{1,0:T(8,128)(2,1)S(1)}, bf16[928,256]{1,0:T(8,128)(2,1)S(1)}, u32[]{:S(2)}, u32[]{:S(2)}) collective-permute-start(bf16[928,256]{1,0:T(8,128)(2,1)S(1)} %add.132), channel_id=1, source_target_pairs={{0,4},{4,8},{8,12},{12,14},{14,10},{10,6},{6,2},{2,0},{1,5},{5,9},... | collective-permute-start | bytes 1425416 | tf_op jit(solution)/shard_map/ppermute | solution.py:714
  232.3 20.0 %collective-permute-start.43 = (bf16[880,256]{1,0:T(8,128)(2,1)S(1)}, bf16[880,256]{1,0:T(8,128)(2,1)S(1)}, u32[]{:S(2)}, u32[]{:S(2)}) collective-permute-start(bf16[880,256]{1,0:T(8,128)(2,1)S(1)} %add.133), channel_id=1, source_target_pairs={{4,0},{8,4},{12,8},{14,12},{10,14},{6,10},{2,6},{0,2},{5,1},{9,5},... | collective-permute-start | bytes 1351688 | tf_op jit(solution)/shard_map/ppermute | solution.py:714
  249.4 20.0 %collective-permute-start.41 = (bf16[928,256]{1,0:T(8,128)(2,1)S(1)}, bf16[928,256]{1,0:T(8,128)(2,1)S(1)}, u32[]{:S(2)}, u32[]{:S(2)}) collective-permute-start(bf16[928,256]{1,0:T(8,128)(2,1)S(1)} %add.136), channel_id=1, source_target_pairs={{0,4},{4,8},{8,12},{12,14},{14,10},{10,6},{6,2},{2,0},{1,5},{5,9},... | collective-permute-start | bytes 1425416 | tf_op jit(solution)/shard_map/ppermute | solution.py:714
  252.4 20.0 %collective-permute-start.47 = (bf16[880,256]{1,0:T(8,128)(2,1)S(1)}, bf16[880,256]{1,0:T(8,128)(2,1)S(1)}, u32[]{:S(2)}, u32[]{:S(2)}) collective-permute-start(bf16[880,256]{1,0:T(8,128)(2,1)S(1)} %add.137), channel_id=1, source_target_pairs={{4,0},{8,4},{12,8},{14,12},{10,14},{6,10},{2,6},{0,2},{5,1},{9,5},... | collective-permute-start | bytes 1351688 | tf_op jit(solution)/shard_map/ppermute | solution.py:714
  269.6 20.0 %collective-permute-start.45 = (bf16[928,256]{1,0:T(8,128)(2,1)S(1)}, bf16[928,256]{1,0:T(8,128)(2,1)S(1)}, u32[]{:S(2)}, u32[]{:S(2)}) collective-permute-start(bf16[928,256]{1,0:T(8,128)(2,1)S(1)} %add.140), channel_id=1, source_target_pairs={{0,4},{4,8},{8,12},{12,14},{14,10},{10,6},{6,2},{2,0},{1,5},{5,9},... | collective-permute-start | bytes 1425416 | tf_op jit(solution)/shard_map/ppermute | solution.py:714
  289.7 20.0 %collective-permute-start.49 = (bf16[928,256]{1,0:T(8,128)(2,1)S(1)}, bf16[928,256]{1,0:T(8,128)(2,1)S(1)}, u32[]{:S(2)}, u32[]{:S(2)}) collective-permute-start(bf16[928,256]{1,0:T(8,128)(2,1)S(1)} %add.144), channel_id=1, source_target_pairs={{0,4},{4,8},{8,12},{12,14},{14,10},{10,6},{6,2},{2,0},{1,5},{5,9},... | collective-permute-start | bytes 1425416 | tf_op jit(solution)/shard_map/ppermute | solution.py:714
  309.9 22.6 %collective-permute-start.53 = (bf16[928,256]{1,0:T(8,128)(2,1)S(1)}, bf16[928,256]{1,0:T(8,128)(2,1)S(1)}, u32[]{:S(2)}, u32[]{:S(2)}) collective-permute-start(bf16[928,256]{1,0:T(8,128)(2,1)S(1)} %add.146.refs_2_.refs_0_), channel_id=1, source_target_pairs={{0,4},{4,8},{8,12},{12,14},{14,10},{10,6},{6,2},{2,0},{1,5},{5,9},... | collective-permute-start | bytes 1425416 | tf_op jit(solution)/shard_map/ppermute | solution.py:714
  310.9 20.0 %collective-permute-start.59 = (bf16[880,256]{1,0:T(8,128)(2,1)S(1)}, bf16[880,256]{1,0:T(8,128)(2,1)S(1)}, u32[]{:S(2)}, u32[]{:S(2)}) collective-permute-start(bf16[880,256]{1,0:T(8,128)(2,1)S(1)} %add.147.refs_3_.refs_1_), channel_id=1, source_target_pairs={{4,0},{8,4},{12,8},{14,12},{10,14},{6,10},{2,6},{0,2},{5,1},{9,5},... | collective-permute-start | bytes 1351688 | tf_op jit(solution)/shard_map/ppermute | solution.py:714
  330.9 21.9 %collective-permute-start.63 = (bf16[880,256]{1,0:T(8,128)(2,1)S(1)}, bf16[880,256]{1,0:T(8,128)(2,1)S(1)}, u32[]{:S(2)}, u32[]{:S(2)}) collective-permute-start(bf16[880,256]{1,0:T(8,128)(2,1)S(1)} %collective-permute-done.59.refs_7_.refs_3_), channel_id=1, source_target_pairs={{4,0},{8,4},{12,8},{14,12},{10,14},{6,10},{2,6},{0,2},{5,1},{9,5},... | collective-permute-start | bytes 1351688 | tf_op jit(solution)/shard_map/ppermute | solution.py:714
  333.1 21.7 %collective-permute-start.64 = (bf16[1536,256]{1,0:T(8,128)(2,1)S(1)}, bf16[1536,256]{1,0:T(8,128)(2,1)S(1)}, u32[]{:S(2)}, u32[]{:S(2)}) collective-permute-start(bf16[1536,256]{1,0:T(8,128)(2,1)S(1)} %pad_maximum_fusion), channel_id=1, source_target_pairs={{0,16},{16,0},{1,17},{17,1},{2,18},{18,2},{3,19},{19,3},{4,20},{20... | collective-permute-start | bytes 2359304 | tf_op jit(solution)/shard_map/ppermute | solution.py:692
  350.6 23.9 %collective-permute-start.61 = (bf16[928,256]{1,0:T(8,128)(2,1)S(1)}, bf16[928,256]{1,0:T(8,128)(2,1)S(1)}, u32[]{:S(2)}, u32[]{:S(2)}) collective-permute-start(bf16[928,256]{1,0:T(8,128)(2,1)S(1)} %collective-permute-done.57.refs_2_.refs_0_), channel_id=1, source_target_pairs={{0,4},{4,8},{8,12},{12,14},{14,10},{10,6},{6,2},{2,0},{1,5},{5,9},... | collective-permute-start | bytes 1425416 | tf_op jit(solution)/shard_map/ppermute | solution.py:714
  352.8 20.2 %collective-permute-start.68 = (bf16[880,256]{1,0:T(8,128)(2,1)S(1)}, bf16[880,256]{1,0:T(8,128)(2,1)S(1)}, u32[]{:S(2)}, u32[]{:S(2)}) collective-permute-start(bf16[880,256]{1,0:T(8,128)(2,1)S(1)} %collective-permute-done.63.refs_3_.refs_1_), channel_id=1, source_target_pairs={{4,0},{8,4},{12,8},{14,12},{10,14},{6,10},{2,6},{0,2},{5,1},{9,5},... | collective-permute-start | bytes 1351688 | tf_op jit(solution)/shard_map/ppermute | solution.py:714
  373.0 21.1 %collective-permute-start.72 = (bf16[880,256]{1,0:T(8,128)(2,1)S(1)}, bf16[880,256]{1,0:T(8,128)(2,1)S(1)}, u32[]{:S(2)}, u32[]{:S(2)}) collective-permute-start(bf16[880,256]{1,0:T(8,128)(2,1)S(1)} %collective-permute-done.68.refs_7_.refs_3_), channel_id=1, source_target_pairs={{4,0},{8,4},{12,8},{14,12},{10,14},{6,10},{2,6},{0,2},{5,1},{9,5},... | collective-permute-start | bytes 1351688 | tf_op jit(solution)/shard_map/ppermute | solution.py:714
  375.3 23.9 %collective-permute-start.75 = (bf16[1536,256]{1,0:T(8,128)(2,1)S(1)}, bf16[1536,256]{1,0:T(8,128)(2,1)S(1)}, u32[]{:S(2)}, u32[]{:S(2)}) collective-permute-start(bf16[1536,256]{1,0:T(8,128)(2,1)S(1)} %pad_maximum_fusion.1), channel_id=1, source_target_pairs={{0,16},{16,0},{1,17},{17,1},{2,18},{18,2},{3,19},{19,3},{4,20},{20... | collective-permute-start | bytes 2359304 | tf_op jit(solution)/shard_map/ppermute | solution.py:692
  378.0 20.9 %collective-permute-start.73 = (bf16[416,256]{1,0:T(8,128)(2,1)S(1)}, bf16[416,256]{1,0:T(8,128)(2,1)S(1)}, u32[]{:S(2)}, u32[]{:S(2)}) collective-permute-start(bf16[416,256]{1,0:T(8,128)(2,1)S(1)} %slice.66), channel_id=1, source_target_pairs={{4,0},{8,4},{12,8},{14,12},{10,14},{6,10},{2,6},{0,2},{5,1},{9,5},... | collective-permute-start | bytes 638984 | tf_op jit(solution)/shard_map/ppermute | solution.py:714
  394.1 26.1 %collective-permute-start.70 = (bf16[928,256]{1,0:T(8,128)(2,1)S(1)}, bf16[928,256]{1,0:T(8,128)(2,1)S(1)}, u32[]{:S(2)}, u32[]{:S(2)}) collective-permute-start(bf16[928,256]{1,0:T(8,128)(2,1)S(1)} %collective-permute-done.66.refs_2_.refs_0_), channel_id=1, source_target_pairs={{0,4},{4,8},{8,12},{12,14},{14,10},{10,6},{6,2},{2,0},{1,5},{5,9},... | collective-permute-start | bytes 1425416 | tf_op jit(solution)/shard_map/ppermute | solution.py:714
  394.1 23.8 %collective-permute-start.79 = (bf16[880,256]{1,0:T(8,128)(2,1)S(1)}, bf16[880,256]{1,0:T(8,128)(2,1)S(1)}, u32[]{:S(2)}, u32[]{:S(2)}) collective-permute-start(bf16[880,256]{1,0:T(8,128)(2,1)S(1)} %collective-permute-done.72.refs_3_.refs_1_), channel_id=1, source_target_pairs={{4,0},{8,4},{12,8},{14,12},{10,14},{6,10},{2,6},{0,2},{5,1},{9,5},... | collective-permute-start | bytes 1351688 | tf_op jit(solution)/shard_map/ppermute | solution.py:714
  420.4 23.0 %collective-permute-start.85 = (bf16[1536,256]{1,0:T(8,128)(2,1)S(1)}, bf16[1536,256]{1,0:T(8,128)(2,1)S(1)}, u32[]{:S(2)}, u32[]{:S(2)}) collective-permute-start(bf16[1536,256]{1,0:T(8,128)(2,1)S(1)} %pad_maximum_fusion.2), channel_id=1, source_target_pairs={{0,16},{16,0},{1,17},{17,1},{2,18},{18,2},{3,19},{19,3},{4,20},{20... | collective-permute-start | bytes 2359304 | tf_op jit(solution)/shard_map/ppermute | solution.py:692
  (148 other events, 1862.0 us)

commit v3 on v2

--- a/solution.py
+++ b/solution.py
@@ -154,7 +154,7 @@
         copy.wait()
 
 
-def tail_forward(residual, contexts, out_w, gain, shift, up_w, down_w, kept, mixed):
+def tail_forward(residual, contexts, out_w, gain, shift, up_w, down_w, kept, mixed, leave=None):
     normed_ref, hidden, slopes, unit1, inv1, unit2, inv2 = kept
     branch = times(contexts[0], out_w[0].get()[...]) + times(contexts[1], out_w[1].get()[...])
     unit, inverse = norm_rows(residual.astype(FULL) + branch)
@@ -163,6 +163,8 @@
     normed = unit * gain[0:1, :] + shift[0:1, :]
     normed_ref[...] = normed.astype(LOW)
     mixed[...] = normed
+    if leave is not None:
+        leave.go(normed_ref, unit1, inv1)
     for half in range(2):
         up, down = up_w[half].get(), down_w[half].get()
         for start in range(0, up.shape[1], TILE):
@@ -171,13 +173,15 @@
             hidden[half][:, span] = value.astype(LOW)
             slopes[half][:, span] = slope
             mixed[...] += times(hidden[half][:, span], down[span, :])
+        if leave is not None:
+            leave.go(hidden[half], slopes[half])
     unit, inverse = norm_rows(mixed[...])
     unit2[...] = unit
     inv2[...] = wide(inverse)
     return unit * gain[1:2, :] + shift[1:2, :]
 
 
-def tail_backward(seed, kept, out_w, gain, up_w, down_w, grads, total):
+def tail_backward(seed, kept, out_w, gain, up_w, down_w, grads, total, leave=None):
     slopes, unit1, inv1, unit2, inv2 = kept
     df, du, da, dgain, dshift = grads
     dsecond, dgain1, dshift1 = norm_back(
@@ -199,6 +203,8 @@
     dshift[...] = jnp.concatenate([dshift0, dshift1], axis=0)
     total[...] = dfirst
     da[...] = dfirst.astype(LOW)
+    if leave is not None:
+        leave.go(df, du[0], da, total)
     return [times_back(da[...], w.get()[...]).astype(LOW) for w in out_w]
 
 
@@ -206,19 +212,44 @@
     return jax.ShapeDtypeStruct((rows, columns), kind)
 
 
+class Leave:
+    def __init__(self, buffers, targets, signals):
+        self.buffers, self.targets, self.signals = buffers, targets, signals
+        self.begun = {}
+
+    def go(self, *buffers):
+        for buffer in buffers:
+            number = [one is buffer for one in self.buffers].index(True)
+            copy = pltpu.make_async_copy(buffer, self.targets[number], self.signals.at[number])
+            copy.start()
+            self.begun[number] = copy
+
+    def finish(self):
+        self.go(*[one for number, one in enumerate(self.buffers) if number not in self.begun])
+        for copy in self.begun.values():
+            copy.wait()
+        self.begun = {}
+
+
 def launch(body, outputs, args, far=(), scratch=(), flag=None, work=0, name=None):
-    whole = pl.BlockSpec(memory_space=pltpu.VMEM)
+    whole, anywhere = pl.BlockSpec(memory_space=pltpu.VMEM), pl.BlockSpec(memory_space=pl.ANY)
     moved = sum(
         math.prod(v.shape) * v.dtype.itemsize for v in tuple(args) + tuple(far) + tuple(outputs)
     )
-    specs = [pl.BlockSpec(memory_space=pltpu.SMEM)] + [whole] * len(args)
-    specs += [pl.BlockSpec(memory_space=pl.ANY)] * len(far)
+    total, results = len(args) + len(far), len(outputs)
+
+    def whole_body(info, *refs):
+        targets, refs = refs[total : total + results], refs[:total] + refs[total + results :]
+        outs, signals = refs[total : total + results], refs[total + results]
+        body(Leave(outs, targets, signals), info, *refs[:total], *outs, *refs[total + results + 1 :])
+
+    own = [pltpu.VMEM(v.shape, v.dtype) for v in outputs] + [pltpu.SemaphoreType.DMA((results,))]
     return pl.pallas_call(
-        body,
+        whole_body,
         out_shape=tuple(outputs),
-        in_specs=specs,
-        out_specs=tuple([whole] * len(outputs)),
-        scratch_shapes=list(scratch),
+        in_specs=[pl.BlockSpec(memory_space=pltpu.SMEM)] + [whole] * len(args) + [anywhere] * len(far),
+        out_specs=tuple([anywhere] * results),
+        scratch_shapes=own + list(scratch),
         compiler_params=pltpu.CompilerParams(vmem_limit_bytes=ROOM),
         cost_estimate=pl.CostEstimate(flops=work, bytes_accessed=moved, transcendentals=0),
         name=name,
@@ -238,7 +269,7 @@
 
 
 def cross_forward(
-    pairs, rows_t, rows_i, real_t, info, x_t, x_i, keep, far_t, far_i,
+    pairs, rows_t, rows_i, real_t, leave, info, x_t, x_i, keep, far_t, far_i,
     xt_own, xt_other, xi_own, xi_other, tp, ip, ct_own, ct_other, ci_own, ci_other, xt, xi, wt, wi, signals,
 ):
     half = pairs // 2
@@ -251,13 +282,19 @@
         (xt_own, xt_other)[place // half][inside * rows_t : (inside + 1) * rows_t, :] = text
         (xi_own, xi_other)[place // half][inside * rows_i : (inside + 1) * rows_i, :] = image
 
+    @pl.when(info[0] == 0)
+    def idle():
+        leave.finish()
+
     @pl.when(info[0] == 1)
     def work():
         width = ct_own.shape[1]
         weights = fetch((far_t, far_i), (wt, wi), signals)
+        leave.go(xt_own, xt_other, xi_own, xi_other)
         for late, x, p in ((weights[0], xt, tp), (weights[1], xi, ip)):
             for slot in range(3):
                 p[:, pl.ds(slot * width, width)] = times(x[...], late.get()[slot]).astype(LOW)
+            leave.go(p)
         text_keys = lax.broadcasted_iota(jnp.int32, (1, rows_t), 1) < real_t
         slabs = width // 128
 
@@ -277,11 +314,12 @@
                     ci[at_i, slab(n)] = image
             return carry
 
-        lax.fori_loop(0, half, each, 0)
+        lax.fori_loop(0, half, each, 0, unroll=True)
+        leave.finish()
 
 
 def first_tail(
-    info, x, c0, c1, gain, shift, *refs
+    leave, info, x, c0, c1, gain, shift, *refs
 ):
     far, refs = refs[:6], refs[6:]
     out, y, h0, h1, s0, s1, n1, i1, n2, i2, mixed = refs[:11]
@@ -292,12 +330,13 @@
         o0, o1, u0, d0, u1, d1 = fetch(far, near, signals)
         kept = (y, (h0, h1), (s0, s1), n1, i1, n2, i2)
         out[...] = tail_forward(
-            x[...], (c0[...], c1[...]), (o0, o1), gain, shift, (u0, u1), (d0, d1), kept, mixed
+            x[...], (c0[...], c1[...]), (o0, o1), gain, shift, (u0, u1), (d0, d1), kept, mixed, leave
         ).astype(LOW)
+        leave.finish()
 
 
 def self_layer(
-    masked, half, rows, real, size, stride, info, x, seed, gain, shift, keep, *refs
+    masked, half, rows, real, size, stride, leave, info, x, seed, gain, shift, keep, *refs
 ):
     far, refs = refs[:12], refs[12:]
     (out, dx, c0, p0, da, df, du0, du1, y, h0, dgain, dshift, give) = refs[:13]
@@ -313,6 +352,10 @@
     def pass_on():
         targets = (y, h0, c0, give.at[:, spans[0]], give.at[:, spans[1]])
         pass_through((far[8], far[9], far[11], far[8], far[10]), targets, signals)
+        leave.go(y, h0, c0, give)
+        for copy in leave.begun.values():
+            copy.wait()
+        leave.begun = {}
 
     @pl.when(info[0] == 0)
     def work():
@@ -348,12 +391,14 @@
                 (c0, c1)[n // slabs][at, slab(n % slabs)] = value
             return carry
 
-        lax.fori_loop(0, half, forward, 0)
+        lax.fori_loop(0, half, forward, 0, unroll=True)
+        leave.go(c0)
         used = pl.ds(0, width)
         kept = (y, (h0, h1), (s0, s1), n1, i1, n2, i2)
         out[...] = tail_forward(
             x[...], (c0[:, used], c1[:, used]), (o0, o1), gain, shift, (u0, u1), (d0, d1), kept, mixed
         ).astype(LOW)
+        leave.go(out, y, h0)
         held = ((Here(s0), Here(s1)), Here(n1), Here(i1), Here(n2), Here(i2))
         dcs = tail_backward(
             seed[...].astype(FULL),
@@ -365,6 +410,7 @@
             (df, (du0, du1), da, dgain, dshift),
             mixed,
         )
+        leave.go(da, df, du0, du1, dgain, dshift)
         dc0[...] = dcs[0]
         dc1[...] = dcs[1]
 
@@ -383,16 +429,18 @@
                     (p0, p1)[n // slabs][at, pl.ds(column, 128)] = grads[slot]
             return carry
 
-        lax.fori_loop(0, half, backward, 0)
+        lax.fori_loop(0, half, backward, 0, unroll=True)
+        for span, value in zip(spans, (y, h1, c1, p1, x)):
+            give[:, span] = value[...]
+        leave.go(p0, give)
         for w, p in ((w0, p0), (w1, p1)):
             for slot in range(3):
                 mixed[...] += times_back(p[:, pl.ds(slot * stride, width)], w.get()[slot])
         dx[...] = mixed[...].astype(LOW)
-        for span, value in zip(spans, (y, h1, c1, p1, x)):
-            give[:, span] = value[...]
-
-
-def first_tail_back(info, seed, gain, *refs):
+        leave.finish()
+
+
+def first_tail_back(leave, info, seed, gain, *refs):
     far, refs = refs[:18], refs[18:]
     df, du0, da, dgain, dshift, dres, dc0, give = refs[:8]
     du1, near, signals = refs[8], refs[9:21], refs[21]
@@ -408,6 +456,7 @@
             (df, du0, da, dgain, dshift) + tuple(give.at[:, span] for span in spans[:3]),
             signals,
         )
+        leave.finish()
 
     @pl.when(info[0] == 1)
     def work():
@@ -421,14 +470,16 @@
             (d0, d1),
             (df, (du0, du1), da, dgain, dshift),
             dres,
+            leave,
         )
         dc0[...] = dcs[0]
         for span, value in zip(spans, (df[...], du1[...], da[...], dcs[1])):
             give[:, span] = value
+        leave.finish()
 
 
 def cross_backward(
-    wides, pairs, rows_t, rows_i, real_t, info,
+    wides, pairs, rows_t, rows_i, real_t, leave, info,
     tp, ip, dct_own, dci_own, keep, *refs
 ):
     far, refs = refs[:8], refs[8:]
@@ -445,6 +496,7 @@
             start = got.shape[1] - wides[len(sources) // 2] - mine.shape[1]
             sources += [mine, got.at[:, pl.ds(start, mine.shape[1])]]
         pass_through(sources, (dtp_own, dtp_other, dip_own, dip_other), signals)
+        leave.finish()
 
     @pl.when(info[0] == 1)
     def work():
@@ -477,7 +529,8 @@
                     dip[at_i, first], dtp[at_t, second], dtp[at_t, third] = image
             return carry
 
-        lax.fori_loop(0, half, each, 0)
+        lax.fori_loop(0, half, each, 0, unroll=True)
+        leave.go(dtp_own, dtp_other, dip_own, dip_other)
         for late, triples in (
             (weights[0], ((dtp_own, dxt_own), (dtp_other, dxt_other))),
             (weights[1], ((dip_own, dxi_own), (dip_other, dxi_other))),
@@ -487,6 +540,8 @@
                 for slot in range(1, 3):
                     total += times_back(dp[:, pl.ds(slot * width, width)], late.get()[slot])
                 dx[...] = total
+                leave.go(dx)
+        leave.finish()
 
 
 def round_up(value, step):
@@ -494,7 +549,7 @@
 
 
 class Layout:
-    def __init__(self, blocks, weights):
+    def __init__(self, blocks, weights, firsts=None):
         self.blocks, self.weights = blocks, weights
         self.sizes = [0, 0]
         self.units = []
@@ -503,6 +558,8 @@
             real = depth // blocks
             for unit in range(width // UNIT):
                 way = 0 if self.sizes[0] <= self.sizes[1] else 1
+                if firsts:
+                    way = 0 if unit < firsts[name] else 1
                 self.units.append((index, unit, way, self.sizes[way], real))
                 self.sizes[way] += round_up(real, 16)
             self.after[name] = list(self.sizes)
@@ -917,6 +974,7 @@
             ("up_i", wide_i, ff_i),
             ("down_i", ff_i, wide_i),
         ],
+        {"down_t": 1, "up_t": 3, "up_i": 2, "down_i": 1},
     )
     attn_layout = Layout(
         blocks,

time: 468 us -> 455 us (0.972)
  Pallas kernels: 131 us -> 123 us
    pallas_call x8, Pallas kernels: 74.9 us -> 66.7 us  [launch(): pl.pallas_call(whole_body, out_shape=tuple(outputs), in_specs=[pl.BlockSp...]
  transfers between devices with their start and end apart: 86 -> 86, of which waited for: 38 -> 32; matrix products, arithmetic and copies ran while one was open for 4% -> 4% of each run, Pallas kernels for 22% -> 21%
where the time goes in v3:
time: 455 us; the launch traced here: 447 us
  waiting for transfers between devices  218 us (48%)
  Pallas kernels  123 us (27%)
  starting transfers between devices  73.4 us (16%)
  local copies, waits for them, and re-layouts  22 us (5%)
  other arithmetic  9.04 us (2%)
    ppermute x58, waiting for transfers between devices, to_next(): return lax.ppermute(values, 'dp', route)  179 us
    pallas_call x8, Pallas kernels, launch(): pl.pallas_call(whole_body, out_shape=tuple(outputs), in_specs=[pl.BlockSp...  66.7 us
    ppermute x58, starting transfers between devices, to_next(): return lax.ppermute(values, 'dp', route)  62.2 us
    pallas_call x9, Pallas kernels, unpack(): pl.pallas_call(functools.partial(unpack_body, moves, rows, blocks, len(fo...  37 us
    ppermute x4, waiting for transfers between devices, to_layer(): return lax.ppermute(values, 'section', [(1 - layer, layer)])  28.5 us
    pallas_call x2, Pallas kernels, pack(): pl.pallas_call(functools.partial(pack_body, layout, chosen, kinds, len(fo...  19.1 us
    unnamed x196, local copies, waits for them, and re-layouts  14.9 us
    ppermute x20, waiting for transfers between devices, to_other_core(): return lax.ppermute(values, 'tensor', CORES)  10.6 us
  transfers between devices with their start and end apart: 86, of which 32 were waited for; matrix products, arithmetic and copies ran while one was open for 4% of the time, Pallas kernels for 21%

profile of v3, /device:TPU:0, one launch (start us, length us, event | category | flops | bytes accessed | tf_op | source)
XLA Modules:
  0.0 447.4 jit_solution(11364065912814898693)
XLA Ops:
  6.9 10.4 %cross_forward.1 = (bf16[192,768]{1,0:T(8,128)(2,1)}, bf16[192,768]{1,0:T(8,128)(2,1)}, bf16[224,1024]{1,0:T(8,128)(2,1)}, bf16[224,1024]{1,0:T(8,128)(2,1)}, bf...) custom-call(s32[3]{0:T(128)} %pad_add_fusion.info, ...), custom_call_target="tpu_custom_call" | custom-call | flops 2315255808 | bytes 11929344 | tf_op jit(solution)/shard_map/cross_forward/pallas_call | solution.py:247
  24.6 7.2 %tail_i.1 = (bf16[224,1024]{1,0:T(8,128)(2,1)}, bf16[224,1024]{1,0:T(8,128)(2,1)}, bf16[224,512]{1,0:T(8,128)(2,1)}, bf16[224,512]{1,0:T(8,128)(2,1)}, f32[224,5...) custom-call(s32[3]{0:T(128)} %pad_add_fusion.info, ...), custom_call_target="tpu_custom_call" | custom-call | flops 1409286144 | bytes 11583488 | tf_op jit(solution)/shard_map/tail_i/pallas_call | solution.py:247
  34.0 9.1 %tail_t.1 = (bf16[192,768]{1,0:T(8,128)(2,1)}, bf16[192,768]{1,0:T(8,128)(2,1)}, bf16[192,1536]{1,0:T(8,128)(2,1)}, bf16[192,1536]{1,0:T(8,128)(2,1)}, f32[192,1...) custom-call(s32[3]{0:T(128)} %pad_add_fusion.info, ...), custom_call_target="tpu_custom_call" | custom-call | flops 2113929216 | bytes 17215488 | tf_op jit(solution)/shard_map/tail_t/pallas_call | solution.py:247
  46.3 4.4 self_i.1
  52.7 4.8 %self_t.1 = (bf16[192,768]{1,0:T(8,128)(2,1)}, bf16[192,768]{1,0:T(8,128)(2,1)}, bf16[192,512]{1,0:T(8,128)(2,1)}, bf16[192,1536]{1,0:T(8,128)(2,1)}, bf16[192,7...) custom-call(s32[3]{0:T(128)} %pad_add_fusion.info, ...), custom_call_target="tpu_custom_call" | custom-call | flops 5435817984 | bytes 22439680 | tf_op jit(solution)/shard_map/self_t/pallas_call | solution.py:247
  59.1 18.5 %collective-permute-done.14.refs_0_ = bf16[224,1024]{1,0:T(8,128)(2,1)S(1)} collective-permute-done((bf16[224,1024]{1,0:T(8,128)(2,1)}, bf16[224,1024]{1,0:T(8,128)(2,1)S(1)}, u32[]{:S(2)}, u32[]{:S(2)}) %collective-permute-start.14) | collective-permute-done | bytes 458784 | tf_op jit(solution)/shard_map/ppermute | solution.py:753
  78.3 7.8 %tail_back_i.1 = (bf16[224,1024]{1,0:T(8,128)(2,1)}, bf16[224,512]{1,0:T(8,128)(2,1)}, bf16[224,1024]{1,0:T(8,128)(2,1)}, f32[2,1024]{1,0:T(2,128)}, f32[2,1024]...) custom-call(s32[3]{0:T(128)} %pad_add_fusion.info, ...), custom_call_target="tpu_custom_call" | custom-call | flops 1409286144 | bytes 14819328 | tf_op jit(solution)/shard_map/tail_back_i/pallas_call | solution.py:247
  86.1 10.0 %collective-permute-done.13.refs_0_ = bf16[192,768]{1,0:T(8,128)(2,1)S(1)} collective-permute-done((bf16[192,768]{1,0:T(8,128)(2,1)}, bf16[192,768]{1,0:T(8,128)(2,1)S(1)}, u32[]{:S(2)}, u32[]{:S(2)}) %collective-permute-start.13) | collective-permute-done | bytes 294944 | tf_op jit(solution)/shard_map/ppermute | solution.py:753
  96.8 10.1 %tail_back_t.1 = (bf16[192,768]{1,0:T(8,128)(2,1)}, bf16[192,1536]{1,0:T(8,128)(2,1)}, bf16[192,768]{1,0:T(8,128)(2,1)}, f32[2,768]{1,0:T(2,128)}, f32[2,768]{1,...) custom-call(s32[3]{0:T(128)} %pad_add_fusion.info, ...), custom_call_target="tpu_custom_call" | custom-call | flops 2113929216 | bytes 20183040 | tf_op jit(solution)/shard_map/tail_back_t/pallas_call | solution.py:247
  114.3 9.4 %pack_ff.1 = (bf16[800,256]{1,0:T(8,128)(2,1)}, bf16[800,256]{1,0:T(8,128)(2,1)}, bf16[800,256]{1,0:T(8,128)(2,1)}, bf16[800,256]{1,0:T(8,128)(2,1)}, bf16[800,2...) custom-call(s32[3]{0:T(128)} %pad_add_fusion.info, ...), custom_call_target="tpu_custom_call" | custom-call | flops 2751463424 | bytes 13631488 | tf_op jit(solution)/shard_map/pack_ff/pallas_call | solution.py:665
  127.1 13.0 %cross_backward.1 = (bf16[192,1536]{1,0:T(8,128)(2,1)}, bf16[192,1536]{1,0:T(8,128)(2,1)}, bf16[224,1536]{1,0:T(8,128)(2,1)}, bf16[224,1536]{1,0:T(8,128)(2,1)},...) custom-call(s32[3]{0:T(128)} %pad_add_fusion.info, ...), custom_call_target="tpu_custom_call" | custom-call | flops 2315255808 | bytes 22120192 | tf_op jit(solution)/shard_map/cross_backward/pallas_call | solution.py:247
  140.4 9.6 %pack_attention.1 = (bf16[928,256]{1,0:T(8,128)(2,1)}, bf16[928,256]{1,0:T(8,128)(2,1)}, bf16[928,256]{1,0:T(8,128)(2,1)}, bf16[928,256]{1,0:T(8,128)(2,1)}, bf1...) custom-call(s32[3]{0:T(128)} %pad_add_fusion.info, ...), custom_call_target="tpu_custom_call" | custom-call | flops 2999975936 | bytes 14811136 | tf_op jit(solution)/shard_map/pack_attention/pallas_call | solution.py:665
  164.0 6.4 %collective-permute-done.28 = bf16[864,256]{1,0:T(8,128)(2,1)S(1)} collective-permute-done((bf16[864,256]{1,0:T(8,128)(2,1)S(1)}, bf16[864,256]{1,0:T(8,128)(2,1)S(1)}, u32[]{:S(2)}, u32[]{:S(2)}) %collective-permute-start.28) | collective-permute-done | bytes 442400 | tf_op jit(solution)/shard_map/ppermute | solution.py:771
  170.7 6.5 %collective-permute-done.26 = bf16[928,256]{1,0:T(8,128)(2,1)S(1)} collective-permute-done((bf16[928,256]{1,0:T(8,128)(2,1)S(1)}, bf16[928,256]{1,0:T(8,128)(2,1)S(1)}, u32[]{:S(2)}, u32[]{:S(2)}) %collective-permute-start.26) | collective-permute-done | bytes 475168 | tf_op jit(solution)/shard_map/ppermute | solution.py:771
  181.7 16.8 %collective-permute-done.30 = bf16[800,256]{1,0:T(8,128)(2,1)S(1)} collective-permute-done((bf16[800,256]{1,0:T(8,128)(2,1)S(1)}, bf16[800,256]{1,0:T(8,128)(2,1)S(1)}, u32[]{:S(2)}, u32[]{:S(2)}) %collective-permute-start.30) | collective-permute-done | bytes 409632 | tf_op jit(solution)/shard_map/ppermute | solution.py:771
  203.4 15.9 %collective-permute-done.34 = bf16[800,256]{1,0:T(8,128)(2,1)S(1)} collective-permute-done((bf16[800,256]{1,0:T(8,128)(2,1)S(1)}, bf16[800,256]{1,0:T(8,128)(2,1)S(1)}, u32[]{:S(2)}, u32[]{:S(2)}) %collective-permute-start.34) | collective-permute-done | bytes 409632 | tf_op jit(solution)/shard_map/ppermute | solution.py:771
  224.0 15.1 %collective-permute-done.38 = bf16[800,256]{1,0:T(8,128)(2,1)S(1)} collective-permute-done((bf16[800,256]{1,0:T(8,128)(2,1)S(1)}, bf16[800,256]{1,0:T(8,128)(2,1)S(1)}, u32[]{:S(2)}, u32[]{:S(2)}) %collective-permute-start.38) | collective-permute-done | bytes 409632 | tf_op jit(solution)/shard_map/ppermute | solution.py:771
  243.8 15.1 %collective-permute-done.42 = bf16[800,256]{1,0:T(8,128)(2,1)S(1)} collective-permute-done((bf16[800,256]{1,0:T(8,128)(2,1)S(1)}, bf16[800,256]{1,0:T(8,128)(2,1)S(1)}, u32[]{:S(2)}, u32[]{:S(2)}) %collective-permute-start.42) | collective-permute-done | bytes 409632 | tf_op jit(solution)/shard_map/ppermute | solution.py:771
  263.6 15.1 %collective-permute-done.46 = bf16[800,256]{1,0:T(8,128)(2,1)S(1)} collective-permute-done((bf16[800,256]{1,0:T(8,128)(2,1)S(1)}, bf16[800,256]{1,0:T(8,128)(2,1)S(1)}, u32[]{:S(2)}, u32[]{:S(2)}) %collective-permute-start.46) | collective-permute-done | bytes 409632 | tf_op jit(solution)/shard_map/ppermute | solution.py:771
  283.5 15.3 %collective-permute-done.50.refs_4_ = bf16[800,256]{1,0:T(8,128)(2,1)S(1)} collective-permute-done((bf16[800,256]{1,0:T(8,128)(2,1)S(1)}, bf16[800,256]{1,0:T(8,128)(2,1)S(1)}, u32[]{:S(2)}, u32[]{:S(2)}) %collective-permute-start.50) | collective-permute-done | bytes 409632 | tf_op jit(solution)/shard_map/ppermute | solution.py:771
  303.3 15.5 %collective-permute-done.54.refs_0_ = bf16[800,256]{1,0:T(8,128)(2,1)S(1)} collective-permute-done((bf16[800,256]{1,0:T(8,128)(2,1)S(1)}, bf16[800,256]{1,0:T(8,128)(2,1)S(1)}, u32[]{:S(2)}, u32[]{:S(2)}) %collective-permute-start.54) | collective-permute-done | bytes 409632 | tf_op jit(solution)/shard_map/ppermute | solution.py:771
  323.6 4.9 %unpack.9 = (f32[1536,768]{1,0:T(8,128)}, f32[768,1536]{1,0:T(8,128)}, f32[1024,512]{1,0:T(8,128)}, f32[512,1024]{1,0:T(8,128)}, f32[3,1024,512]{2,1,0:T(8,128)}...) custom-call(s32[3]{0:T(128)} %pad_add_fusion.info, bf16[800,256]{1,0:T(8,128)(2,1)} %copy-done.28, bf16[864,256]{1,0:T(8,128)(2,1)} %copy-done.27, ...), custom_call_target="tpu_custom_call" | custom-call | bytes 10665984 | tf_op jit(solution)/shard_map/unpack/pallas_call | solution.py:727
  332.2 6.4 %collective-permute-done.57.refs_2_.refs_0_ = bf16[928,256]{1,0:T(8,128)(2,1)S(1)} collective-permute-done((bf16[928,256]{1,0:T(8,128)(2,1)S(1)}, bf16[928,256]{1,0:T(8,128)(2,1)S(1)}, u32[]{:S(2)}, u32[]{:S(2)}) %collective-permute-start.57) | collective-permute-done | bytes 475168 | tf_op jit(solution)/shard_map/ppermute | solution.py:771
  344.8 4.0 unpack.10
  348.9 4.3 collective-permute-done.65.refs_1_
  353.8 4.6 %collective-permute-done.62.refs_0_ = bf16[800,256]{1,0:T(8,128)(2,1)S(1)} collective-permute-done((bf16[800,256]{1,0:T(8,128)(2,1)S(1)}, bf16[800,256]{1,0:T(8,128)(2,1)S(1)}, u32[]{:S(2)}, u32[]{:S(2)}) %collective-permute-start.62) | collective-permute-done | bytes 409632 | tf_op jit(solution)/shard_map/ppermute | solution.py:771
  365.2 5.7 %collective-permute-done.67.refs_4_ = bf16[800,256]{1,0:T(8,128)(2,1)S(1)} collective-permute-done((bf16[800,256]{1,0:T(8,128)(2,1)S(1)}, bf16[800,256]{1,0:T(8,128)(2,1)S(1)}, u32[]{:S(2)}, u32[]{:S(2)}) %collective-permute-start.67) | collective-permute-done | bytes 409632 | tf_op jit(solution)/shard_map/ppermute | solution.py:771
  373.0 4.9 %unpack.11 = (f32[1536,768]{1,0:T(8,128)}, f32[768,1536]{1,0:T(8,128)}, f32[1024,512]{1,0:T(8,128)}, f32[512,1024]{1,0:T(8,128)}, f32[3,1024,512]{2,1,0:T(8,128)...) custom-call(s32[3]{0:T(128)} %pad_add_fusion.info, ...), custom_call_target="tpu_custom_call", output_to_operand_aliasing={{0}: (9, {}), {1}: (10, {}), {2}: (11, {}), {3}: (12, {}), ... | custom-call | bytes 10665984 | tf_op jit(solution)/shard_map/unpack/pallas_call | solution.py:727
  393.2 9.7 %collective-permute-done.76.refs_1_ = bf16[864,256]{1,0:T(8,128)(2,1)S(1)} collective-permute-done((bf16[864,256]{1,0:T(8,128)(2,1)S(1)}, bf16[864,256]{1,0:T(8,128)(2,1)S(1)}, u32[]{:S(2)}, u32[]{:S(2)}) %collective-permute-start.76) | collective-permute-done | bytes 442400 | tf_op jit(solution)/shard_map/ppermute | solution.py:771
  407.2 4.9 %unpack.13 = (f32[1536,768]{1,0:T(8,128)}, f32[768,1536]{1,0:T(8,128)}, f32[1024,512]{1,0:T(8,128)}, f32[512,1024]{1,0:T(8,128)}, f32[3,1024,512]{2,1,0:T(8,128)...) custom-call(s32[3]{0:T(128)} %pad_add_fusion.info, ...), custom_call_target="tpu_custom_call", output_to_operand_aliasing={{0}: (9, {}), {1}: (10, {}), {2}: (11, {}), {3}: (12, {}), ... | custom-call | bytes 10665984 | tf_op jit(solution)/shard_map/unpack/pallas_call | solution.py:727
  415.9 5.6 %collective-permute-done.77.refs_2_.refs_0_ = bf16[928,256]{1,0:T(8,128)(2,1)} collective-permute-done((bf16[928,256]{1,0:T(8,128)(2,1)S(1)}, bf16[928,256]{1,0:T(8,128)(2,1)}, u32[]{:S(2)}, u32[]{:S(2)}) %collective-permute-start.77) | collective-permute-done | bytes 475168 | tf_op jit(solution)/shard_map/ppermute | solution.py:771
  432.3 4.0 unpack.15
  (425 shorter events, 150.1 us)
Async XLA Ops:
  32.1 20.2 %collective-permute-start.11 = (bf16[3,768,384]{2,1,0:T(8,128)(2,1)}, bf16[3,768,384]{2,1,0:T(8,128)(2,1)}, u32[]{:S(2)}, u32[]{:S(2)}) collective-permute-start(bf16[3,768,384]{2,1,0:T(8,128)(2,1)} %bitcast.106), channel_id=1, source_target_pairs={{0,1},{1,0},{2,3},{3,2},{4,5},{5,4},{6,7},{7,6},{8,9},{9,8},{10,11... | collective-permute-start | bytes 5308424 | tf_op jit(solution)/shard_map/ppermute | solution.py:745
  50.7 26.9 %collective-permute-start.14 = (bf16[224,1024]{1,0:T(8,128)(2,1)}, bf16[224,1024]{1,0:T(8,128)(2,1)S(1)}, u32[]{:S(2)}, u32[]{:S(2)}) collective-permute-start(bf16[224,1024]{1,0:T(8,128)(2,1)} %get-tuple-element.264), channel_id=1, source_target_pairs={{16,0},{17,1},{18,2},{19,3},{20,4},{21,5},{22,6},{23,7},{24,8},{25... | collective-permute-start | bytes 1376264 | tf_op jit(solution)/shard_map/ppermute | solution.py:753
  52.0 60.5 %collective-permute-start.18 = (bf16[224,4608]{1,0:T(8,128)(2,1)}, bf16[224,4608]{1,0:T(8,128)(2,1)S(1)}, u32[]{:S(2)}, u32[]{:S(2)}) collective-permute-start(bf16[224,4608]{1,0:T(8,128)(2,1)} %get-tuple-element.312), channel_id=1, source_target_pairs={{0,1},{1,0},{2,3},{3,2},{4,5},{5,4},{6,7},{7,6},{8,9},{9,8},{10,11... | collective-permute-start | bytes 6193160 | tf_op jit(solution)/shard_map/ppermute | solution.py:745
  57.5 55.1 %collective-permute-start.15 = (bf16[192,5120]{1,0:T(8,128)(2,1)}, bf16[192,5120]{1,0:T(8,128)(2,1)}, u32[]{:S(2)}, u32[]{:S(2)}) collective-permute-start(bf16[192,5120]{1,0:T(8,128)(2,1)} %get-tuple-element.301), channel_id=1, source_target_pairs={{0,1},{1,0},{2,3},{3,2},{4,5},{5,4},{6,7},{7,6},{8,9},{9,8},{10,11... | collective-permute-start | bytes 5898248 | tf_op jit(solution)/shard_map/ppermute | solution.py:745
  57.8 38.3 %collective-permute-start.13 = (bf16[192,768]{1,0:T(8,128)(2,1)}, bf16[192,768]{1,0:T(8,128)(2,1)S(1)}, u32[]{:S(2)}, u32[]{:S(2)}) collective-permute-start(bf16[192,768]{1,0:T(8,128)(2,1)} %get-tuple-element.271), channel_id=1, source_target_pairs={{16,0},{17,1},{18,2},{19,3},{20,4},{21,5},{22,6},{23,7},{24,8},{25... | collective-permute-start | bytes 884744 | tf_op jit(solution)/shard_map/ppermute | solution.py:753
  157.5 19.8 %collective-permute-start.26 = (bf16[928,256]{1,0:T(8,128)(2,1)S(1)}, bf16[928,256]{1,0:T(8,128)(2,1)S(1)}, u32[]{:S(2)}, u32[]{:S(2)}) collective-permute-start(bf16[928,256]{1,0:T(8,128)(2,1)S(1)} %copy-done.93), channel_id=1, source_target_pairs={{0,4},{4,8},{8,12},{12,14},{14,10},{10,6},{6,2},{2,0},{1,5},{5,9},... | collective-permute-start | bytes 1425416 | tf_op jit(solution)/shard_map/ppermute | solution.py:771
  159.4 21.9 %collective-permute-start.31 = (bf16[880,256]{1,0:T(8,128)(2,1)}, bf16[880,256]{1,0:T(8,128)(2,1)S(1)}, u32[]{:S(2)}, u32[]{:S(2)}) collective-permute-start(bf16[880,256]{1,0:T(8,128)(2,1)} %get-tuple-element.355), channel_id=1, source_target_pairs={{4,0},{8,4},{12,8},{14,12},{10,14},{6,10},{2,6},{0,2},{5,1},{9,5},... | collective-permute-start | bytes 1351688 | tf_op jit(solution)/shard_map/ppermute | solution.py:771
  177.4 21.4 %collective-permute-start.29 = (bf16[928,256]{1,0:T(8,128)(2,1)S(1)}, bf16[928,256]{1,0:T(8,128)(2,1)S(1)}, u32[]{:S(2)}, u32[]{:S(2)}) collective-permute-start(bf16[928,256]{1,0:T(8,128)(2,1)S(1)} %add.124), channel_id=1, source_target_pairs={{0,4},{4,8},{8,12},{12,14},{14,10},{10,6},{6,2},{2,0},{1,5},{5,9},... | collective-permute-start | bytes 1425416 | tf_op jit(solution)/shard_map/ppermute | solution.py:771
  179.3 19.4 %collective-permute-start.32 = (bf16[864,256]{1,0:T(8,128)(2,1)S(1)}, bf16[864,256]{1,0:T(8,128)(2,1)S(1)}, u32[]{:S(2)}, u32[]{:S(2)}) collective-permute-start(bf16[864,256]{1,0:T(8,128)(2,1)S(1)} %add.123), channel_id=1, source_target_pairs={{4,0},{8,4},{12,8},{14,12},{10,14},{6,10},{2,6},{0,2},{5,1},{9,5},... | collective-permute-start | bytes 1327112 | tf_op jit(solution)/shard_map/ppermute | solution.py:771
  181.5 21.4 %collective-permute-start.35 = (bf16[880,256]{1,0:T(8,128)(2,1)S(1)}, bf16[880,256]{1,0:T(8,128)(2,1)S(1)}, u32[]{:S(2)}, u32[]{:S(2)}) collective-permute-start(bf16[880,256]{1,0:T(8,128)(2,1)S(1)} %add.125), channel_id=1, source_target_pairs={{4,0},{8,4},{12,8},{14,12},{10,14},{6,10},{2,6},{0,2},{5,1},{9,5},... | collective-permute-start | bytes 1351688 | tf_op jit(solution)/shard_map/ppermute | solution.py:771
  199.0 20.6 %collective-permute-start.33 = (bf16[928,256]{1,0:T(8,128)(2,1)S(1)}, bf16[928,256]{1,0:T(8,128)(2,1)S(1)}, u32[]{:S(2)}, u32[]{:S(2)}) collective-permute-start(bf16[928,256]{1,0:T(8,128)(2,1)S(1)} %add.128), channel_id=1, source_target_pairs={{0,4},{4,8},{8,12},{12,14},{14,10},{10,6},{6,2},{2,0},{1,5},{5,9},... | collective-permute-start | bytes 1425416 | tf_op jit(solution)/shard_map/ppermute | solution.py:771
  203.0 20.3 %collective-permute-start.39 = (bf16[880,256]{1,0:T(8,128)(2,1)S(1)}, bf16[880,256]{1,0:T(8,128)(2,1)S(1)}, u32[]{:S(2)}, u32[]{:S(2)}) collective-permute-start(bf16[880,256]{1,0:T(8,128)(2,1)S(1)} %add.129), channel_id=1, source_target_pairs={{4,0},{8,4},{12,8},{14,12},{10,14},{6,10},{2,6},{0,2},{5,1},{9,5},... | collective-permute-start | bytes 1351688 | tf_op jit(solution)/shard_map/ppermute | solution.py:771
  219.7 19.7 %collective-permute-start.37 = (bf16[928,256]{1,0:T(8,128)(2,1)S(1)}, bf16[928,256]{1,0:T(8,128)(2,1)S(1)}, u32[]{:S(2)}, u32[]{:S(2)}) collective-permute-start(bf16[928,256]{1,0:T(8,128)(2,1)S(1)} %add.132), channel_id=1, source_target_pairs={{0,4},{4,8},{8,12},{12,14},{14,10},{10,6},{6,2},{2,0},{1,5},{5,9},... | collective-permute-start | bytes 1425416 | tf_op jit(solution)/shard_map/ppermute | solution.py:771
  223.4 19.7 %collective-permute-start.43 = (bf16[880,256]{1,0:T(8,128)(2,1)S(1)}, bf16[880,256]{1,0:T(8,128)(2,1)S(1)}, u32[]{:S(2)}, u32[]{:S(2)}) collective-permute-start(bf16[880,256]{1,0:T(8,128)(2,1)S(1)} %add.133), channel_id=1, source_target_pairs={{4,0},{8,4},{12,8},{14,12},{10,14},{6,10},{2,6},{0,2},{5,1},{9,5},... | collective-permute-start | bytes 1351688 | tf_op jit(solution)/shard_map/ppermute | solution.py:771
  239.5 19.7 %collective-permute-start.41 = (bf16[928,256]{1,0:T(8,128)(2,1)S(1)}, bf16[928,256]{1,0:T(8,128)(2,1)S(1)}, u32[]{:S(2)}, u32[]{:S(2)}) collective-permute-start(bf16[928,256]{1,0:T(8,128)(2,1)S(1)} %add.136), channel_id=1, source_target_pairs={{0,4},{4,8},{8,12},{12,14},{14,10},{10,6},{6,2},{2,0},{1,5},{5,9},... | collective-permute-start | bytes 1425416 | tf_op jit(solution)/shard_map/ppermute | solution.py:771
  243.2 19.7 %collective-permute-start.47 = (bf16[880,256]{1,0:T(8,128)(2,1)S(1)}, bf16[880,256]{1,0:T(8,128)(2,1)S(1)}, u32[]{:S(2)}, u32[]{:S(2)}) collective-permute-start(bf16[880,256]{1,0:T(8,128)(2,1)S(1)} %add.137), channel_id=1, source_target_pairs={{4,0},{8,4},{12,8},{14,12},{10,14},{6,10},{2,6},{0,2},{5,1},{9,5},... | collective-permute-start | bytes 1351688 | tf_op jit(solution)/shard_map/ppermute | solution.py:771
  259.3 19.6 %collective-permute-start.45 = (bf16[928,256]{1,0:T(8,128)(2,1)S(1)}, bf16[928,256]{1,0:T(8,128)(2,1)S(1)}, u32[]{:S(2)}, u32[]{:S(2)}) collective-permute-start(bf16[928,256]{1,0:T(8,128)(2,1)S(1)} %add.140), channel_id=1, source_target_pairs={{0,4},{4,8},{8,12},{12,14},{14,10},{10,6},{6,2},{2,0},{1,5},{5,9},... | collective-permute-start | bytes 1425416 | tf_op jit(solution)/shard_map/ppermute | solution.py:771
  279.2 19.6 %collective-permute-start.49 = (bf16[928,256]{1,0:T(8,128)(2,1)S(1)}, bf16[928,256]{1,0:T(8,128)(2,1)S(1)}, u32[]{:S(2)}, u32[]{:S(2)}) collective-permute-start(bf16[928,256]{1,0:T(8,128)(2,1)S(1)} %add.144), channel_id=1, source_target_pairs={{0,4},{4,8},{8,12},{12,14},{14,10},{10,6},{6,2},{2,0},{1,5},{5,9},... | collective-permute-start | bytes 1425416 | tf_op jit(solution)/shard_map/ppermute | solution.py:771
  281.4 19.1 %collective-permute-start.55 = (bf16[880,256]{1,0:T(8,128)(2,1)S(1)}, bf16[880,256]{1,0:T(8,128)(2,1)S(1)}, u32[]{:S(2)}, u32[]{:S(2)}) collective-permute-start(bf16[880,256]{1,0:T(8,128)(2,1)S(1)} %add.145), channel_id=1, source_target_pairs={{4,0},{8,4},{12,8},{14,12},{10,14},{6,10},{2,6},{0,2},{5,1},{9,5},... | collective-permute-start | bytes 1351688 | tf_op jit(solution)/shard_map/ppermute | solution.py:771
  299.0 23.7 %collective-permute-start.53 = (bf16[928,256]{1,0:T(8,128)(2,1)S(1)}, bf16[928,256]{1,0:T(8,128)(2,1)S(1)}, u32[]{:S(2)}, u32[]{:S(2)}) collective-permute-start(bf16[928,256]{1,0:T(8,128)(2,1)S(1)} %add.146.refs_2_.refs_0_), channel_id=1, source_target_pairs={{0,4},{4,8},{8,12},{12,14},{14,10},{10,6},{6,2},{2,0},{1,5},{5,9},... | collective-permute-start | bytes 1425416 | tf_op jit(solution)/shard_map/ppermute | solution.py:771
  300.6 20.6 %collective-permute-start.59 = (bf16[880,256]{1,0:T(8,128)(2,1)S(1)}, bf16[880,256]{1,0:T(8,128)(2,1)S(1)}, u32[]{:S(2)}, u32[]{:S(2)}) collective-permute-start(bf16[880,256]{1,0:T(8,128)(2,1)S(1)} %add.147.refs_3_.refs_1_), channel_id=1, source_target_pairs={{4,0},{8,4},{12,8},{14,12},{10,14},{6,10},{2,6},{0,2},{5,1},{9,5},... | collective-permute-start | bytes 1351688 | tf_op jit(solution)/shard_map/ppermute | solution.py:771
  301.2 19.4 %collective-permute-start.56 = (bf16[864,256]{1,0:T(8,128)(2,1)S(1)}, bf16[864,256]{1,0:T(8,128)(2,1)S(1)}, u32[]{:S(2)}, u32[]{:S(2)}) collective-permute-start(bf16[864,256]{1,0:T(8,128)(2,1)S(1)} %collective-permute-done.52.refs_5_), channel_id=1, source_target_pairs={{4,0},{8,4},{12,8},{14,12},{10,14},{6,10},{2,6},{0,2},{5,1},{9,5},... | collective-permute-start | bytes 1327112 | tf_op jit(solution)/shard_map/ppermute | solution.py:771
  321.2 20.7 %collective-permute-start.63 = (bf16[880,256]{1,0:T(8,128)(2,1)S(1)}, bf16[880,256]{1,0:T(8,128)(2,1)S(1)}, u32[]{:S(2)}, u32[]{:S(2)}) collective-permute-start(bf16[880,256]{1,0:T(8,128)(2,1)S(1)} %collective-permute-done.59.refs_7_.refs_3_), channel_id=1, source_target_pairs={{4,0},{8,4},{12,8},{14,12},{10,14},{6,10},{2,6},{0,2},{5,1},{9,5},... | collective-permute-start | bytes 1351688 | tf_op jit(solution)/shard_map/ppermute | solution.py:771
  323.5 20.5 %collective-permute-start.64 = (bf16[1536,256]{1,0:T(8,128)(2,1)S(1)}, bf16[1536,256]{1,0:T(8,128)(2,1)S(1)}, u32[]{:S(2)}, u32[]{:S(2)}) collective-permute-start(bf16[1536,256]{1,0:T(8,128)(2,1)S(1)} %pad_maximum_fusion), channel_id=1, source_target_pairs={{0,16},{16,0},{1,17},{17,1},{2,18},{18,2},{3,19},{19,3},{4,20},{20... | collective-permute-start | bytes 2359304 | tf_op jit(solution)/shard_map/ppermute | solution.py:749
  338.6 24.9 %collective-permute-start.61 = (bf16[928,256]{1,0:T(8,128)(2,1)S(1)}, bf16[928,256]{1,0:T(8,128)(2,1)S(1)}, u32[]{:S(2)}, u32[]{:S(2)}) collective-permute-start(bf16[928,256]{1,0:T(8,128)(2,1)S(1)} %collective-permute-done.57.refs_2_.refs_0_), channel_id=1, source_target_pairs={{0,4},{4,8},{8,12},{12,14},{14,10},{10,6},{6,2},{2,0},{1,5},{5,9},... | collective-permute-start | bytes 1425416 | tf_op jit(solution)/shard_map/ppermute | solution.py:771
  341.9 20.9 %collective-permute-start.68 = (bf16[880,256]{1,0:T(8,128)(2,1)S(1)}, bf16[880,256]{1,0:T(8,128)(2,1)S(1)}, u32[]{:S(2)}, u32[]{:S(2)}) collective-permute-start(bf16[880,256]{1,0:T(8,128)(2,1)S(1)} %collective-permute-done.63.refs_3_.refs_1_), channel_id=1, source_target_pairs={{4,0},{8,4},{12,8},{14,12},{10,14},{6,10},{2,6},{0,2},{5,1},{9,5},... | collective-permute-start | bytes 1351688 | tf_op jit(solution)/shard_map/ppermute | solution.py:771
  353.2 19.1 %collective-permute-start.69 = (bf16[864,256]{1,0:T(8,128)(2,1)S(1)}, bf16[864,256]{1,0:T(8,128)(2,1)S(1)}, u32[]{:S(2)}, u32[]{:S(2)}) collective-permute-start(bf16[864,256]{1,0:T(8,128)(2,1)S(1)} %collective-permute-done.65.refs_1_), channel_id=1, source_target_pairs={{4,0},{8,4},{12,8},{14,12},{10,14},{6,10},{2,6},{0,2},{5,1},{9,5},... | collective-permute-start | bytes 1327112 | tf_op jit(solution)/shard_map/ppermute | solution.py:771
  362.9 19.6 %collective-permute-start.72 = (bf16[880,256]{1,0:T(8,128)(2,1)S(1)}, bf16[880,256]{1,0:T(8,128)(2,1)S(1)}, u32[]{:S(2)}, u32[]{:S(2)}) collective-permute-start(bf16[880,256]{1,0:T(8,128)(2,1)S(1)} %collective-permute-done.68.refs_7_.refs_3_), channel_id=1, source_target_pairs={{4,0},{8,4},{12,8},{14,12},{10,14},{6,10},{2,6},{0,2},{5,1},{9,5},... | collective-permute-start | bytes 1351688 | tf_op jit(solution)/shard_map/ppermute | solution.py:771
  365.1 23.1 %collective-permute-start.75 = (bf16[1536,256]{1,0:T(8,128)(2,1)S(1)}, bf16[1536,256]{1,0:T(8,128)(2,1)S(1)}, u32[]{:S(2)}, u32[]{:S(2)}) collective-permute-start(bf16[1536,256]{1,0:T(8,128)(2,1)S(1)} %pad_maximum_fusion.1), channel_id=1, source_target_pairs={{0,16},{16,0},{1,17},{17,1},{2,18},{18,2},{3,19},{19,3},{4,20},{20... | collective-permute-start | bytes 2359304 | tf_op jit(solution)/shard_map/ppermute | solution.py:749
  381.1 24.5 %collective-permute-start.70 = (bf16[928,256]{1,0:T(8,128)(2,1)S(1)}, bf16[928,256]{1,0:T(8,128)(2,1)S(1)}, u32[]{:S(2)}, u32[]{:S(2)}) collective-permute-start(bf16[928,256]{1,0:T(8,128)(2,1)S(1)} %collective-permute-done.66.refs_2_.refs_0_), channel_id=1, source_target_pairs={{0,4},{4,8},{8,12},{12,14},{14,10},{10,6},{6,2},{2,0},{1,5},{5,9},... | collective-permute-start | bytes 1425416 | tf_op jit(solution)/shard_map/ppermute | solution.py:771
  382.5 22.5 %collective-permute-start.79 = (bf16[880,256]{1,0:T(8,128)(2,1)S(1)}, bf16[880,256]{1,0:T(8,128)(2,1)S(1)}, u32[]{:S(2)}, u32[]{:S(2)}) collective-permute-start(bf16[880,256]{1,0:T(8,128)(2,1)S(1)} %collective-permute-done.72.refs_3_.refs_1_), channel_id=1, source_target_pairs={{4,0},{8,4},{12,8},{14,12},{10,14},{6,10},{2,6},{0,2},{5,1},{9,5},... | collective-permute-start | bytes 1351688 | tf_op jit(solution)/shard_map/ppermute | solution.py:771
  407.1 24.2 %collective-permute-start.85 = (bf16[1536,256]{1,0:T(8,128)(2,1)S(1)}, bf16[1536,256]{1,0:T(8,128)(2,1)S(1)}, u32[]{:S(2)}, u32[]{:S(2)}) collective-permute-start(bf16[1536,256]{1,0:T(8,128)(2,1)S(1)} %pad_maximum_fusion.2), channel_id=1, source_target_pairs={{0,16},{16,0},{1,17},{17,1},{2,18},{18,2},{3,19},{19,3},{4,20},{20... | collective-permute-start | bytes 2359304 | tf_op jit(solution)/shard_map/ppermute | solution.py:749
  (148 other events, 1883.4 us)

commit v4 on v3

--- a/solution.py
+++ b/solution.py
@@ -1066,23 +1066,34 @@
                 (dip_own, 0, 3 * cross),
                 (dip_other, 0, 3 * cross),
             ),
+        },
+        info,
+        "pack_attention",
+    )
+    token = attn_parts[0][1]
+    if in_ring:
+        token, unused = ff.advance(token)
+    attn_parts = pack(
+        attn_layout,
+        {
             "out_i": (
                 (ci_own, 0, cross),
                 ((ci_give, 0), (left_i, ci_column), cross),
-                (dai, 0, wide_i),
+                (after(dai, token), 0, wide_i),
                 (right_i, wide_i + ff_i, wide_i),
             ),
             "small": ((small, 0, UNIT),),
         },
         info,
-        "pack_attention",
+        "pack_rest",
+        attn_parts,
     )
 
     def choose(first, second):
         return jnp.where(front, first, second)
 
     def result(rest, partial, other, output, rows, real, token):
-        mine = choose(rest + partial + to_other_core(after(other, token)), output.astype(FULL))
+        mine = choose(rest + partial + after(to_other_core(other), token), output.astype(FULL))
         mine = mine.astype(LOW).reshape(half, rows, -1)[:, :real]
         got = to_other_core(mine)
         return jnp.concatenate(

time: 455 us -> 453 us (level)
  waiting for transfers between devices: 218 us -> 201 us
  Pallas kernels: 123 us -> 136 us
    ppermute x4, waiting for transfers between devices: 28.5 us -> 18.7 us  [to_layer(): return lax.ppermute(values, 'section', [(1 - layer, layer)])]
    pallas_call x8, Pallas kernels: 66.7 us -> 76.4 us  [launch(): pl.pallas_call(whole_body, out_shape=tuple(outputs), in_specs=[pl.BlockSp...]
    pallas_call x2 -> x3, Pallas kernels: 19.1 us -> 22.6 us  [pack(): pl.pallas_call(functools.partial(pack_body, layout, chosen, kinds, len(fo...]
    unnamed x196 -> x194, local copies, waits for them, and re-layouts: 14.9 us -> 15.8 us
  transfers between devices with their start and end apart: 86 -> 86, of which waited for: 32 -> 32; matrix products, arithmetic and copies ran while one was open for 4% -> 5% of each run, Pallas kernels for 21% -> 26%
where the time goes in v4:
time: 453 us; the launch traced here: 445 us
  waiting for transfers between devices  201 us (44%)
  Pallas kernels  136 us (30%)
  starting transfers between devices  72.8 us (16%)
  local copies, waits for them, and re-layouts  22.9 us (5%)
  other arithmetic  10.2 us (2%)
    ppermute x58, waiting for transfers between devices, to_next(): return lax.ppermute(values, 'dp', route)  174 us
    pallas_call x8, Pallas kernels, launch(): pl.pallas_call(whole_body, out_shape=tuple(outputs), in_specs=[pl.BlockSp...  76.4 us
    ppermute x58, starting transfers between devices, to_next(): return lax.ppermute(values, 'dp', route)  62 us
    pallas_call x9, Pallas kernels, unpack(): pl.pallas_call(functools.partial(unpack_body, moves, rows, blocks, len(fo...  37 us
    pallas_call x3, Pallas kernels, pack(): pl.pallas_call(functools.partial(pack_body, layout, chosen, kinds, len(fo...  22.6 us
    ppermute x4, waiting for transfers between devices, to_layer(): return lax.ppermute(values, 'section', [(1 - layer, layer)])  18.7 us
    unnamed x194, local copies, waits for them, and re-layouts  15.8 us
  transfers between devices with their start and end apart: 86, of which 32 were waited for; matrix products, arithmetic and copies ran while one was open for 5% of the time, Pallas kernels for 26%

profile of v4, /device:TPU:0, one launch (start us, length us, event | category | flops | bytes accessed | tf_op | source)
XLA Modules:
  0.0 445.2 jit_solution(17289474688586787629)
XLA Ops:
  6.9 10.4 %cross_forward.1 = (bf16[192,768]{1,0:T(8,128)(2,1)}, bf16[192,768]{1,0:T(8,128)(2,1)}, bf16[224,1024]{1,0:T(8,128)(2,1)}, bf16[224,1024]{1,0:T(8,128)(2,1)}, bf...) custom-call(s32[3]{0:T(128)} %pad_add_fusion.info, ...), custom_call_target="tpu_custom_call" | custom-call | flops 2315255808 | bytes 11929344 | tf_op jit(solution)/shard_map/cross_forward/pallas_call | solution.py:247
  24.7 7.2 %tail_i.1 = (bf16[224,1024]{1,0:T(8,128)(2,1)}, bf16[224,1024]{1,0:T(8,128)(2,1)}, bf16[224,512]{1,0:T(8,128)(2,1)}, bf16[224,512]{1,0:T(8,128)(2,1)}, f32[224,5...) custom-call(s32[3]{0:T(128)} %pad_add_fusion.info, ...), custom_call_target="tpu_custom_call" | custom-call | flops 1409286144 | bytes 11583488 | tf_op jit(solution)/shard_map/tail_i/pallas_call | solution.py:247
  34.1 18.8 %tail_t.1 = (bf16[192,768]{1,0:T(8,128)(2,1)}, bf16[192,768]{1,0:T(8,128)(2,1)}, bf16[192,1536]{1,0:T(8,128)(2,1)}, bf16[192,1536]{1,0:T(8,128)(2,1)}, f32[192,1...) custom-call(s32[3]{0:T(128)} %pad_add_fusion.info, ...), custom_call_target="tpu_custom_call" | custom-call | flops 2113929216 | bytes 17215488 | tf_op jit(solution)/shard_map/tail_t/pallas_call | solution.py:247
  56.1 4.4 self_i.1
  62.5 4.8 %self_t.1 = (bf16[192,768]{1,0:T(8,128)(2,1)}, bf16[192,768]{1,0:T(8,128)(2,1)}, bf16[192,512]{1,0:T(8,128)(2,1)}, bf16[192,1536]{1,0:T(8,128)(2,1)}, bf16[192,7...) custom-call(s32[3]{0:T(128)} %pad_add_fusion.info, ...), custom_call_target="tpu_custom_call" | custom-call | flops 5435817984 | bytes 22439680 | tf_op jit(solution)/shard_map/self_t/pallas_call | solution.py:247
  68.9 8.8 %collective-permute-done.14.refs_0_ = bf16[224,1024]{1,0:T(8,128)(2,1)S(1)} collective-permute-done((bf16[224,1024]{1,0:T(8,128)(2,1)}, bf16[224,1024]{1,0:T(8,128)(2,1)S(1)}, u32[]{:S(2)}, u32[]{:S(2)}) %collective-permute-start.14) | collective-permute-done | bytes 458784 | tf_op jit(solution)/shard_map/ppermute | solution.py:753
  78.4 7.8 %tail_back_i.1 = (bf16[224,1024]{1,0:T(8,128)(2,1)}, bf16[224,512]{1,0:T(8,128)(2,1)}, bf16[224,1024]{1,0:T(8,128)(2,1)}, f32[2,1024]{1,0:T(2,128)}, f32[2,1024]...) custom-call(s32[3]{0:T(128)} %pad_add_fusion.info, ...), custom_call_target="tpu_custom_call" | custom-call | flops 1409286144 | bytes 14819328 | tf_op jit(solution)/shard_map/tail_back_i/pallas_call | solution.py:247
  86.2 10.0 %collective-permute-done.13.refs_0_ = bf16[192,768]{1,0:T(8,128)(2,1)S(1)} collective-permute-done((bf16[192,768]{1,0:T(8,128)(2,1)}, bf16[192,768]{1,0:T(8,128)(2,1)S(1)}, u32[]{:S(2)}, u32[]{:S(2)}) %collective-permute-start.13) | collective-permute-done | bytes 294944 | tf_op jit(solution)/shard_map/ppermute | solution.py:753
  96.9 10.1 %tail_back_t.1 = (bf16[192,768]{1,0:T(8,128)(2,1)}, bf16[192,1536]{1,0:T(8,128)(2,1)}, bf16[192,768]{1,0:T(8,128)(2,1)}, f32[2,768]{1,0:T(2,128)}, f32[2,768]{1,...) custom-call(s32[3]{0:T(128)} %pad_add_fusion.info, ...), custom_call_target="tpu_custom_call" | custom-call | flops 2113929216 | bytes 20183040 | tf_op jit(solution)/shard_map/tail_back_t/pallas_call | solution.py:247
  114.3 9.4 %pack_ff.1 = (bf16[800,256]{1,0:T(8,128)(2,1)}, bf16[800,256]{1,0:T(8,128)(2,1)}, bf16[800,256]{1,0:T(8,128)(2,1)}, bf16[800,256]{1,0:T(8,128)(2,1)}, bf16[800,2...) custom-call(s32[3]{0:T(128)} %pad_add_fusion.info, ...), custom_call_target="tpu_custom_call" | custom-call | flops 2751463424 | bytes 13631488 | tf_op jit(solution)/shard_map/pack_ff/pallas_call | solution.py:665
  127.1 13.0 %cross_backward.1 = (bf16[192,1536]{1,0:T(8,128)(2,1)}, bf16[192,1536]{1,0:T(8,128)(2,1)}, bf16[224,1536]{1,0:T(8,128)(2,1)}, bf16[224,1536]{1,0:T(8,128)(2,1)},...) custom-call(s32[3]{0:T(128)} %pad_add_fusion.info, ...), custom_call_target="tpu_custom_call" | custom-call | flops 2315255808 | bytes 22120192 | tf_op jit(solution)/shard_map/cross_backward/pallas_call | solution.py:247
  143.1 8.9 %pack_attention.1 = (bf16[928,256]{1,0:T(8,128)(2,1)}, bf16[928,256]{1,0:T(8,128)(2,1)}, bf16[928,256]{1,0:T(8,128)(2,1)}, bf16[928,256]{1,0:T(8,128)(2,1)}, bf1...) custom-call(s32[3]{0:T(128)} %pad_add_fusion.info, ...), custom_call_target="tpu_custom_call" | custom-call | flops 2503999488 | bytes 14811136 | tf_op jit(solution)/shard_map/pack_attention/pallas_call | solution.py:665
  154.4 4.3 pack_rest.1
  175.3 8.1 %collective-permute-done.28 = bf16[928,256]{1,0:T(8,128)(2,1)S(1)} collective-permute-done((bf16[928,256]{1,0:T(8,128)(2,1)S(1)}, bf16[928,256]{1,0:T(8,128)(2,1)S(1)}, u32[]{:S(2)}, u32[]{:S(2)}) %collective-permute-start.28) | collective-permute-done | bytes 475168 | tf_op jit(solution)/shard_map/ppermute | solution.py:771
  187.8 16.9 %collective-permute-done.32 = bf16[800,256]{1,0:T(8,128)(2,1)S(1)} collective-permute-done((bf16[800,256]{1,0:T(8,128)(2,1)S(1)}, bf16[800,256]{1,0:T(8,128)(2,1)S(1)}, u32[]{:S(2)}, u32[]{:S(2)}) %collective-permute-start.32) | collective-permute-done | bytes 409632 | tf_op jit(solution)/shard_map/ppermute | solution.py:771
  209.7 15.9 %collective-permute-done.36 = bf16[800,256]{1,0:T(8,128)(2,1)S(1)} collective-permute-done((bf16[800,256]{1,0:T(8,128)(2,1)S(1)}, bf16[800,256]{1,0:T(8,128)(2,1)S(1)}, u32[]{:S(2)}, u32[]{:S(2)}) %collective-permute-start.36) | collective-permute-done | bytes 409632 | tf_op jit(solution)/shard_map/ppermute | solution.py:771
  230.3 15.1 %collective-permute-done.40 = bf16[800,256]{1,0:T(8,128)(2,1)S(1)} collective-permute-done((bf16[800,256]{1,0:T(8,128)(2,1)S(1)}, bf16[800,256]{1,0:T(8,128)(2,1)S(1)}, u32[]{:S(2)}, u32[]{:S(2)}) %collective-permute-start.40) | collective-permute-done | bytes 409632 | tf_op jit(solution)/shard_map/ppermute | solution.py:771
  250.2 15.0 %collective-permute-done.44 = bf16[800,256]{1,0:T(8,128)(2,1)S(1)} collective-permute-done((bf16[800,256]{1,0:T(8,128)(2,1)S(1)}, bf16[800,256]{1,0:T(8,128)(2,1)S(1)}, u32[]{:S(2)}, u32[]{:S(2)}) %collective-permute-start.44) | collective-permute-done | bytes 409632 | tf_op jit(solution)/shard_map/ppermute | solution.py:771
  270.0 15.3 %collective-permute-done.48.refs_4_ = bf16[800,256]{1,0:T(8,128)(2,1)S(1)} collective-permute-done((bf16[800,256]{1,0:T(8,128)(2,1)S(1)}, bf16[800,256]{1,0:T(8,128)(2,1)S(1)}, u32[]{:S(2)}, u32[]{:S(2)}) %collective-permute-start.48) | collective-permute-done | bytes 409632 | tf_op jit(solution)/shard_map/ppermute | solution.py:771
  289.8 15.3 %collective-permute-done.52.refs_0_ = bf16[800,256]{1,0:T(8,128)(2,1)S(1)} collective-permute-done((bf16[800,256]{1,0:T(8,128)(2,1)S(1)}, bf16[800,256]{1,0:T(8,128)(2,1)S(1)}, u32[]{:S(2)}, u32[]{:S(2)}) %collective-permute-start.52) | collective-permute-done | bytes 409632 | tf_op jit(solution)/shard_map/ppermute | solution.py:771
  309.7 15.5 %collective-permute-done.56.refs_4_ = bf16[800,256]{1,0:T(8,128)(2,1)S(1)} collective-permute-done((bf16[800,256]{1,0:T(8,128)(2,1)S(1)}, bf16[800,256]{1,0:T(8,128)(2,1)S(1)}, u32[]{:S(2)}, u32[]{:S(2)}) %collective-permute-start.56) | collective-permute-done | bytes 409632 | tf_op jit(solution)/shard_map/ppermute | solution.py:771
  330.0 4.8 %unpack.9 = (f32[1536,768]{1,0:T(8,128)}, f32[768,1536]{1,0:T(8,128)}, f32[1024,512]{1,0:T(8,128)}, f32[512,1024]{1,0:T(8,128)}, f32[3,1024,512]{2,1,0:T(8,128)}...) custom-call(s32[3]{0:T(128)} %pad_add_fusion.info, bf16[800,256]{1,0:T(8,128)(2,1)} %copy-done.42, bf16[864,256]{1,0:T(8,128)(2,1)} %copy-done.41, ...), custom_call_target="tpu_custom_call" | custom-call | bytes 10665984 | tf_op jit(solution)/shard_map/unpack/pallas_call | solution.py:727
  337.9 7.1 %collective-permute-done.59.refs_2_.refs_0_ = bf16[928,256]{1,0:T(8,128)(2,1)S(1)} collective-permute-done((bf16[928,256]{1,0:T(8,128)(2,1)S(1)}, bf16[928,256]{1,0:T(8,128)(2,1)S(1)}, u32[]{:S(2)}, u32[]{:S(2)}) %collective-permute-start.59) | collective-permute-done | bytes 475168 | tf_op jit(solution)/shard_map/ppermute | solution.py:771
  350.5 4.0 unpack.10
  354.5 4.3 collective-permute-done.67.refs_5_
  360.2 4.6 %collective-permute-done.64.refs_4_ = bf16[800,256]{1,0:T(8,128)(2,1)S(1)} collective-permute-done((bf16[800,256]{1,0:T(8,128)(2,1)S(1)}, bf16[800,256]{1,0:T(8,128)(2,1)S(1)}, u32[]{:S(2)}, u32[]{:S(2)}) %collective-permute-start.64) | collective-permute-done | bytes 409632 | tf_op jit(solution)/shard_map/ppermute | solution.py:771
  370.9 6.3 %collective-permute-done.69.refs_0_ = bf16[800,256]{1,0:T(8,128)(2,1)S(1)} collective-permute-done((bf16[800,256]{1,0:T(8,128)(2,1)S(1)}, bf16[800,256]{1,0:T(8,128)(2,1)S(1)}, u32[]{:S(2)}, u32[]{:S(2)}) %collective-permute-start.69) | collective-permute-done | bytes 409632 | tf_op jit(solution)/shard_map/ppermute | solution.py:771
  379.3 4.9 %unpack.11 = (f32[1536,768]{1,0:T(8,128)}, f32[768,1536]{1,0:T(8,128)}, f32[1024,512]{1,0:T(8,128)}, f32[512,1024]{1,0:T(8,128)}, f32[3,1024,512]{2,1,0:T(8,128)...) custom-call(s32[3]{0:T(128)} %pad_add_fusion.info, ...), custom_call_target="tpu_custom_call", output_to_operand_aliasing={{0}: (9, {}), {1}: (10, {}), {2}: (11, {}), {3}: (12, {}), ... | custom-call | bytes 10665984 | tf_op jit(solution)/shard_map/unpack/pallas_call | solution.py:727
  394.8 4.0 unpack.12
  398.9 9.6 %collective-permute-done.78.refs_1_ = bf16[864,256]{1,0:T(8,128)(2,1)S(1)} collective-permute-done((bf16[864,256]{1,0:T(8,128)(2,1)S(1)}, bf16[864,256]{1,0:T(8,128)(2,1)S(1)}, u32[]{:S(2)}, u32[]{:S(2)}) %collective-permute-start.78) | collective-permute-done | bytes 442400 | tf_op jit(solution)/shard_map/ppermute | solution.py:771
  410.9 4.9 %unpack.13 = (f32[1536,768]{1,0:T(8,128)}, f32[768,1536]{1,0:T(8,128)}, f32[1024,512]{1,0:T(8,128)}, f32[512,1024]{1,0:T(8,128)}, f32[3,1024,512]{2,1,0:T(8,128)...) custom-call(s32[3]{0:T(128)} %pad_add_fusion.info, ...), custom_call_target="tpu_custom_call", output_to_operand_aliasing={{0}: (9, {}), {1}: (10, {}), {2}: (11, {}), {3}: (12, {}), ... | custom-call | bytes 10665984 | tf_op jit(solution)/shard_map/unpack/pallas_call | solution.py:727
  430.2 4.0 unpack.15
  (424 shorter events, 149.3 us)
Async XLA Ops:
  31.9 22.4 %collective-permute-start.10 = (bf16[3,1024,512]{2,1,0:T(8,128)(2,1)S(1)}, bf16[3,1024,512]{2,1,0:T(8,128)(2,1)S(1)}, u32[]{:S(2)}, u32[]{:S(2)}) collective-permute-start(bf16[3,1024,512]{2,1,0:T(8,128)(2,1)S(1)} %bitcast.80), channel_id=1, source_target_pairs={{0,1},{1,0},{2,3},{3,2},{4,5},{5,4},{6,7},{7,6},{8,9},{9,8},{10,11... | collective-permute-start | bytes 9437192 | tf_op jit(solution)/shard_map/ppermute | solution.py:745
  32.2 29.9 %collective-permute-start.11 = (bf16[3,768,384]{2,1,0:T(8,128)(2,1)}, bf16[3,768,384]{2,1,0:T(8,128)(2,1)}, u32[]{:S(2)}, u32[]{:S(2)}) collective-permute-start(bf16[3,768,384]{2,1,0:T(8,128)(2,1)} %bitcast.106), channel_id=1, source_target_pairs={{0,1},{1,0},{2,3},{3,2},{4,5},{5,4},{6,7},{7,6},{8,9},{9,8},{10,11... | collective-permute-start | bytes 5308424 | tf_op jit(solution)/shard_map/ppermute | solution.py:745
  32.5 21.8 %collective-permute-start.9 = (bf16[224,1024]{1,0:T(8,128)(2,1)}, bf16[224,1024]{1,0:T(8,128)(2,1)S(1)}, u32[]{:S(2)}, u32[]{:S(2)}) collective-permute-start(bf16[224,1024]{1,0:T(8,128)(2,1)} %get-tuple-element.273), channel_id=1, source_target_pairs={{0,16},{1,17},{2,18},{3,19},{4,20},{5,21},{6,22},{7,23},{8,24},{9,... | collective-permute-start | bytes 1376264 | tf_op jit(solution)/shard_map/ppermute | solution.py:753
  33.8 28.3 %collective-permute-start.12 = (bf16[384,768]{1,0:T(8,128)(2,1)}, bf16[384,768]{1,0:T(8,128)(2,1)}, u32[]{:S(2)}, u32[]{:S(2)}) collective-permute-start(bf16[384,768]{1,0:T(8,128)(2,1)} %refs_7_.1), channel_id=1, source_target_pairs={{0,1},{1,0},{2,3},{3,2},{4,5},{5,4},{6,7},{7,6},{8,9},{9,8},{10,11... | collective-permute-start | bytes 1769480 | tf_op jit(solution)/shard_map/ppermute | solution.py:745
  61.8 50.8 %collective-permute-start.18 = (bf16[224,4608]{1,0:T(8,128)(2,1)}, bf16[224,4608]{1,0:T(8,128)(2,1)S(1)}, u32[]{:S(2)}, u32[]{:S(2)}) collective-permute-start(bf16[224,4608]{1,0:T(8,128)(2,1)} %get-tuple-element.329), channel_id=1, source_target_pairs={{0,1},{1,0},{2,3},{3,2},{4,5},{5,4},{6,7},{7,6},{8,9},{9,8},{10,11... | collective-permute-start | bytes 6193160 | tf_op jit(solution)/shard_map/ppermute | solution.py:745
  67.2 45.3 %collective-permute-start.15 = (bf16[192,5120]{1,0:T(8,128)(2,1)}, bf16[192,5120]{1,0:T(8,128)(2,1)}, u32[]{:S(2)}, u32[]{:S(2)}) collective-permute-start(bf16[192,5120]{1,0:T(8,128)(2,1)} %get-tuple-element.318), channel_id=1, source_target_pairs={{0,1},{1,0},{2,3},{3,2},{4,5},{5,4},{6,7},{7,6},{8,9},{9,8},{10,11... | collective-permute-start | bytes 5898248 | tf_op jit(solution)/shard_map/ppermute | solution.py:745
  67.6 28.6 %collective-permute-start.13 = (bf16[192,768]{1,0:T(8,128)(2,1)}, bf16[192,768]{1,0:T(8,128)(2,1)S(1)}, u32[]{:S(2)}, u32[]{:S(2)}) collective-permute-start(bf16[192,768]{1,0:T(8,128)(2,1)} %get-tuple-element.288), channel_id=1, source_target_pairs={{16,0},{17,1},{18,2},{19,3},{20,4},{21,5},{22,6},{23,7},{24,8},{25... | collective-permute-start | bytes 884744 | tf_op jit(solution)/shard_map/ppermute | solution.py:753
  140.2 19.7 %collective-permute-start.26 = (f32[224,1024]{1,0:T(8,128)}, f32[224,1024]{1,0:T(8,128)S(1)}, u32[]{:S(2)}, u32[]{:S(2)}) collective-permute-start(f32[224,1024]{1,0:T(8,128)} %get-tuple-element.384), channel_id=1, source_target_pairs={{0,1},{1,0},{2,3},{3,2},{4,5},{5,4},{6,7},{7,6},{8,9},{9,8},{10,11... | collective-permute-start | bytes 2752520 | tf_op jit(solution)/shard_map/ppermute | solution.py:745
  163.4 20.0 %collective-permute-start.28 = (bf16[928,256]{1,0:T(8,128)(2,1)S(1)}, bf16[928,256]{1,0:T(8,128)(2,1)S(1)}, u32[]{:S(2)}, u32[]{:S(2)}) collective-permute-start(bf16[928,256]{1,0:T(8,128)(2,1)S(1)} %copy-done.51), channel_id=1, source_target_pairs={{0,4},{4,8},{8,12},{12,14},{14,10},{10,6},{6,2},{2,0},{1,5},{5,9},... | collective-permute-start | bytes 1425416 | tf_op jit(solution)/shard_map/ppermute | solution.py:771
  164.1 22.2 %collective-permute-start.33 = (bf16[880,256]{1,0:T(8,128)(2,1)S(1)}, bf16[880,256]{1,0:T(8,128)(2,1)S(1)}, u32[]{:S(2)}, u32[]{:S(2)}) collective-permute-start(bf16[880,256]{1,0:T(8,128)(2,1)S(1)} %copy-done.55), channel_id=1, source_target_pairs={{4,0},{8,4},{12,8},{14,12},{10,14},{6,10},{2,6},{0,2},{5,1},{9,5},... | collective-permute-start | bytes 1351688 | tf_op jit(solution)/shard_map/ppermute | solution.py:771
  183.5 21.5 %collective-permute-start.31 = (bf16[928,256]{1,0:T(8,128)(2,1)S(1)}, bf16[928,256]{1,0:T(8,128)(2,1)S(1)}, u32[]{:S(2)}, u32[]{:S(2)}) collective-permute-start(bf16[928,256]{1,0:T(8,128)(2,1)S(1)} %add.126), channel_id=1, source_target_pairs={{0,4},{4,8},{8,12},{12,14},{14,10},{10,6},{6,2},{2,0},{1,5},{5,9},... | collective-permute-start | bytes 1425416 | tf_op jit(solution)/shard_map/ppermute | solution.py:771
  184.3 20.6 %collective-permute-start.34 = (bf16[864,256]{1,0:T(8,128)(2,1)S(1)}, bf16[864,256]{1,0:T(8,128)(2,1)S(1)}, u32[]{:S(2)}, u32[]{:S(2)}) collective-permute-start(bf16[864,256]{1,0:T(8,128)(2,1)S(1)} %add.125), channel_id=1, source_target_pairs={{4,0},{8,4},{12,8},{14,12},{10,14},{6,10},{2,6},{0,2},{5,1},{9,5},... | collective-permute-start | bytes 1327112 | tf_op jit(solution)/shard_map/ppermute | solution.py:771
  186.5 21.7 %collective-permute-start.37 = (bf16[880,256]{1,0:T(8,128)(2,1)S(1)}, bf16[880,256]{1,0:T(8,128)(2,1)S(1)}, u32[]{:S(2)}, u32[]{:S(2)}) collective-permute-start(bf16[880,256]{1,0:T(8,128)(2,1)S(1)} %add.127), channel_id=1, source_target_pairs={{4,0},{8,4},{12,8},{14,12},{10,14},{6,10},{2,6},{0,2},{5,1},{9,5},... | collective-permute-start | bytes 1351688 | tf_op jit(solution)/shard_map/ppermute | solution.py:771
  205.2 20.6 %collective-permute-start.35 = (bf16[928,256]{1,0:T(8,128)(2,1)S(1)}, bf16[928,256]{1,0:T(8,128)(2,1)S(1)}, u32[]{:S(2)}, u32[]{:S(2)}) collective-permute-start(bf16[928,256]{1,0:T(8,128)(2,1)S(1)} %add.130), channel_id=1, source_target_pairs={{0,4},{4,8},{8,12},{12,14},{14,10},{10,6},{6,2},{2,0},{1,5},{5,9},... | collective-permute-start | bytes 1425416 | tf_op jit(solution)/shard_map/ppermute | solution.py:771
  206.0 19.7 %collective-permute-start.38 = (bf16[864,256]{1,0:T(8,128)(2,1)S(1)}, bf16[864,256]{1,0:T(8,128)(2,1)S(1)}, u32[]{:S(2)}, u32[]{:S(2)}) collective-permute-start(bf16[864,256]{1,0:T(8,128)(2,1)S(1)} %add.129), channel_id=1, source_target_pairs={{4,0},{8,4},{12,8},{14,12},{10,14},{6,10},{2,6},{0,2},{5,1},{9,5},... | collective-permute-start | bytes 1327112 | tf_op jit(solution)/shard_map/ppermute | solution.py:771
  208.3 20.5 %collective-permute-start.41 = (bf16[880,256]{1,0:T(8,128)(2,1)S(1)}, bf16[880,256]{1,0:T(8,128)(2,1)S(1)}, u32[]{:S(2)}, u32[]{:S(2)}) collective-permute-start(bf16[880,256]{1,0:T(8,128)(2,1)S(1)} %add.131), channel_id=1, source_target_pairs={{4,0},{8,4},{12,8},{14,12},{10,14},{6,10},{2,6},{0,2},{5,1},{9,5},... | collective-permute-start | bytes 1351688 | tf_op jit(solution)/shard_map/ppermute | solution.py:771
  226.0 19.7 %collective-permute-start.39 = (bf16[928,256]{1,0:T(8,128)(2,1)S(1)}, bf16[928,256]{1,0:T(8,128)(2,1)S(1)}, u32[]{:S(2)}, u32[]{:S(2)}) collective-permute-start(bf16[928,256]{1,0:T(8,128)(2,1)S(1)} %add.134), channel_id=1, source_target_pairs={{0,4},{4,8},{8,12},{12,14},{14,10},{10,6},{6,2},{2,0},{1,5},{5,9},... | collective-permute-start | bytes 1425416 | tf_op jit(solution)/shard_map/ppermute | solution.py:771
  229.0 19.7 %collective-permute-start.45 = (bf16[880,256]{1,0:T(8,128)(2,1)S(1)}, bf16[880,256]{1,0:T(8,128)(2,1)S(1)}, u32[]{:S(2)}, u32[]{:S(2)}) collective-permute-start(bf16[880,256]{1,0:T(8,128)(2,1)S(1)} %add.135), channel_id=1, source_target_pairs={{4,0},{8,4},{12,8},{14,12},{10,14},{6,10},{2,6},{0,2},{5,1},{9,5},... | collective-permute-start | bytes 1351688 | tf_op jit(solution)/shard_map/ppermute | solution.py:771
  245.9 19.6 %collective-permute-start.43 = (bf16[928,256]{1,0:T(8,128)(2,1)S(1)}, bf16[928,256]{1,0:T(8,128)(2,1)S(1)}, u32[]{:S(2)}, u32[]{:S(2)}) collective-permute-start(bf16[928,256]{1,0:T(8,128)(2,1)S(1)} %add.138), channel_id=1, source_target_pairs={{0,4},{4,8},{8,12},{12,14},{14,10},{10,6},{6,2},{2,0},{1,5},{5,9},... | collective-permute-start | bytes 1425416 | tf_op jit(solution)/shard_map/ppermute | solution.py:771
  248.9 19.7 %collective-permute-start.49 = (bf16[880,256]{1,0:T(8,128)(2,1)S(1)}, bf16[880,256]{1,0:T(8,128)(2,1)S(1)}, u32[]{:S(2)}, u32[]{:S(2)}) collective-permute-start(bf16[880,256]{1,0:T(8,128)(2,1)S(1)} %add.139), channel_id=1, source_target_pairs={{4,0},{8,4},{12,8},{14,12},{10,14},{6,10},{2,6},{0,2},{5,1},{9,5},... | collective-permute-start | bytes 1351688 | tf_op jit(solution)/shard_map/ppermute | solution.py:771
  265.7 19.6 %collective-permute-start.47 = (bf16[928,256]{1,0:T(8,128)(2,1)S(1)}, bf16[928,256]{1,0:T(8,128)(2,1)S(1)}, u32[]{:S(2)}, u32[]{:S(2)}) collective-permute-start(bf16[928,256]{1,0:T(8,128)(2,1)S(1)} %add.142), channel_id=1, source_target_pairs={{0,4},{4,8},{8,12},{12,14},{14,10},{10,6},{6,2},{2,0},{1,5},{5,9},... | collective-permute-start | bytes 1425416 | tf_op jit(solution)/shard_map/ppermute | solution.py:771
  285.5 19.6 %collective-permute-start.51 = (bf16[928,256]{1,0:T(8,128)(2,1)S(1)}, bf16[928,256]{1,0:T(8,128)(2,1)S(1)}, u32[]{:S(2)}, u32[]{:S(2)}) collective-permute-start(bf16[928,256]{1,0:T(8,128)(2,1)S(1)} %add.144), channel_id=1, source_target_pairs={{0,4},{4,8},{8,12},{12,14},{14,10},{10,6},{6,2},{2,0},{1,5},{5,9},... | collective-permute-start | bytes 1425416 | tf_op jit(solution)/shard_map/ppermute | solution.py:771
  305.3 23.9 %collective-permute-start.55 = (bf16[928,256]{1,0:T(8,128)(2,1)S(1)}, bf16[928,256]{1,0:T(8,128)(2,1)S(1)}, u32[]{:S(2)}, u32[]{:S(2)}) collective-permute-start(bf16[928,256]{1,0:T(8,128)(2,1)S(1)} %add.146.refs_2_.refs_0_), channel_id=1, source_target_pairs={{0,4},{4,8},{8,12},{12,14},{14,10},{10,6},{6,2},{2,0},{1,5},{5,9},... | collective-permute-start | bytes 1425416 | tf_op jit(solution)/shard_map/ppermute | solution.py:771
  306.3 21.3 %collective-permute-start.61 = (bf16[880,256]{1,0:T(8,128)(2,1)S(1)}, bf16[880,256]{1,0:T(8,128)(2,1)S(1)}, u32[]{:S(2)}, u32[]{:S(2)}) collective-permute-start(bf16[880,256]{1,0:T(8,128)(2,1)S(1)} %add.147.refs_3_.refs_1_), channel_id=1, source_target_pairs={{4,0},{8,4},{12,8},{14,12},{10,14},{6,10},{2,6},{0,2},{5,1},{9,5},... | collective-permute-start | bytes 1351688 | tf_op jit(solution)/shard_map/ppermute | solution.py:771
  327.6 20.0 %collective-permute-start.65 = (bf16[880,256]{1,0:T(8,128)(2,1)S(1)}, bf16[880,256]{1,0:T(8,128)(2,1)S(1)}, u32[]{:S(2)}, u32[]{:S(2)}) collective-permute-start(bf16[880,256]{1,0:T(8,128)(2,1)S(1)} %collective-permute-done.61.refs_7_.refs_3_), channel_id=1, source_target_pairs={{4,0},{8,4},{12,8},{14,12},{10,14},{6,10},{2,6},{0,2},{5,1},{9,5},... | collective-permute-start | bytes 1351688 | tf_op jit(solution)/shard_map/ppermute | solution.py:771
  329.8 19.8 %collective-permute-start.66 = (bf16[1536,256]{1,0:T(8,128)(2,1)S(1)}, bf16[1536,256]{1,0:T(8,128)(2,1)S(1)}, u32[]{:S(2)}, u32[]{:S(2)}) collective-permute-start(bf16[1536,256]{1,0:T(8,128)(2,1)S(1)} %pad_maximum_fusion), channel_id=1, source_target_pairs={{0,16},{16,0},{1,17},{17,1},{2,18},{18,2},{3,19},{19,3},{4,20},{20... | collective-permute-start | bytes 2359304 | tf_op jit(solution)/shard_map/ppermute | solution.py:749
  345.0 24.9 %collective-permute-start.63 = (bf16[928,256]{1,0:T(8,128)(2,1)S(1)}, bf16[928,256]{1,0:T(8,128)(2,1)S(1)}, u32[]{:S(2)}, u32[]{:S(2)}) collective-permute-start(bf16[928,256]{1,0:T(8,128)(2,1)S(1)} %collective-permute-done.59.refs_2_.refs_0_), channel_id=1, source_target_pairs={{0,4},{4,8},{8,12},{12,14},{14,10},{10,6},{6,2},{2,0},{1,5},{5,9},... | collective-permute-start | bytes 1425416 | tf_op jit(solution)/shard_map/ppermute | solution.py:771
  347.6 20.9 %collective-permute-start.70 = (bf16[880,256]{1,0:T(8,128)(2,1)S(1)}, bf16[880,256]{1,0:T(8,128)(2,1)S(1)}, u32[]{:S(2)}, u32[]{:S(2)}) collective-permute-start(bf16[880,256]{1,0:T(8,128)(2,1)S(1)} %collective-permute-done.65.refs_3_.refs_1_), channel_id=1, source_target_pairs={{4,0},{8,4},{12,8},{14,12},{10,14},{6,10},{2,6},{0,2},{5,1},{9,5},... | collective-permute-start | bytes 1351688 | tf_op jit(solution)/shard_map/ppermute | solution.py:771
  368.5 19.6 %collective-permute-start.74 = (bf16[880,256]{1,0:T(8,128)(2,1)S(1)}, bf16[880,256]{1,0:T(8,128)(2,1)S(1)}, u32[]{:S(2)}, u32[]{:S(2)}) collective-permute-start(bf16[880,256]{1,0:T(8,128)(2,1)S(1)} %collective-permute-done.70.refs_7_.refs_3_), channel_id=1, source_target_pairs={{4,0},{8,4},{12,8},{14,12},{10,14},{6,10},{2,6},{0,2},{5,1},{9,5},... | collective-permute-start | bytes 1351688 | tf_op jit(solution)/shard_map/ppermute | solution.py:771
  370.8 23.1 %collective-permute-start.77 = (bf16[1536,256]{1,0:T(8,128)(2,1)S(1)}, bf16[1536,256]{1,0:T(8,128)(2,1)S(1)}, u32[]{:S(2)}, u32[]{:S(2)}) collective-permute-start(bf16[1536,256]{1,0:T(8,128)(2,1)S(1)} %pad_maximum_fusion.1), channel_id=1, source_target_pairs={{0,16},{16,0},{1,17},{17,1},{2,18},{18,2},{3,19},{19,3},{4,20},{20... | collective-permute-start | bytes 2359304 | tf_op jit(solution)/shard_map/ppermute | solution.py:749
  387.4 22.5 %collective-permute-start.72 = (bf16[928,256]{1,0:T(8,128)(2,1)S(1)}, bf16[928,256]{1,0:T(8,128)(2,1)S(1)}, u32[]{:S(2)}, u32[]{:S(2)}) collective-permute-start(bf16[928,256]{1,0:T(8,128)(2,1)S(1)} %collective-permute-done.68.refs_2_.refs_0_), channel_id=1, source_target_pairs={{0,4},{4,8},{8,12},{12,14},{14,10},{10,6},{6,2},{2,0},{1,5},{5,9},... | collective-permute-start | bytes 1425416 | tf_op jit(solution)/shard_map/ppermute | solution.py:771
  388.1 20.4 %collective-permute-start.80 = (bf16[880,256]{1,0:T(8,128)(2,1)S(1)}, bf16[880,256]{1,0:T(8,128)(2,1)S(1)}, u32[]{:S(2)}, u32[]{:S(2)}) collective-permute-start(bf16[880,256]{1,0:T(8,128)(2,1)S(1)} %collective-permute-done.74.refs_3_.refs_1_), channel_id=1, source_target_pairs={{4,0},{8,4},{12,8},{14,12},{10,14},{6,10},{2,6},{0,2},{5,1},{9,5},... | collective-permute-start | bytes 1351688 | tf_op jit(solution)/shard_map/ppermute | solution.py:771
  (147 other events, 1913.9 us)

commit v5 on v4

--- a/solution.py
+++ b/solution.py
@@ -158,7 +158,7 @@
     normed_ref, hidden, slopes, unit1, inv1, unit2, inv2 = kept
     branch = times(contexts[0], out_w[0].get()[...]) + times(contexts[1], out_w[1].get()[...])
     unit, inverse = norm_rows(residual.astype(FULL) + branch)
-    unit1[...] = unit
+    unit1[...] = unit.astype(unit1.dtype)
     inv1[...] = wide(inverse)
     normed = unit * gain[0:1, :] + shift[0:1, :]
     normed_ref[...] = normed.astype(LOW)
@@ -171,12 +171,12 @@
             span = pl.ds(start, TILE)
             value, slope = gelu_both(times(normed_ref[...], up[:, span]))
             hidden[half][:, span] = value.astype(LOW)
-            slopes[half][:, span] = slope
+            slopes[half][:, span] = slope.astype(slopes[half].dtype)
             mixed[...] += times(hidden[half][:, span], down[span, :])
         if leave is not None:
             leave.go(hidden[half], slopes[half])
     unit, inverse = norm_rows(mixed[...])
-    unit2[...] = unit
+    unit2[...] = unit.astype(unit2.dtype)
     inv2[...] = wide(inverse)
     return unit * gain[1:2, :] + shift[1:2, :]
 
@@ -185,7 +185,7 @@
     slopes, unit1, inv1, unit2, inv2 = kept
     df, du, da, dgain, dshift = grads
     dsecond, dgain1, dshift1 = norm_back(
-        unit2.get()[...], inv2.get()[:, 0:1], gain[1:2, :], seed
+        unit2.get()[...].astype(FULL), inv2.get()[:, 0:1], gain[1:2, :], seed
     )
     total[...] = dsecond
     df[...] = dsecond.astype(LOW)
@@ -194,10 +194,10 @@
         for start in range(0, up.shape[1], TILE):
             span = pl.ds(start, TILE)
             dhidden = times_back(df[...], down[span, :])
-            du[half][:, span] = (dhidden * slope[:, span]).astype(LOW)
+            du[half][:, span] = (dhidden * slope[:, span].astype(FULL)).astype(LOW)
             total[...] += times_back(du[half][:, span], up[:, span])
     dfirst, dgain0, dshift0 = norm_back(
-        unit1.get()[...], inv1.get()[:, 0:1], gain[0:1, :], total[...]
+        unit1.get()[...].astype(FULL), inv1.get()[:, 0:1], gain[0:1, :], total[...]
     )
     dgain[...] = jnp.concatenate([dgain0, dgain1], axis=0)
     dshift[...] = jnp.concatenate([dshift0, dshift1], axis=0)
@@ -600,12 +600,11 @@
         for column in range(0, width, span):
             area = pl.ds(column, span)
             if chosen[name] == 1:
-                total[0:depth, 0:span] = mine[0][:, area]
+                total[0:depth, 0:span] = mine[0][:, area].astype(total.dtype)
             else:
                 x0, x1, y0, y1 = mine
-                total[0:depth, 0:span] = back_times(x0[...], y0[:, area]) + back_times(
-                    x1[...], y1[:, area]
-                )
+                product = back_times(x0[...], y0[:, area]) + back_times(x1[...], y1[:, area])
+                total[0:depth, 0:span] = product.astype(total.dtype)
             for unused, unit, way, row, real in units:
                 inside = unit * UNIT - column
                 if not 0 <= inside < span:
@@ -613,7 +612,7 @@
                 rows = round_up(real, 16)
                 for hop in range(blocks):
                     block = lax.rem(place + (blocks - hop if way == 0 else hop), blocks)
-                    source = pl.ds(pl.multiple_of(block * real, 8), rows)
+                    source = pl.ds(pl.multiple_of(block * real, math.gcd(real, 16)), rows)
                     outs[way * blocks + hop][row : row + rows, :] = total[
                         source, inside : inside + UNIT
                     ].astype(LOW)
@@ -638,6 +637,7 @@
     outputs = [shape_of(layout.sizes[way], UNIT) for way in range(2) for hop in range(blocks)]
     deepest = max(weight[1] for weight in layout.weights) + 32
     arrays, kinds, buffers, work = [], [], [], 0
+    even = all(weight[1] // blocks % 16 == 0 for weight in layout.weights)
 
     def number_of(array):
         for number, one in enumerate(arrays):
@@ -670,7 +670,7 @@
         scratch_shapes=buffers
         + [pltpu.VMEM(v.shape, v.dtype) for v in outputs]
         + [
-            pltpu.VMEM((deepest, TILE), FULL),
+            pltpu.VMEM((deepest, TILE), LOW if even else FULL),
             pltpu.SemaphoreType.DMA((len(buffers),)),
             pltpu.SemaphoreType.DMA((2 * blocks * len(chosen),)),
         ],
@@ -882,8 +882,8 @@
         return launch(
             first_tail,
             [low_w, low_w, low_h, low_h]
-            + [shape_of(rows, hidden, FULL)] * 2
-            + [shape_of(rows, width, FULL), shape_of(rows, 128, FULL)] * 2,
+            + [shape_of(rows, hidden)] * 2
+            + [shape_of(rows, width), shape_of(rows, 128, FULL)] * 2,
             (x, c0, c1, gain, shift),
             far=far,
             scratch=[pltpu.VMEM((rows, width), FULL)] + buffers_for(far),

time: 453 us -> 452 us (level)
  Pallas kernels: 136 us -> 125 us
  waiting for transfers between devices: 201 us -> 211 us
    ppermute x4, waiting for transfers between devices: 18.7 us -> 29 us  [to_layer(): return lax.ppermute(values, 'section', [(1 - layer, layer)])]
    pallas_call x8, Pallas kernels: 76.4 us -> 66.4 us  [launch(): pl.pallas_call(whole_body, out_shape=tuple(outputs), in_specs=[pl.BlockSp...]
  transfers between devices with their start and end apart: 86 -> 86, of which waited for: 32 -> 33; matrix products, arithmetic and copies ran while one was open for 5% -> 5% of each run, Pallas kernels for 26% -> 24%
where the time goes in v5:
time: 452 us; the launch traced here: 445 us
  waiting for transfers between devices  211 us (47%)
  Pallas kernels  125 us (28%)
  starting transfers between devices  72.1 us (16%)
  local copies, waits for them, and re-layouts  23.1 us (5%)
  other arithmetic  10.2 us (2%)
    ppermute x58, waiting for transfers between devices, to_next(): return lax.ppermute(values, 'dp', route)  175 us
    pallas_call x8, Pallas kernels, launch(): pl.pallas_call(whole_body, out_shape=tuple(outputs), in_specs=[pl.BlockSp...  66.4 us
    ppermute x58, starting transfers between devices, to_next(): return lax.ppermute(values, 'dp', route)  61.6 us
    pallas_call x9, Pallas kernels, unpack(): pl.pallas_call(functools.partial(unpack_body, moves, rows, blocks, len(fo...  37 us
    ppermute x4, waiting for transfers between devices, to_layer(): return lax.ppermute(values, 'section', [(1 - layer, layer)])  29 us
    pallas_call x3, Pallas kernels, pack(): pl.pallas_call(functools.partial(pack_body, layout, chosen, kinds, len(fo...  22.1 us
    unnamed x194, local copies, waits for them, and re-layouts  15.9 us
  transfers between devices with their start and end apart: 86, of which 33 were waited for; matrix products, arithmetic and copies ran while one was open for 5% of the time, Pallas kernels for 24%

profile of v5, /device:TPU:0, one launch (start us, length us, event | category | flops | bytes accessed | tf_op | source)
XLA Modules:
  0.0 444.6 jit_solution(18276525882814689701)
XLA Ops:
  6.9 10.3 %cross_forward.1 = (bf16[192,768]{1,0:T(8,128)(2,1)}, bf16[192,768]{1,0:T(8,128)(2,1)}, bf16[224,1024]{1,0:T(8,128)(2,1)}, bf16[224,1024]{1,0:T(8,128)(2,1)}, bf...) custom-call(s32[3]{0:T(128)} %pad_add_fusion.info, ...), custom_call_target="tpu_custom_call" | custom-call | flops 2315255808 | bytes 11929344 | tf_op jit(solution)/shard_map/cross_forward/pallas_call | solution.py:247
  24.6 7.1 %tail_i.1 = (bf16[224,1024]{1,0:T(8,128)(2,1)}, bf16[224,1024]{1,0:T(8,128)(2,1)}, bf16[224,512]{1,0:T(8,128)(2,1)}, bf16[224,512]{1,0:T(8,128)(2,1)}, bf16[224,...) custom-call(s32[3]{0:T(128)} %pad_add_fusion.info, ...), custom_call_target="tpu_custom_call" | custom-call | flops 1409286144 | bytes 10207232 | tf_op jit(solution)/shard_map/tail_i/pallas_call | solution.py:247
  33.9 9.0 %tail_t.1 = (bf16[192,768]{1,0:T(8,128)(2,1)}, bf16[192,768]{1,0:T(8,128)(2,1)}, bf16[192,1536]{1,0:T(8,128)(2,1)}, bf16[192,1536]{1,0:T(8,128)(2,1)}, bf16[192,...) custom-call(s32[3]{0:T(128)} %pad_add_fusion.info, ...), custom_call_target="tpu_custom_call" | custom-call | flops 2113929216 | bytes 15446016 | tf_op jit(solution)/shard_map/tail_t/pallas_call | solution.py:247
  46.1 4.4 self_i.1
  52.5 4.8 %self_t.1 = (bf16[192,768]{1,0:T(8,128)(2,1)}, bf16[192,768]{1,0:T(8,128)(2,1)}, bf16[192,512]{1,0:T(8,128)(2,1)}, bf16[192,1536]{1,0:T(8,128)(2,1)}, bf16[192,7...) custom-call(s32[3]{0:T(128)} %pad_add_fusion.info, ...), custom_call_target="tpu_custom_call" | custom-call | flops 5435817984 | bytes 22439680 | tf_op jit(solution)/shard_map/self_t/pallas_call | solution.py:247
  58.9 18.5 %collective-permute-done.14.refs_0_ = bf16[224,1024]{1,0:T(8,128)(2,1)S(1)} collective-permute-done((bf16[224,1024]{1,0:T(8,128)(2,1)}, bf16[224,1024]{1,0:T(8,128)(2,1)S(1)}, u32[]{:S(2)}, u32[]{:S(2)}) %collective-permute-start.14) | collective-permute-done | bytes 458784 | tf_op jit(solution)/shard_map/ppermute | solution.py:753
  78.1 7.6 %tail_back_i.1 = (bf16[224,1024]{1,0:T(8,128)(2,1)}, bf16[224,512]{1,0:T(8,128)(2,1)}, bf16[224,1024]{1,0:T(8,128)(2,1)}, f32[2,1024]{1,0:T(2,128)}, f32[2,1024]...) custom-call(s32[3]{0:T(128)} %pad_add_fusion.info, ...), custom_call_target="tpu_custom_call" | custom-call | flops 1409286144 | bytes 13443072 | tf_op jit(solution)/shard_map/tail_back_i/pallas_call | solution.py:247
  85.7 10.3 %collective-permute-done.13.refs_0_ = bf16[192,768]{1,0:T(8,128)(2,1)S(1)} collective-permute-done((bf16[192,768]{1,0:T(8,128)(2,1)}, bf16[192,768]{1,0:T(8,128)(2,1)S(1)}, u32[]{:S(2)}, u32[]{:S(2)}) %collective-permute-start.13) | collective-permute-done | bytes 294944 | tf_op jit(solution)/shard_map/ppermute | solution.py:753
  96.7 9.8 %tail_back_t.1 = (bf16[192,768]{1,0:T(8,128)(2,1)}, bf16[192,1536]{1,0:T(8,128)(2,1)}, bf16[192,768]{1,0:T(8,128)(2,1)}, f32[2,768]{1,0:T(2,128)}, f32[2,768]{1,...) custom-call(s32[3]{0:T(128)} %pad_add_fusion.info, ...), custom_call_target="tpu_custom_call" | custom-call | flops 2113929216 | bytes 18413568 | tf_op jit(solution)/shard_map/tail_back_t/pallas_call | solution.py:247
  113.9 9.2 %pack_ff.1 = (bf16[800,256]{1,0:T(8,128)(2,1)}, bf16[800,256]{1,0:T(8,128)(2,1)}, bf16[800,256]{1,0:T(8,128)(2,1)}, bf16[800,256]{1,0:T(8,128)(2,1)}, bf16[800,2...) custom-call(s32[3]{0:T(128)} %pad_add_fusion.info, ...), custom_call_target="tpu_custom_call" | custom-call | flops 2751463424 | bytes 13631488 | tf_op jit(solution)/shard_map/pack_ff/pallas_call | solution.py:665
  126.1 13.4 %cross_backward.1 = (bf16[192,1536]{1,0:T(8,128)(2,1)}, bf16[192,1536]{1,0:T(8,128)(2,1)}, bf16[224,1536]{1,0:T(8,128)(2,1)}, bf16[224,1536]{1,0:T(8,128)(2,1)},...) custom-call(s32[3]{0:T(128)} %pad_add_fusion.info, ...), custom_call_target="tpu_custom_call" | custom-call | flops 2315255808 | bytes 22120192 | tf_op jit(solution)/shard_map/cross_backward/pallas_call | solution.py:247
  142.4 8.7 %pack_attention.1 = (bf16[928,256]{1,0:T(8,128)(2,1)}, bf16[928,256]{1,0:T(8,128)(2,1)}, bf16[928,256]{1,0:T(8,128)(2,1)}, bf16[928,256]{1,0:T(8,128)(2,1)}, bf1...) custom-call(s32[3]{0:T(128)} %pad_add_fusion.info, ...), custom_call_target="tpu_custom_call" | custom-call | flops 2503999488 | bytes 14811136 | tf_op jit(solution)/shard_map/pack_attention/pallas_call | solution.py:665
  153.8 4.3 pack_rest.1
  174.6 8.1 %collective-permute-done.28 = bf16[928,256]{1,0:T(8,128)(2,1)S(1)} collective-permute-done((bf16[928,256]{1,0:T(8,128)(2,1)S(1)}, bf16[928,256]{1,0:T(8,128)(2,1)S(1)}, u32[]{:S(2)}, u32[]{:S(2)}) %collective-permute-start.28) | collective-permute-done | bytes 475168 | tf_op jit(solution)/shard_map/ppermute | solution.py:771
  187.1 16.9 %collective-permute-done.32 = bf16[800,256]{1,0:T(8,128)(2,1)S(1)} collective-permute-done((bf16[800,256]{1,0:T(8,128)(2,1)S(1)}, bf16[800,256]{1,0:T(8,128)(2,1)S(1)}, u32[]{:S(2)}, u32[]{:S(2)}) %collective-permute-start.32) | collective-permute-done | bytes 409632 | tf_op jit(solution)/shard_map/ppermute | solution.py:771
  209.0 15.9 %collective-permute-done.36 = bf16[800,256]{1,0:T(8,128)(2,1)S(1)} collective-permute-done((bf16[800,256]{1,0:T(8,128)(2,1)S(1)}, bf16[800,256]{1,0:T(8,128)(2,1)S(1)}, u32[]{:S(2)}, u32[]{:S(2)}) %collective-permute-start.36) | collective-permute-done | bytes 409632 | tf_op jit(solution)/shard_map/ppermute | solution.py:771
  229.7 15.1 %collective-permute-done.40 = bf16[800,256]{1,0:T(8,128)(2,1)S(1)} collective-permute-done((bf16[800,256]{1,0:T(8,128)(2,1)S(1)}, bf16[800,256]{1,0:T(8,128)(2,1)S(1)}, u32[]{:S(2)}, u32[]{:S(2)}) %collective-permute-start.40) | collective-permute-done | bytes 409632 | tf_op jit(solution)/shard_map/ppermute | solution.py:771
  249.5 15.0 %collective-permute-done.44 = bf16[800,256]{1,0:T(8,128)(2,1)S(1)} collective-permute-done((bf16[800,256]{1,0:T(8,128)(2,1)S(1)}, bf16[800,256]{1,0:T(8,128)(2,1)S(1)}, u32[]{:S(2)}, u32[]{:S(2)}) %collective-permute-start.44) | collective-permute-done | bytes 409632 | tf_op jit(solution)/shard_map/ppermute | solution.py:771
  269.3 15.3 %collective-permute-done.48.refs_4_ = bf16[800,256]{1,0:T(8,128)(2,1)S(1)} collective-permute-done((bf16[800,256]{1,0:T(8,128)(2,1)S(1)}, bf16[800,256]{1,0:T(8,128)(2,1)S(1)}, u32[]{:S(2)}, u32[]{:S(2)}) %collective-permute-start.48) | collective-permute-done | bytes 409632 | tf_op jit(solution)/shard_map/ppermute | solution.py:771
  289.2 15.3 %collective-permute-done.52.refs_0_ = bf16[800,256]{1,0:T(8,128)(2,1)S(1)} collective-permute-done((bf16[800,256]{1,0:T(8,128)(2,1)S(1)}, bf16[800,256]{1,0:T(8,128)(2,1)S(1)}, u32[]{:S(2)}, u32[]{:S(2)}) %collective-permute-start.52) | collective-permute-done | bytes 409632 | tf_op jit(solution)/shard_map/ppermute | solution.py:771
  309.0 15.5 %collective-permute-done.56.refs_4_ = bf16[800,256]{1,0:T(8,128)(2,1)S(1)} collective-permute-done((bf16[800,256]{1,0:T(8,128)(2,1)S(1)}, bf16[800,256]{1,0:T(8,128)(2,1)S(1)}, u32[]{:S(2)}, u32[]{:S(2)}) %collective-permute-start.56) | collective-permute-done | bytes 409632 | tf_op jit(solution)/shard_map/ppermute | solution.py:771
  329.4 4.8 %unpack.9 = (f32[1536,768]{1,0:T(8,128)}, f32[768,1536]{1,0:T(8,128)}, f32[1024,512]{1,0:T(8,128)}, f32[512,1024]{1,0:T(8,128)}, f32[3,1024,512]{2,1,0:T(8,128)}...) custom-call(s32[3]{0:T(128)} %pad_add_fusion.info, bf16[800,256]{1,0:T(8,128)(2,1)} %copy-done.42, bf16[864,256]{1,0:T(8,128)(2,1)} %copy-done.41, ...), custom_call_target="tpu_custom_call" | custom-call | bytes 10665984 | tf_op jit(solution)/shard_map/unpack/pallas_call | solution.py:727
  337.3 7.1 %collective-permute-done.59.refs_2_.refs_0_ = bf16[928,256]{1,0:T(8,128)(2,1)S(1)} collective-permute-done((bf16[928,256]{1,0:T(8,128)(2,1)S(1)}, bf16[928,256]{1,0:T(8,128)(2,1)S(1)}, u32[]{:S(2)}, u32[]{:S(2)}) %collective-permute-start.59) | collective-permute-done | bytes 475168 | tf_op jit(solution)/shard_map/ppermute | solution.py:771
  349.9 4.0 unpack.10
  353.9 4.3 collective-permute-done.67.refs_5_
  359.5 4.6 %collective-permute-done.64.refs_4_ = bf16[800,256]{1,0:T(8,128)(2,1)S(1)} collective-permute-done((bf16[800,256]{1,0:T(8,128)(2,1)S(1)}, bf16[800,256]{1,0:T(8,128)(2,1)S(1)}, u32[]{:S(2)}, u32[]{:S(2)}) %collective-permute-start.64) | collective-permute-done | bytes 409632 | tf_op jit(solution)/shard_map/ppermute | solution.py:771
  370.2 6.3 %collective-permute-done.69.refs_0_ = bf16[800,256]{1,0:T(8,128)(2,1)S(1)} collective-permute-done((bf16[800,256]{1,0:T(8,128)(2,1)S(1)}, bf16[800,256]{1,0:T(8,128)(2,1)S(1)}, u32[]{:S(2)}, u32[]{:S(2)}) %collective-permute-start.69) | collective-permute-done | bytes 409632 | tf_op jit(solution)/shard_map/ppermute | solution.py:771
  378.7 4.9 %unpack.11 = (f32[1536,768]{1,0:T(8,128)}, f32[768,1536]{1,0:T(8,128)}, f32[1024,512]{1,0:T(8,128)}, f32[512,1024]{1,0:T(8,128)}, f32[3,1024,512]{2,1,0:T(8,128)...) custom-call(s32[3]{0:T(128)} %pad_add_fusion.info, ...), custom_call_target="tpu_custom_call", output_to_operand_aliasing={{0}: (9, {}), {1}: (10, {}), {2}: (11, {}), {3}: (12, {}), ... | custom-call | bytes 10665984 | tf_op jit(solution)/shard_map/unpack/pallas_call | solution.py:727
  394.2 4.0 unpack.12
  398.2 9.7 %collective-permute-done.78.refs_1_ = bf16[864,256]{1,0:T(8,128)(2,1)S(1)} collective-permute-done((bf16[864,256]{1,0:T(8,128)(2,1)S(1)}, bf16[864,256]{1,0:T(8,128)(2,1)S(1)}, u32[]{:S(2)}, u32[]{:S(2)}) %collective-permute-start.78) | collective-permute-done | bytes 442400 | tf_op jit(solution)/shard_map/ppermute | solution.py:771
  410.2 4.9 %unpack.13 = (f32[1536,768]{1,0:T(8,128)}, f32[768,1536]{1,0:T(8,128)}, f32[1024,512]{1,0:T(8,128)}, f32[512,1024]{1,0:T(8,128)}, f32[3,1024,512]{2,1,0:T(8,128)...) custom-call(s32[3]{0:T(128)} %pad_add_fusion.info, ...), custom_call_target="tpu_custom_call", output_to_operand_aliasing={{0}: (9, {}), {1}: (10, {}), {2}: (11, {}), {3}: (12, {}), ... | custom-call | bytes 10665984 | tf_op jit(solution)/shard_map/unpack/pallas_call | solution.py:727
  429.5 4.0 unpack.15
  (424 shorter events, 149.0 us)
Async XLA Ops:
  32.0 20.1 %collective-permute-start.11 = (bf16[3,768,384]{2,1,0:T(8,128)(2,1)}, bf16[3,768,384]{2,1,0:T(8,128)(2,1)}, u32[]{:S(2)}, u32[]{:S(2)}) collective-permute-start(bf16[3,768,384]{2,1,0:T(8,128)(2,1)} %bitcast.106), channel_id=1, source_target_pairs={{0,1},{1,0},{2,3},{3,2},{4,5},{5,4},{6,7},{7,6},{8,9},{9,8},{10,11... | collective-permute-start | bytes 5308424 | tf_op jit(solution)/shard_map/ppermute | solution.py:745
  50.5 26.9 %collective-permute-start.14 = (bf16[224,1024]{1,0:T(8,128)(2,1)}, bf16[224,1024]{1,0:T(8,128)(2,1)S(1)}, u32[]{:S(2)}, u32[]{:S(2)}) collective-permute-start(bf16[224,1024]{1,0:T(8,128)(2,1)} %get-tuple-element.281), channel_id=1, source_target_pairs={{16,0},{17,1},{18,2},{19,3},{20,4},{21,5},{22,6},{23,7},{24,8},{25... | collective-permute-start | bytes 1376264 | tf_op jit(solution)/shard_map/ppermute | solution.py:753
  51.8 60.4 %collective-permute-start.18 = (bf16[224,4608]{1,0:T(8,128)(2,1)}, bf16[224,4608]{1,0:T(8,128)(2,1)S(1)}, u32[]{:S(2)}, u32[]{:S(2)}) collective-permute-start(bf16[224,4608]{1,0:T(8,128)(2,1)} %get-tuple-element.329), channel_id=1, source_target_pairs={{0,1},{1,0},{2,3},{3,2},{4,5},{5,4},{6,7},{7,6},{8,9},{9,8},{10,11... | collective-permute-start | bytes 6193160 | tf_op jit(solution)/shard_map/ppermute | solution.py:745
  57.3 54.8 %collective-permute-start.15 = (bf16[192,5120]{1,0:T(8,128)(2,1)}, bf16[192,5120]{1,0:T(8,128)(2,1)}, u32[]{:S(2)}, u32[]{:S(2)}) collective-permute-start(bf16[192,5120]{1,0:T(8,128)(2,1)} %get-tuple-element.318), channel_id=1, source_target_pairs={{0,1},{1,0},{2,3},{3,2},{4,5},{5,4},{6,7},{7,6},{8,9},{9,8},{10,11... | collective-permute-start | bytes 5898248 | tf_op jit(solution)/shard_map/ppermute | solution.py:745
  57.6 38.5 %collective-permute-start.13 = (bf16[192,768]{1,0:T(8,128)(2,1)}, bf16[192,768]{1,0:T(8,128)(2,1)S(1)}, u32[]{:S(2)}, u32[]{:S(2)}) collective-permute-start(bf16[192,768]{1,0:T(8,128)(2,1)} %get-tuple-element.288), channel_id=1, source_target_pairs={{16,0},{17,1},{18,2},{19,3},{20,4},{21,5},{22,6},{23,7},{24,8},{25... | collective-permute-start | bytes 884744 | tf_op jit(solution)/shard_map/ppermute | solution.py:753
  139.5 19.7 %collective-permute-start.26 = (f32[224,1024]{1,0:T(8,128)}, f32[224,1024]{1,0:T(8,128)S(1)}, u32[]{:S(2)}, u32[]{:S(2)}) collective-permute-start(f32[224,1024]{1,0:T(8,128)} %get-tuple-element.384), channel_id=1, source_target_pairs={{0,1},{1,0},{2,3},{3,2},{4,5},{5,4},{6,7},{7,6},{8,9},{9,8},{10,11... | collective-permute-start | bytes 2752520 | tf_op jit(solution)/shard_map/ppermute | solution.py:745
  162.7 20.0 %collective-permute-start.28 = (bf16[928,256]{1,0:T(8,128)(2,1)S(1)}, bf16[928,256]{1,0:T(8,128)(2,1)S(1)}, u32[]{:S(2)}, u32[]{:S(2)}) collective-permute-start(bf16[928,256]{1,0:T(8,128)(2,1)S(1)} %copy-done.51), channel_id=1, source_target_pairs={{0,4},{4,8},{8,12},{12,14},{14,10},{10,6},{6,2},{2,0},{1,5},{5,9},... | collective-permute-start | bytes 1425416 | tf_op jit(solution)/shard_map/ppermute | solution.py:771
  163.5 22.2 %collective-permute-start.33 = (bf16[880,256]{1,0:T(8,128)(2,1)S(1)}, bf16[880,256]{1,0:T(8,128)(2,1)S(1)}, u32[]{:S(2)}, u32[]{:S(2)}) collective-permute-start(bf16[880,256]{1,0:T(8,128)(2,1)S(1)} %copy-done.55), channel_id=1, source_target_pairs={{4,0},{8,4},{12,8},{14,12},{10,14},{6,10},{2,6},{0,2},{5,1},{9,5},... | collective-permute-start | bytes 1351688 | tf_op jit(solution)/shard_map/ppermute | solution.py:771
  182.8 21.5 %collective-permute-start.31 = (bf16[928,256]{1,0:T(8,128)(2,1)S(1)}, bf16[928,256]{1,0:T(8,128)(2,1)S(1)}, u32[]{:S(2)}, u32[]{:S(2)}) collective-permute-start(bf16[928,256]{1,0:T(8,128)(2,1)S(1)} %add.126), channel_id=1, source_target_pairs={{0,4},{4,8},{8,12},{12,14},{14,10},{10,6},{6,2},{2,0},{1,5},{5,9},... | collective-permute-start | bytes 1425416 | tf_op jit(solution)/shard_map/ppermute | solution.py:771
  183.6 20.6 %collective-permute-start.34 = (bf16[864,256]{1,0:T(8,128)(2,1)S(1)}, bf16[864,256]{1,0:T(8,128)(2,1)S(1)}, u32[]{:S(2)}, u32[]{:S(2)}) collective-permute-start(bf16[864,256]{1,0:T(8,128)(2,1)S(1)} %add.125), channel_id=1, source_target_pairs={{4,0},{8,4},{12,8},{14,12},{10,14},{6,10},{2,6},{0,2},{5,1},{9,5},... | collective-permute-start | bytes 1327112 | tf_op jit(solution)/shard_map/ppermute | solution.py:771
  184.9 19.2 %collective-permute-start.32 = (bf16[800,256]{1,0:T(8,128)(2,1)S(1)}, bf16[800,256]{1,0:T(8,128)(2,1)S(1)}, u32[]{:S(2)}, u32[]{:S(2)}) collective-permute-start(bf16[800,256]{1,0:T(8,128)(2,1)S(1)} %add.124), channel_id=1, source_target_pairs={{0,4},{4,8},{8,12},{12,14},{14,10},{10,6},{6,2},{2,0},{1,5},{5,9},... | collective-permute-start | bytes 1228808 | tf_op jit(solution)/shard_map/ppermute | solution.py:771
  185.8 21.6 %collective-permute-start.37 = (bf16[880,256]{1,0:T(8,128)(2,1)S(1)}, bf16[880,256]{1,0:T(8,128)(2,1)S(1)}, u32[]{:S(2)}, u32[]{:S(2)}) collective-permute-start(bf16[880,256]{1,0:T(8,128)(2,1)S(1)} %add.127), channel_id=1, source_target_pairs={{4,0},{8,4},{12,8},{14,12},{10,14},{6,10},{2,6},{0,2},{5,1},{9,5},... | collective-permute-start | bytes 1351688 | tf_op jit(solution)/shard_map/ppermute | solution.py:771
  204.5 20.6 %collective-permute-start.35 = (bf16[928,256]{1,0:T(8,128)(2,1)S(1)}, bf16[928,256]{1,0:T(8,128)(2,1)S(1)}, u32[]{:S(2)}, u32[]{:S(2)}) collective-permute-start(bf16[928,256]{1,0:T(8,128)(2,1)S(1)} %add.130), channel_id=1, source_target_pairs={{0,4},{4,8},{8,12},{12,14},{14,10},{10,6},{6,2},{2,0},{1,5},{5,9},... | collective-permute-start | bytes 1425416 | tf_op jit(solution)/shard_map/ppermute | solution.py:771
  205.3 19.7 %collective-permute-start.38 = (bf16[864,256]{1,0:T(8,128)(2,1)S(1)}, bf16[864,256]{1,0:T(8,128)(2,1)S(1)}, u32[]{:S(2)}, u32[]{:S(2)}) collective-permute-start(bf16[864,256]{1,0:T(8,128)(2,1)S(1)} %add.129), channel_id=1, source_target_pairs={{4,0},{8,4},{12,8},{14,12},{10,14},{6,10},{2,6},{0,2},{5,1},{9,5},... | collective-permute-start | bytes 1327112 | tf_op jit(solution)/shard_map/ppermute | solution.py:771
  207.5 20.7 %collective-permute-start.41 = (bf16[880,256]{1,0:T(8,128)(2,1)S(1)}, bf16[880,256]{1,0:T(8,128)(2,1)S(1)}, u32[]{:S(2)}, u32[]{:S(2)}) collective-permute-start(bf16[880,256]{1,0:T(8,128)(2,1)S(1)} %add.131), channel_id=1, source_target_pairs={{4,0},{8,4},{12,8},{14,12},{10,14},{6,10},{2,6},{0,2},{5,1},{9,5},... | collective-permute-start | bytes 1351688 | tf_op jit(solution)/shard_map/ppermute | solution.py:771
  225.3 19.7 %collective-permute-start.39 = (bf16[928,256]{1,0:T(8,128)(2,1)S(1)}, bf16[928,256]{1,0:T(8,128)(2,1)S(1)}, u32[]{:S(2)}, u32[]{:S(2)}) collective-permute-start(bf16[928,256]{1,0:T(8,128)(2,1)S(1)} %add.134), channel_id=1, source_target_pairs={{0,4},{4,8},{8,12},{12,14},{14,10},{10,6},{6,2},{2,0},{1,5},{5,9},... | collective-permute-start | bytes 1425416 | tf_op jit(solution)/shard_map/ppermute | solution.py:771
  228.3 19.7 %collective-permute-start.45 = (bf16[880,256]{1,0:T(8,128)(2,1)S(1)}, bf16[880,256]{1,0:T(8,128)(2,1)S(1)}, u32[]{:S(2)}, u32[]{:S(2)}) collective-permute-start(bf16[880,256]{1,0:T(8,128)(2,1)S(1)} %add.135), channel_id=1, source_target_pairs={{4,0},{8,4},{12,8},{14,12},{10,14},{6,10},{2,6},{0,2},{5,1},{9,5},... | collective-permute-start | bytes 1351688 | tf_op jit(solution)/shard_map/ppermute | solution.py:771
  245.2 19.6 %collective-permute-start.43 = (bf16[928,256]{1,0:T(8,128)(2,1)S(1)}, bf16[928,256]{1,0:T(8,128)(2,1)S(1)}, u32[]{:S(2)}, u32[]{:S(2)}) collective-permute-start(bf16[928,256]{1,0:T(8,128)(2,1)S(1)} %add.138), channel_id=1, source_target_pairs={{0,4},{4,8},{8,12},{12,14},{14,10},{10,6},{6,2},{2,0},{1,5},{5,9},... | collective-permute-start | bytes 1425416 | tf_op jit(solution)/shard_map/ppermute | solution.py:771
  248.2 19.7 %collective-permute-start.49 = (bf16[880,256]{1,0:T(8,128)(2,1)S(1)}, bf16[880,256]{1,0:T(8,128)(2,1)S(1)}, u32[]{:S(2)}, u32[]{:S(2)}) collective-permute-start(bf16[880,256]{1,0:T(8,128)(2,1)S(1)} %add.139), channel_id=1, source_target_pairs={{4,0},{8,4},{12,8},{14,12},{10,14},{6,10},{2,6},{0,2},{5,1},{9,5},... | collective-permute-start | bytes 1351688 | tf_op jit(solution)/shard_map/ppermute | solution.py:771
  265.0 19.6 %collective-permute-start.47 = (bf16[928,256]{1,0:T(8,128)(2,1)S(1)}, bf16[928,256]{1,0:T(8,128)(2,1)S(1)}, u32[]{:S(2)}, u32[]{:S(2)}) collective-permute-start(bf16[928,256]{1,0:T(8,128)(2,1)S(1)} %add.142), channel_id=1, source_target_pairs={{0,4},{4,8},{8,12},{12,14},{14,10},{10,6},{6,2},{2,0},{1,5},{5,9},... | collective-permute-start | bytes 1425416 | tf_op jit(solution)/shard_map/ppermute | solution.py:771
  284.8 19.6 %collective-permute-start.51 = (bf16[928,256]{1,0:T(8,128)(2,1)S(1)}, bf16[928,256]{1,0:T(8,128)(2,1)S(1)}, u32[]{:S(2)}, u32[]{:S(2)}) collective-permute-start(bf16[928,256]{1,0:T(8,128)(2,1)S(1)} %add.144), channel_id=1, source_target_pairs={{0,4},{4,8},{8,12},{12,14},{14,10},{10,6},{6,2},{2,0},{1,5},{5,9},... | collective-permute-start | bytes 1425416 | tf_op jit(solution)/shard_map/ppermute | solution.py:771
  304.7 23.9 %collective-permute-start.55 = (bf16[928,256]{1,0:T(8,128)(2,1)S(1)}, bf16[928,256]{1,0:T(8,128)(2,1)S(1)}, u32[]{:S(2)}, u32[]{:S(2)}) collective-permute-start(bf16[928,256]{1,0:T(8,128)(2,1)S(1)} %add.146.refs_2_.refs_0_), channel_id=1, source_target_pairs={{0,4},{4,8},{8,12},{12,14},{14,10},{10,6},{6,2},{2,0},{1,5},{5,9},... | collective-permute-start | bytes 1425416 | tf_op jit(solution)/shard_map/ppermute | solution.py:771
  305.6 21.3 %collective-permute-start.61 = (bf16[880,256]{1,0:T(8,128)(2,1)S(1)}, bf16[880,256]{1,0:T(8,128)(2,1)S(1)}, u32[]{:S(2)}, u32[]{:S(2)}) collective-permute-start(bf16[880,256]{1,0:T(8,128)(2,1)S(1)} %add.147.refs_3_.refs_1_), channel_id=1, source_target_pairs={{4,0},{8,4},{12,8},{14,12},{10,14},{6,10},{2,6},{0,2},{5,1},{9,5},... | collective-permute-start | bytes 1351688 | tf_op jit(solution)/shard_map/ppermute | solution.py:771
  327.0 20.0 %collective-permute-start.65 = (bf16[880,256]{1,0:T(8,128)(2,1)S(1)}, bf16[880,256]{1,0:T(8,128)(2,1)S(1)}, u32[]{:S(2)}, u32[]{:S(2)}) collective-permute-start(bf16[880,256]{1,0:T(8,128)(2,1)S(1)} %collective-permute-done.61.refs_7_.refs_3_), channel_id=1, source_target_pairs={{4,0},{8,4},{12,8},{14,12},{10,14},{6,10},{2,6},{0,2},{5,1},{9,5},... | collective-permute-start | bytes 1351688 | tf_op jit(solution)/shard_map/ppermute | solution.py:771
  329.2 19.8 %collective-permute-start.66 = (bf16[1536,256]{1,0:T(8,128)(2,1)S(1)}, bf16[1536,256]{1,0:T(8,128)(2,1)S(1)}, u32[]{:S(2)}, u32[]{:S(2)}) collective-permute-start(bf16[1536,256]{1,0:T(8,128)(2,1)S(1)} %pad_maximum_fusion), channel_id=1, source_target_pairs={{0,16},{16,0},{1,17},{17,1},{2,18},{18,2},{3,19},{19,3},{4,20},{20... | collective-permute-start | bytes 2359304 | tf_op jit(solution)/shard_map/ppermute | solution.py:749
  344.3 24.9 %collective-permute-start.63 = (bf16[928,256]{1,0:T(8,128)(2,1)S(1)}, bf16[928,256]{1,0:T(8,128)(2,1)S(1)}, u32[]{:S(2)}, u32[]{:S(2)}) collective-permute-start(bf16[928,256]{1,0:T(8,128)(2,1)S(1)} %collective-permute-done.59.refs_2_.refs_0_), channel_id=1, source_target_pairs={{0,4},{4,8},{8,12},{12,14},{14,10},{10,6},{6,2},{2,0},{1,5},{5,9},... | collective-permute-start | bytes 1425416 | tf_op jit(solution)/shard_map/ppermute | solution.py:771
  346.9 20.9 %collective-permute-start.70 = (bf16[880,256]{1,0:T(8,128)(2,1)S(1)}, bf16[880,256]{1,0:T(8,128)(2,1)S(1)}, u32[]{:S(2)}, u32[]{:S(2)}) collective-permute-start(bf16[880,256]{1,0:T(8,128)(2,1)S(1)} %collective-permute-done.65.refs_3_.refs_1_), channel_id=1, source_target_pairs={{4,0},{8,4},{12,8},{14,12},{10,14},{6,10},{2,6},{0,2},{5,1},{9,5},... | collective-permute-start | bytes 1351688 | tf_op jit(solution)/shard_map/ppermute | solution.py:771
  358.2 19.1 %collective-permute-start.71 = (bf16[864,256]{1,0:T(8,128)(2,1)S(1)}, bf16[864,256]{1,0:T(8,128)(2,1)S(1)}, u32[]{:S(2)}, u32[]{:S(2)}) collective-permute-start(bf16[864,256]{1,0:T(8,128)(2,1)S(1)} %collective-permute-done.67.refs_5_), channel_id=1, source_target_pairs={{4,0},{8,4},{12,8},{14,12},{10,14},{6,10},{2,6},{0,2},{5,1},{9,5},... | collective-permute-start | bytes 1327112 | tf_op jit(solution)/shard_map/ppermute | solution.py:771
  367.9 19.6 %collective-permute-start.74 = (bf16[880,256]{1,0:T(8,128)(2,1)S(1)}, bf16[880,256]{1,0:T(8,128)(2,1)S(1)}, u32[]{:S(2)}, u32[]{:S(2)}) collective-permute-start(bf16[880,256]{1,0:T(8,128)(2,1)S(1)} %collective-permute-done.70.refs_7_.refs_3_), channel_id=1, source_target_pairs={{4,0},{8,4},{12,8},{14,12},{10,14},{6,10},{2,6},{0,2},{5,1},{9,5},... | collective-permute-start | bytes 1351688 | tf_op jit(solution)/shard_map/ppermute | solution.py:771
  370.1 23.1 %collective-permute-start.77 = (bf16[1536,256]{1,0:T(8,128)(2,1)S(1)}, bf16[1536,256]{1,0:T(8,128)(2,1)S(1)}, u32[]{:S(2)}, u32[]{:S(2)}) collective-permute-start(bf16[1536,256]{1,0:T(8,128)(2,1)S(1)} %pad_maximum_fusion.1), channel_id=1, source_target_pairs={{0,16},{16,0},{1,17},{17,1},{2,18},{18,2},{3,19},{19,3},{4,20},{20... | collective-permute-start | bytes 2359304 | tf_op jit(solution)/shard_map/ppermute | solution.py:749
  386.7 22.5 %collective-permute-start.72 = (bf16[928,256]{1,0:T(8,128)(2,1)S(1)}, bf16[928,256]{1,0:T(8,128)(2,1)S(1)}, u32[]{:S(2)}, u32[]{:S(2)}) collective-permute-start(bf16[928,256]{1,0:T(8,128)(2,1)S(1)} %collective-permute-done.68.refs_2_.refs_0_), channel_id=1, source_target_pairs={{0,4},{4,8},{8,12},{12,14},{14,10},{10,6},{6,2},{2,0},{1,5},{5,9},... | collective-permute-start | bytes 1425416 | tf_op jit(solution)/shard_map/ppermute | solution.py:771
  387.5 20.3 %collective-permute-start.80 = (bf16[880,256]{1,0:T(8,128)(2,1)S(1)}, bf16[880,256]{1,0:T(8,128)(2,1)S(1)}, u32[]{:S(2)}, u32[]{:S(2)}) collective-permute-start(bf16[880,256]{1,0:T(8,128)(2,1)S(1)} %collective-permute-done.74.refs_3_.refs_1_), channel_id=1, source_target_pairs={{4,0},{8,4},{12,8},{14,12},{10,14},{6,10},{2,6},{0,2},{5,1},{9,5},... | collective-permute-start | bytes 1351688 | tf_op jit(solution)/shard_map/ppermute | solution.py:771
  (147 other events, 1901.4 us)
